TPU v7x, 128 devices: a whole 4x4x4 slice. The times are simulated.
128 devices in a mesh: ctx: 32 (over z, x_lo, y), tp: 4 (over x_hi, core).
Axes of the slice: x: 4 (x_hi: 2, x_lo: 2; x = x_hi * 2 + x_lo), y: 4, z: 4, core: 2. Of those that a mesh axis runs over, the one named last changes fastest.
Arguments:
- queries: bfloat16 [24576, 2048], P('ctx', 'tp'), may hold values from -6 to 6
- keys: bfloat16 [24576, 2048], P('ctx', 'tp'), may hold values from -6 to 6
- values: bfloat16 [24576, 2048], P('ctx', 'tp'), may hold values from -6 to 6
- out_grad: bfloat16 [24576, 2048], P('ctx', 'tp'), may hold values from -6 to 6
- key_blocks: int32 [96, 16], replicated, may hold values from -1 to 95, as said below
- target_counts: int32 [96], replicated, may hold values from 0 to 128, as said below
Outputs:
- query_grad: bfloat16 [24576, 2048], P('ctx', 'tp')
- key_grad: bfloat16 [24576, 2048], P('ctx', 'tp')
- value_grad: bfloat16 [24576, 2048], P('ctx', 'tp')
Inputs may be any that keep to these rules, and one draw needn't show every extreme that they name: `key_blocks`: entry 0 of row b is b itself; the other entries are distinct blocks k with b - 24 <= k < b, or -1 for an empty slot; a row has empty slots only where fewer than 15 such blocks exist. The last target_counts[b] events of block b are targets: no other event reads them as keys.
All inputs are finite; a program needn't handle non-finite values.
Results may differ from a plain program's by a relative error of at most 0.005.
Values may be sent and summed in bfloat16 or wider, within the bound.
No kernel may reach another device: no remote copies, remote signals or barrier semaphores. Data moves between devices by JAX's collectives and lax.ppermute only.
A program may use at most 64 MiB of HBM per device.

v0:
```python
import math

import jax
import jax.numpy as jnp
from jax import lax
from jax.sharding import PartitionSpec as P

HEAD = 128
BLK = 256
KPB = 16


def from_behind(array, axis, by):
    length = lax.axis_size(axis)
    pairs = [(i, i + by) for i in range(length) if 0 <= i + by < length]
    return lax.ppermute(array, axis, pairs)


def passed_along(array, axis, by):
    length = lax.axis_size(axis)
    return lax.ppermute(array, axis, [(i, (i + by) % length) for i in range(length)])


def block_mask(query_id, key_id, target_counts):
    row_index = jnp.arange(BLK, dtype=jnp.int32)[:, None]
    col_index = jnp.arange(BLK, dtype=jnp.int32)[None, :]
    own_targets = target_counts[query_id]
    key_targets = target_counts[key_id]
    diagonal = (col_index <= row_index) & (
        (col_index < BLK - own_targets) | (col_index == row_index)
    )
    earlier = jnp.broadcast_to(col_index < BLK - key_targets, diagonal.shape)
    return jnp.where(query_id == key_id, diagonal, earlier).astype(jnp.float32)


def tile_grads(query_tile, grad_tile, key_tile, value_tile, allowed):
    head_factor = 1.0 / math.sqrt(HEAD)
    norm_scale = 1.0 / math.sqrt(KPB * BLK)
    scores = (
        jnp.einsum("ihd,jhd->hij", query_tile, key_tile, preferred_element_type=jnp.float32)
        * head_factor
    )
    sigmoid_part = jax.nn.sigmoid(scores)
    gated = allowed[None] * norm_scale
    weights = (scores * sigmoid_part * gated).astype(jnp.bfloat16)
    weight_grad = jnp.einsum(
        "ihd,jhd->hij", grad_tile, value_tile, preferred_element_type=jnp.float32
    )
    score_grad = (
        weight_grad * gated * sigmoid_part * (1.0 + scores * (1.0 - sigmoid_part))
    ).astype(jnp.bfloat16)
    query_part = (
        jnp.einsum("hij,jhd->ihd", score_grad, key_tile, preferred_element_type=jnp.float32)
        * head_factor
    )
    key_part = (
        jnp.einsum("hij,ihd->jhd", score_grad, query_tile, preferred_element_type=jnp.float32)
        * head_factor
    )
    payload_portion = jnp.einsum(
        "hij,ihd->jhd", weights, grad_tile, preferred_element_type=jnp.float32
    )
    return (query_part, key_part, payload_portion)


def visit(
    query_base,
    key_base,
    active,
    query_here,
    grad_here,
    key_here,
    value_here,
    grads,
    key_blocks,
    target_counts,
):
    per_device = query_here.shape[0]
    total_blocks = key_blocks.shape[0]

    def pair_step(pair_index, present_value):
        query_slot = pair_index // per_device
        key_slot = pair_index % per_device
        query_id = jnp.clip(query_base + query_slot, 0, total_blocks - 1)
        key_id = key_base + key_slot
        listed = active & jnp.any(key_blocks[query_id] == key_id)

        def work(accums):
            query_acc, key_acc, value_acc = accums
            safe_key = jnp.clip(key_id, 0, total_blocks - 1)
            allowed = block_mask(query_id, safe_key, target_counts)
            query_part, key_part, payload_portion = tile_grads(
                query_here[query_slot],
                grad_here[query_slot],
                key_here[key_slot],
                value_here[key_slot],
                allowed,
            )
            return (
                query_acc.at[query_slot].add(query_part),
                key_acc.at[key_slot].add(key_part),
                value_acc.at[key_slot].add(payload_portion),
            )

        return lax.cond(listed, work, lambda unchanged: unchanged, present_value)

    return lax.fori_loop(0, per_device * per_device, pair_step, grads)


def body(queries, keys, values, out_grad, key_blocks, target_counts):
    cycle_size = lax.axis_size("ctx")
    reach_hops = cycle_size // 4
    position = lax.axis_index("ctx")
    per_device = queries.shape[0] // BLK
    heads_here = queries.shape[1] // HEAD
    block_shape = (per_device, BLK, heads_here, HEAD)
    query_blocks = queries.reshape(block_shape)
    key_tiles = keys.reshape(block_shape)
    value_tiles = values.reshape(block_shape)
    grad_blocks = out_grad.reshape(block_shape)
    empty = jnp.zeros(block_shape, jnp.float32)

    def query_hop(hop_index, state):
        query_here, grad_here, query_acc, key_acc, value_acc = state
        source = position + hop_index
        query_acc, key_acc, value_acc = visit(
            source * per_device,
            position * per_device,
            source < cycle_size,
            query_here,
            grad_here,
            key_tiles,
            value_tiles,
            (query_acc, key_acc, value_acc),
            key_blocks,
            target_counts,
        )
        query_here, grad_here = from_behind((query_here, grad_here), "ctx", -1)
        query_acc = passed_along(query_acc, "ctx", -1)
        return (query_here, grad_here, query_acc, key_acc, value_acc)

    state = lax.fori_loop(
        0, reach_hops, query_hop, (query_blocks, grad_blocks, empty, empty, empty)
    )
    query_here, grad_here, query_acc, key_acc, value_acc = state
    source = position + reach_hops
    query_acc, key_acc, value_acc = visit(
        source * per_device,
        position * per_device,
        source < cycle_size,
        query_here,
        grad_here,
        key_tiles,
        value_tiles,
        (query_acc, key_acc, value_acc),
        key_blocks,
        target_counts,
    )
    query_acc = passed_along(query_acc.astype(jnp.bfloat16), "ctx", reach_hops).astype(
        query_acc.dtype
    )
    flat = queries.shape
    return (
        query_acc.reshape(flat).astype(jnp.bfloat16),
        key_acc.reshape(flat).astype(jnp.bfloat16),
        value_acc.reshape(flat).astype(jnp.bfloat16),
    )


def solution(mesh):
    in_specs = (P("ctx", "tp"), P("ctx", "tp"), P("ctx", "tp"), P("ctx", "tp"), P(), P())
    out_specs = (P("ctx", "tp"), P("ctx", "tp"), P("ctx", "tp"))
    return jax.shard_map(body, mesh=mesh, in_specs=in_specs, out_specs=out_specs, check_vma=False)
```

profile of v0, /device:TPU:92, one launch (start us, length us, event | category | flops | bytes accessed | tf_op | source)
XLA Modules:
  0.0 1438.7 jit_solution(7109819680452405573)
XLA Ops:
  9.0 1331.2 %while.90 = (s32[]{:T(128)}, bf16[3,256,4,128]{3,1,2,0:T(8,128)(2,1)}, bf16[3,256,4,128]{3,1,2,0:T(8,128)(2,1)}, f32[3,256,4,128]{1,3,2,0:T(8,128)S(1)}, f32[3,2...) while((s32[]{:T(128)}, ...), condition=%wide.region_8.9_spmd, body=%wide.region_0.8_spmd.sunk | while | flops 341443200 | bytes 57675284 | solution.py:142
  12.2 69.5 %while.92 = (s32[]{:T(128)}, f32[3,256,4,128]{1,3,2,0:T(8,128)S(1)}, f32[3,256,4,128]{1,3,2,0:T(8,128)}, f32[3,256,4,128]{1,3,2,0:T(8,128)}, s32[]{:T(128)}, /*i...) while((s32[]{:T(128)}, ...), condition=%wide.region_7.7_spmd, body=%wide.region_1.6_spmd.sunk | while | flops 341443200 | bytes 38800408 | solution.py:107
  86.8 34.5 %collective-permute-done.2 = f32[3,256,4,128]{1,3,2,0:T(8,128)} collective-permute-done((f32[3,256,4,128]{1,3,2,0:T(8,128)S(1)}, f32[3,256,4,128]{1,3,2,0:T(8,128)}, u32[]{:S(2)}, u32[]{:S(2)}) %collective-permute-start.2) | collective-permute-done | bytes 1572896 | tf_op jit(solution)/shard_map/while/body/eval_jaxpr/ppermute | solution.py:21
  122.7 15.4 %collective-permute-done = bf16[3,256,4,128]{3,1,2,0:T(8,128)(2,1)} collective-permute-done((bf16[3,256,4,128]{3,1,2,0:T(8,128)(2,1)S(1)}, bf16[3,256,4,128]{3,1,2,0:T(8,128)(2,1)}, u32[]{:S(2)}, u32[]{:S(2)}) %collective-permute-start) | collective-permute-done | bytes 786464 | tf_op jit(solution)/shard_map/while/body/eval_jaxpr/ppermute | solution.py:16
  138.1 15.7 %collective-permute-done.1 = bf16[3,256,4,128]{3,1,2,0:T(8,128)(2,1)} collective-permute-done((bf16[3,256,4,128]{3,1,2,0:T(8,128)(2,1)}, bf16[3,256,4,128]{3,1,2,0:T(8,128)(2,1)}, u32[]{:S(2)}, u32[]{:S(2)}) %collective-permute-start.1) | collective-permute-done | bytes 786464 | tf_op jit(solution)/shard_map/while/body/eval_jaxpr/ppermute | solution.py:16
  157.0 97.9 %while.92 = (s32[]{:T(128)}, f32[3,256,4,128]{1,3,2,0:T(8,128)S(1)}, f32[3,256,4,128]{1,3,2,0:T(8,128)}, f32[3,256,4,128]{1,3,2,0:T(8,128)}, s32[]{:T(128)}, /*i...) while((s32[]{:T(128)}, ...), condition=%wide.region_7.7_spmd, body=%wide.region_1.6_spmd.sunk | while | flops 341443200 | bytes 38800408 | solution.py:107
  258.8 35.7 %collective-permute-done.2 = f32[3,256,4,128]{1,3,2,0:T(8,128)} collective-permute-done((f32[3,256,4,128]{1,3,2,0:T(8,128)S(1)}, f32[3,256,4,128]{1,3,2,0:T(8,128)}, u32[]{:S(2)}, u32[]{:S(2)}) %collective-permute-start.2) | collective-permute-done | bytes 1572896 | tf_op jit(solution)/shard_map/while/body/eval_jaxpr/ppermute | solution.py:21
  295.9 15.4 %collective-permute-done = bf16[3,256,4,128]{3,1,2,0:T(8,128)(2,1)} collective-permute-done((bf16[3,256,4,128]{3,1,2,0:T(8,128)(2,1)S(1)}, bf16[3,256,4,128]{3,1,2,0:T(8,128)(2,1)}, u32[]{:S(2)}, u32[]{:S(2)}) %collective-permute-start) | collective-permute-done | bytes 786464 | tf_op jit(solution)/shard_map/while/body/eval_jaxpr/ppermute | solution.py:16
  329.3 97.9 %while.92 = (s32[]{:T(128)}, f32[3,256,4,128]{1,3,2,0:T(8,128)S(1)}, f32[3,256,4,128]{1,3,2,0:T(8,128)}, f32[3,256,4,128]{1,3,2,0:T(8,128)}, s32[]{:T(128)}, /*i...) while((s32[]{:T(128)}, ...), condition=%wide.region_7.7_spmd, body=%wide.region_1.6_spmd.sunk | while | flops 341443200 | bytes 38800408 | solution.py:107
  431.0 35.7 %collective-permute-done.2 = f32[3,256,4,128]{1,3,2,0:T(8,128)} collective-permute-done((f32[3,256,4,128]{1,3,2,0:T(8,128)S(1)}, f32[3,256,4,128]{1,3,2,0:T(8,128)}, u32[]{:S(2)}, u32[]{:S(2)}) %collective-permute-start.2) | collective-permute-done | bytes 1572896 | tf_op jit(solution)/shard_map/while/body/eval_jaxpr/ppermute | solution.py:21
  468.1 15.4 %collective-permute-done = bf16[3,256,4,128]{3,1,2,0:T(8,128)(2,1)} collective-permute-done((bf16[3,256,4,128]{3,1,2,0:T(8,128)(2,1)S(1)}, bf16[3,256,4,128]{3,1,2,0:T(8,128)(2,1)}, u32[]{:S(2)}, u32[]{:S(2)}) %collective-permute-start) | collective-permute-done | bytes 786464 | tf_op jit(solution)/shard_map/while/body/eval_jaxpr/ppermute | solution.py:16
  500.6 97.9 %while.92 = (s32[]{:T(128)}, f32[3,256,4,128]{1,3,2,0:T(8,128)S(1)}, f32[3,256,4,128]{1,3,2,0:T(8,128)}, f32[3,256,4,128]{1,3,2,0:T(8,128)}, s32[]{:T(128)}, /*i...) while((s32[]{:T(128)}, ...), condition=%wide.region_7.7_spmd, body=%wide.region_1.6_spmd.sunk | while | flops 341443200 | bytes 38800408 | solution.py:107
  602.4 35.7 %collective-permute-done.2 = f32[3,256,4,128]{1,3,2,0:T(8,128)} collective-permute-done((f32[3,256,4,128]{1,3,2,0:T(8,128)S(1)}, f32[3,256,4,128]{1,3,2,0:T(8,128)}, u32[]{:S(2)}, u32[]{:S(2)}) %collective-permute-start.2) | collective-permute-done | bytes 1572896 | tf_op jit(solution)/shard_map/while/body/eval_jaxpr/ppermute | solution.py:21
  639.5 15.4 %collective-permute-done = bf16[3,256,4,128]{3,1,2,0:T(8,128)(2,1)} collective-permute-done((bf16[3,256,4,128]{3,1,2,0:T(8,128)(2,1)S(1)}, bf16[3,256,4,128]{3,1,2,0:T(8,128)(2,1)}, u32[]{:S(2)}, u32[]{:S(2)}) %collective-permute-start) | collective-permute-done | bytes 786464 | tf_op jit(solution)/shard_map/while/body/eval_jaxpr/ppermute | solution.py:16
  671.0 97.9 %while.92 = (s32[]{:T(128)}, f32[3,256,4,128]{1,3,2,0:T(8,128)S(1)}, f32[3,256,4,128]{1,3,2,0:T(8,128)}, f32[3,256,4,128]{1,3,2,0:T(8,128)}, s32[]{:T(128)}, /*i...) while((s32[]{:T(128)}, ...), condition=%wide.region_7.7_spmd, body=%wide.region_1.6_spmd.sunk | while | flops 341443200 | bytes 38800408 | solution.py:107
  772.8 35.7 %collective-permute-done.2 = f32[3,256,4,128]{1,3,2,0:T(8,128)} collective-permute-done((f32[3,256,4,128]{1,3,2,0:T(8,128)S(1)}, f32[3,256,4,128]{1,3,2,0:T(8,128)}, u32[]{:S(2)}, u32[]{:S(2)}) %collective-permute-start.2) | collective-permute-done | bytes 1572896 | tf_op jit(solution)/shard_map/while/body/eval_jaxpr/ppermute | solution.py:21
  840.5 97.9 %while.92 = (s32[]{:T(128)}, f32[3,256,4,128]{1,3,2,0:T(8,128)S(1)}, f32[3,256,4,128]{1,3,2,0:T(8,128)}, f32[3,256,4,128]{1,3,2,0:T(8,128)}, s32[]{:T(128)}, /*i...) while((s32[]{:T(128)}, ...), condition=%wide.region_7.7_spmd, body=%wide.region_1.6_spmd.sunk | while | flops 341443200 | bytes 38800408 | solution.py:107
  942.3 35.7 %collective-permute-done.2 = f32[3,256,4,128]{1,3,2,0:T(8,128)} collective-permute-done((f32[3,256,4,128]{1,3,2,0:T(8,128)S(1)}, f32[3,256,4,128]{1,3,2,0:T(8,128)}, u32[]{:S(2)}, u32[]{:S(2)}) %collective-permute-start.2) | collective-permute-done | bytes 1572896 | tf_op jit(solution)/shard_map/while/body/eval_jaxpr/ppermute | solution.py:21
  979.4 15.4 %collective-permute-done = bf16[3,256,4,128]{3,1,2,0:T(8,128)(2,1)} collective-permute-done((bf16[3,256,4,128]{3,1,2,0:T(8,128)(2,1)S(1)}, bf16[3,256,4,128]{3,1,2,0:T(8,128)(2,1)}, u32[]{:S(2)}, u32[]{:S(2)}) %collective-permute-start) | collective-permute-done | bytes 786464 | tf_op jit(solution)/shard_map/while/body/eval_jaxpr/ppermute | solution.py:16
  1009.1 97.9 %while.92 = (s32[]{:T(128)}, f32[3,256,4,128]{1,3,2,0:T(8,128)S(1)}, f32[3,256,4,128]{1,3,2,0:T(8,128)}, f32[3,256,4,128]{1,3,2,0:T(8,128)}, s32[]{:T(128)}, /*i...) while((s32[]{:T(128)}, ...), condition=%wide.region_7.7_spmd, body=%wide.region_1.6_spmd.sunk | while | flops 341443200 | bytes 38800408 | solution.py:107
  1110.9 35.7 %collective-permute-done.2 = f32[3,256,4,128]{1,3,2,0:T(8,128)} collective-permute-done((f32[3,256,4,128]{1,3,2,0:T(8,128)S(1)}, f32[3,256,4,128]{1,3,2,0:T(8,128)}, u32[]{:S(2)}, u32[]{:S(2)}) %collective-permute-start.2) | collective-permute-done | bytes 1572896 | tf_op jit(solution)/shard_map/while/body/eval_jaxpr/ppermute | solution.py:21
  1176.8 97.9 %while.92 = (s32[]{:T(128)}, f32[3,256,4,128]{1,3,2,0:T(8,128)S(1)}, f32[3,256,4,128]{1,3,2,0:T(8,128)}, f32[3,256,4,128]{1,3,2,0:T(8,128)}, s32[]{:T(128)}, /*i...) while((s32[]{:T(128)}, ...), condition=%wide.region_7.7_spmd, body=%wide.region_1.6_spmd.sunk | while | flops 341443200 | bytes 38800408 | solution.py:107
  1278.5 35.7 %collective-permute-done.2 = f32[3,256,4,128]{1,3,2,0:T(8,128)} collective-permute-done((f32[3,256,4,128]{1,3,2,0:T(8,128)S(1)}, f32[3,256,4,128]{1,3,2,0:T(8,128)}, u32[]{:S(2)}, u32[]{:S(2)}) %collective-permute-start.2) | collective-permute-done | bytes 1572896 | tf_op jit(solution)/shard_map/while/body/eval_jaxpr/ppermute | solution.py:21
  1340.3 82.7 %while.91 = (s32[]{:T(128)}, f32[3,256,4,128]{1,3,2,0:T(8,128)S(1)}, f32[3,256,4,128]{1,3,2,0:T(8,128)}, f32[3,256,4,128]{1,3,2,0:T(8,128)}, s32[]{:T(128)}, /*i...) while((s32[]{:T(128)}, ...), condition=%wide.region_15.16_spmd, body=%wide.region_9.15_spmd.sunk | while | flops 341443200 | bytes 35658724 | solution.py:107
  (1818 shorter events, 1636.5 us)
Async XLA Ops:
  81.8 39.5 %collective-permute-start.2 = (f32[3,256,4,128]{1,3,2,0:T(8,128)S(1)}, f32[3,256,4,128]{1,3,2,0:T(8,128)}, u32[]{:S(2)}, u32[]{:S(2)}) collective-permute-start(f32[3,256,4,128]{1,3,2,0:T(8,128)S(1)} %get-tuple-element.1505), channel_id=1, source_target_pairs={{0,124},{4,0},{8,4},{12,8},{16,12},{20,16},{24,20},{28,24},{32,28}... | collective-permute-start | bytes 4718600 | tf_op jit(solution)/shard_map/while/body/eval_jaxpr/ppermute | solution.py:21
  81.8 56.3 %collective-permute-start = (bf16[3,256,4,128]{3,1,2,0:T(8,128)(2,1)S(1)}, bf16[3,256,4,128]{3,1,2,0:T(8,128)(2,1)}, u32[]{:S(2)}, u32[]{:S(2)}) collective-permute-start(bf16[3,256,4,128]{3,1,2,0:T(8,128)(2,1)S(1)} %get-tuple-element.1726), channel_id=1, source_target_pairs={{4,0},{8,4},{12,8},{16,12},{20,16},{24,20},{28,24},{32,28},{36,32}... | collective-permute-start | bytes 2359304 | tf_op jit(solution)/shard_map/while/body/eval_jaxpr/ppermute | solution.py:16
  84.9 69.0 %collective-permute-start.1 = (bf16[3,256,4,128]{3,1,2,0:T(8,128)(2,1)}, bf16[3,256,4,128]{3,1,2,0:T(8,128)(2,1)}, u32[]{:S(2)}, u32[]{:S(2)}) collective-permute-start(bf16[3,256,4,128]{3,1,2,0:T(8,128)(2,1)} %get-tuple-element.1735), channel_id=1, source_target_pairs={{4,0},{8,4},{12,8},{16,12},{20,16},{24,20},{28,24},{32,28},{36,32}... | collective-permute-start | bytes 2359304 | tf_op jit(solution)/shard_map/while/body/eval_jaxpr/ppermute | solution.py:16
  254.9 39.5 %collective-permute-start.2 = (f32[3,256,4,128]{1,3,2,0:T(8,128)S(1)}, f32[3,256,4,128]{1,3,2,0:T(8,128)}, u32[]{:S(2)}, u32[]{:S(2)}) collective-permute-start(f32[3,256,4,128]{1,3,2,0:T(8,128)S(1)} %get-tuple-element.1505), channel_id=1, source_target_pairs={{0,124},{4,0},{8,4},{12,8},{16,12},{20,16},{24,20},{28,24},{32,28}... | collective-permute-start | bytes 4718600 | tf_op jit(solution)/shard_map/while/body/eval_jaxpr/ppermute | solution.py:21
  254.9 56.4 %collective-permute-start = (bf16[3,256,4,128]{3,1,2,0:T(8,128)(2,1)S(1)}, bf16[3,256,4,128]{3,1,2,0:T(8,128)(2,1)}, u32[]{:S(2)}, u32[]{:S(2)}) collective-permute-start(bf16[3,256,4,128]{3,1,2,0:T(8,128)(2,1)S(1)} %get-tuple-element.1726), channel_id=1, source_target_pairs={{4,0},{8,4},{12,8},{16,12},{20,16},{24,20},{28,24},{32,28},{36,32}... | collective-permute-start | bytes 2359304 | tf_op jit(solution)/shard_map/while/body/eval_jaxpr/ppermute | solution.py:16
  256.8 69.2 %collective-permute-start.1 = (bf16[3,256,4,128]{3,1,2,0:T(8,128)(2,1)}, bf16[3,256,4,128]{3,1,2,0:T(8,128)(2,1)}, u32[]{:S(2)}, u32[]{:S(2)}) collective-permute-start(bf16[3,256,4,128]{3,1,2,0:T(8,128)(2,1)} %get-tuple-element.1735), channel_id=1, source_target_pairs={{4,0},{8,4},{12,8},{16,12},{20,16},{24,20},{28,24},{32,28},{36,32}... | collective-permute-start | bytes 2359304 | tf_op jit(solution)/shard_map/while/body/eval_jaxpr/ppermute | solution.py:16
  427.2 39.5 %collective-permute-start.2 = (f32[3,256,4,128]{1,3,2,0:T(8,128)S(1)}, f32[3,256,4,128]{1,3,2,0:T(8,128)}, u32[]{:S(2)}, u32[]{:S(2)}) collective-permute-start(f32[3,256,4,128]{1,3,2,0:T(8,128)S(1)} %get-tuple-element.1505), channel_id=1, source_target_pairs={{0,124},{4,0},{8,4},{12,8},{16,12},{20,16},{24,20},{28,24},{32,28}... | collective-permute-start | bytes 4718600 | tf_op jit(solution)/shard_map/while/body/eval_jaxpr/ppermute | solution.py:21
  427.2 56.4 %collective-permute-start = (bf16[3,256,4,128]{3,1,2,0:T(8,128)(2,1)S(1)}, bf16[3,256,4,128]{3,1,2,0:T(8,128)(2,1)}, u32[]{:S(2)}, u32[]{:S(2)}) collective-permute-start(bf16[3,256,4,128]{3,1,2,0:T(8,128)(2,1)S(1)} %get-tuple-element.1726), channel_id=1, source_target_pairs={{4,0},{8,4},{12,8},{16,12},{20,16},{24,20},{28,24},{32,28},{36,32}... | collective-permute-start | bytes 2359304 | tf_op jit(solution)/shard_map/while/body/eval_jaxpr/ppermute | solution.py:16
  429.1 68.3 %collective-permute-start.1 = (bf16[3,256,4,128]{3,1,2,0:T(8,128)(2,1)}, bf16[3,256,4,128]{3,1,2,0:T(8,128)(2,1)}, u32[]{:S(2)}, u32[]{:S(2)}) collective-permute-start(bf16[3,256,4,128]{3,1,2,0:T(8,128)(2,1)} %get-tuple-element.1735), channel_id=1, source_target_pairs={{4,0},{8,4},{12,8},{16,12},{20,16},{24,20},{28,24},{32,28},{36,32}... | collective-permute-start | bytes 2359304 | tf_op jit(solution)/shard_map/while/body/eval_jaxpr/ppermute | solution.py:16
  598.5 39.5 %collective-permute-start.2 = (f32[3,256,4,128]{1,3,2,0:T(8,128)S(1)}, f32[3,256,4,128]{1,3,2,0:T(8,128)}, u32[]{:S(2)}, u32[]{:S(2)}) collective-permute-start(f32[3,256,4,128]{1,3,2,0:T(8,128)S(1)} %get-tuple-element.1505), channel_id=1, source_target_pairs={{0,124},{4,0},{8,4},{12,8},{16,12},{20,16},{24,20},{28,24},{32,28}... | collective-permute-start | bytes 4718600 | tf_op jit(solution)/shard_map/while/body/eval_jaxpr/ppermute | solution.py:21
  598.5 56.4 %collective-permute-start = (bf16[3,256,4,128]{3,1,2,0:T(8,128)(2,1)S(1)}, bf16[3,256,4,128]{3,1,2,0:T(8,128)(2,1)}, u32[]{:S(2)}, u32[]{:S(2)}) collective-permute-start(bf16[3,256,4,128]{3,1,2,0:T(8,128)(2,1)S(1)} %get-tuple-element.1726), channel_id=1, source_target_pairs={{4,0},{8,4},{12,8},{16,12},{20,16},{24,20},{28,24},{32,28},{36,32}... | collective-permute-start | bytes 2359304 | tf_op jit(solution)/shard_map/while/body/eval_jaxpr/ppermute | solution.py:16
  600.4 67.4 %collective-permute-start.1 = (bf16[3,256,4,128]{3,1,2,0:T(8,128)(2,1)}, bf16[3,256,4,128]{3,1,2,0:T(8,128)(2,1)}, u32[]{:S(2)}, u32[]{:S(2)}) collective-permute-start(bf16[3,256,4,128]{3,1,2,0:T(8,128)(2,1)} %get-tuple-element.1735), channel_id=1, source_target_pairs={{4,0},{8,4},{12,8},{16,12},{20,16},{24,20},{28,24},{32,28},{36,32}... | collective-permute-start | bytes 2359304 | tf_op jit(solution)/shard_map/while/body/eval_jaxpr/ppermute | solution.py:16
  769.0 39.5 %collective-permute-start.2 = (f32[3,256,4,128]{1,3,2,0:T(8,128)S(1)}, f32[3,256,4,128]{1,3,2,0:T(8,128)}, u32[]{:S(2)}, u32[]{:S(2)}) collective-permute-start(f32[3,256,4,128]{1,3,2,0:T(8,128)S(1)} %get-tuple-element.1505), channel_id=1, source_target_pairs={{0,124},{4,0},{8,4},{12,8},{16,12},{20,16},{24,20},{28,24},{32,28}... | collective-permute-start | bytes 4718600 | tf_op jit(solution)/shard_map/while/body/eval_jaxpr/ppermute | solution.py:21
  769.0 56.4 %collective-permute-start = (bf16[3,256,4,128]{3,1,2,0:T(8,128)(2,1)S(1)}, bf16[3,256,4,128]{3,1,2,0:T(8,128)(2,1)}, u32[]{:S(2)}, u32[]{:S(2)}) collective-permute-start(bf16[3,256,4,128]{3,1,2,0:T(8,128)(2,1)S(1)} %get-tuple-element.1726), channel_id=1, source_target_pairs={{4,0},{8,4},{12,8},{16,12},{20,16},{24,20},{28,24},{32,28},{36,32}... | collective-permute-start | bytes 2359304 | tf_op jit(solution)/shard_map/while/body/eval_jaxpr/ppermute | solution.py:16
  770.9 66.5 %collective-permute-start.1 = (bf16[3,256,4,128]{3,1,2,0:T(8,128)(2,1)}, bf16[3,256,4,128]{3,1,2,0:T(8,128)(2,1)}, u32[]{:S(2)}, u32[]{:S(2)}) collective-permute-start(bf16[3,256,4,128]{3,1,2,0:T(8,128)(2,1)} %get-tuple-element.1735), channel_id=1, source_target_pairs={{4,0},{8,4},{12,8},{16,12},{20,16},{24,20},{28,24},{32,28},{36,32}... | collective-permute-start | bytes 2359304 | tf_op jit(solution)/shard_map/while/body/eval_jaxpr/ppermute | solution.py:16
  938.4 39.5 %collective-permute-start.2 = (f32[3,256,4,128]{1,3,2,0:T(8,128)S(1)}, f32[3,256,4,128]{1,3,2,0:T(8,128)}, u32[]{:S(2)}, u32[]{:S(2)}) collective-permute-start(f32[3,256,4,128]{1,3,2,0:T(8,128)S(1)} %get-tuple-element.1505), channel_id=1, source_target_pairs={{0,124},{4,0},{8,4},{12,8},{16,12},{20,16},{24,20},{28,24},{32,28}... | collective-permute-start | bytes 4718600 | tf_op jit(solution)/shard_map/while/body/eval_jaxpr/ppermute | solution.py:21
  938.4 56.4 %collective-permute-start = (bf16[3,256,4,128]{3,1,2,0:T(8,128)(2,1)S(1)}, bf16[3,256,4,128]{3,1,2,0:T(8,128)(2,1)}, u32[]{:S(2)}, u32[]{:S(2)}) collective-permute-start(bf16[3,256,4,128]{3,1,2,0:T(8,128)(2,1)S(1)} %get-tuple-element.1726), channel_id=1, source_target_pairs={{4,0},{8,4},{12,8},{16,12},{20,16},{24,20},{28,24},{32,28},{36,32}... | collective-permute-start | bytes 2359304 | tf_op jit(solution)/shard_map/while/body/eval_jaxpr/ppermute | solution.py:16
  940.4 65.5 %collective-permute-start.1 = (bf16[3,256,4,128]{3,1,2,0:T(8,128)(2,1)}, bf16[3,256,4,128]{3,1,2,0:T(8,128)(2,1)}, u32[]{:S(2)}, u32[]{:S(2)}) collective-permute-start(bf16[3,256,4,128]{3,1,2,0:T(8,128)(2,1)} %get-tuple-element.1735), channel_id=1, source_target_pairs={{4,0},{8,4},{12,8},{16,12},{20,16},{24,20},{28,24},{32,28},{36,32}... | collective-permute-start | bytes 2359304 | tf_op jit(solution)/shard_map/while/body/eval_jaxpr/ppermute | solution.py:16
  1107.0 39.5 %collective-permute-start.2 = (f32[3,256,4,128]{1,3,2,0:T(8,128)S(1)}, f32[3,256,4,128]{1,3,2,0:T(8,128)}, u32[]{:S(2)}, u32[]{:S(2)}) collective-permute-start(f32[3,256,4,128]{1,3,2,0:T(8,128)S(1)} %get-tuple-element.1505), channel_id=1, source_target_pairs={{0,124},{4,0},{8,4},{12,8},{16,12},{20,16},{24,20},{28,24},{32,28}... | collective-permute-start | bytes 4718600 | tf_op jit(solution)/shard_map/while/body/eval_jaxpr/ppermute | solution.py:21
  1107.0 56.4 %collective-permute-start = (bf16[3,256,4,128]{3,1,2,0:T(8,128)(2,1)S(1)}, bf16[3,256,4,128]{3,1,2,0:T(8,128)(2,1)}, u32[]{:S(2)}, u32[]{:S(2)}) collective-permute-start(bf16[3,256,4,128]{3,1,2,0:T(8,128)(2,1)S(1)} %get-tuple-element.1726), channel_id=1, source_target_pairs={{4,0},{8,4},{12,8},{16,12},{20,16},{24,20},{28,24},{32,28},{36,32}... | collective-permute-start | bytes 2359304 | tf_op jit(solution)/shard_map/while/body/eval_jaxpr/ppermute | solution.py:16
  1108.9 64.6 %collective-permute-start.1 = (bf16[3,256,4,128]{3,1,2,0:T(8,128)(2,1)}, bf16[3,256,4,128]{3,1,2,0:T(8,128)(2,1)}, u32[]{:S(2)}, u32[]{:S(2)}) collective-permute-start(bf16[3,256,4,128]{3,1,2,0:T(8,128)(2,1)} %get-tuple-element.1735), channel_id=1, source_target_pairs={{4,0},{8,4},{12,8},{16,12},{20,16},{24,20},{28,24},{32,28},{36,32}... | collective-permute-start | bytes 2359304 | tf_op jit(solution)/shard_map/while/body/eval_jaxpr/ppermute | solution.py:16
  1274.7 39.5 %collective-permute-start.2 = (f32[3,256,4,128]{1,3,2,0:T(8,128)S(1)}, f32[3,256,4,128]{1,3,2,0:T(8,128)}, u32[]{:S(2)}, u32[]{:S(2)}) collective-permute-start(f32[3,256,4,128]{1,3,2,0:T(8,128)S(1)} %get-tuple-element.1505), channel_id=1, source_target_pairs={{0,124},{4,0},{8,4},{12,8},{16,12},{20,16},{24,20},{28,24},{32,28}... | collective-permute-start | bytes 4718600 | tf_op jit(solution)/shard_map/while/body/eval_jaxpr/ppermute | solution.py:21
  1274.7 56.4 %collective-permute-start = (bf16[3,256,4,128]{3,1,2,0:T(8,128)(2,1)S(1)}, bf16[3,256,4,128]{3,1,2,0:T(8,128)(2,1)}, u32[]{:S(2)}, u32[]{:S(2)}) collective-permute-start(bf16[3,256,4,128]{3,1,2,0:T(8,128)(2,1)S(1)} %get-tuple-element.1726), channel_id=1, source_target_pairs={{4,0},{8,4},{12,8},{16,12},{20,16},{24,20},{28,24},{32,28},{36,32}... | collective-permute-start | bytes 2359304 | tf_op jit(solution)/shard_map/while/body/eval_jaxpr/ppermute | solution.py:16
  1276.6 63.7 %collective-permute-start.1 = (bf16[3,256,4,128]{3,1,2,0:T(8,128)(2,1)}, bf16[3,256,4,128]{3,1,2,0:T(8,128)(2,1)}, u32[]{:S(2)}, u32[]{:S(2)}) collective-permute-start(bf16[3,256,4,128]{3,1,2,0:T(8,128)(2,1)} %get-tuple-element.1735), channel_id=1, source_target_pairs={{4,0},{8,4},{12,8},{16,12},{20,16},{24,20},{28,24},{32,28},{36,32}... | collective-permute-start | bytes 2359304 | tf_op jit(solution)/shard_map/while/body/eval_jaxpr/ppermute | solution.py:16
  (452 other events, 790.0 us)
where the time goes:
time: 1450 us; the launch traced here: 1440 us
  waiting for transfers between devices  516 us (36%)
  matrix products  381 us (26%)
  local copies, waits for them, and re-layouts  240 us (17%)
  loops' own time  153 us (11%)
  other arithmetic  117 us (8%)
  starting transfers between devices  31.8 us (2%)
    ppermute x9, waiting for transfers between devices, passed_along(): lax.ppermute(array, axis, [(i, (i + by) % length) for i in range(length)])  292 us
    ppermute x16, waiting for transfers between devices, from_behind(): return lax.ppermute(array, axis, pairs)  223 us
    cond x888, local copies, waits for them, and re-layouts  142 us
    dot_general x75, matrix products, tile_grads(): jnp.einsum('ihd,jhd->hij', grad_tile, value_tile, preferred_element_type=...  120 us
    another operation x81, loops' own time, pair_step(): return lax.cond(listed, work, lambda unchanged: unchanged, present_value)  101 us
    dot_general x75, matrix products, tile_grads(): jnp.einsum('hij,ihd->jhd', weights, grad_tile, preferred_element_type=jnp...  86.5 us
    dot_general x75, matrix products, tile_grads(): jnp.einsum('hij,ihd->jhd', score_grad, query_tile, preferred_element_type...  79.1 us
    dot_general x75, matrix products, tile_grads(): jnp.einsum('hij,jhd->ihd', score_grad, key_tile, preferred_element_type=j...  66.4 us
  transfers between devices with their start and end apart: 25, of which 25 were waited for; matrix products, arithmetic and copies ran while one was open for 1% of the time, Pallas kernels for 0%

commit v1 on v0

v1 whole, which is shorter than its diff:
```python
import functools
import math

import jax
import jax.numpy as jnp
from jax import lax
from jax.experimental import pallas as pl
from jax.experimental.pallas import tpu as pltpu
from jax.sharding import PartitionSpec as P

F32, BF = jnp.float32, jnp.bfloat16
HEAD, BLK, KPB = 128, 256, 16
PLANE, HALF = 24, 12
AXES = ("ctx", "tp")
U_SCALE = 0.5 / math.sqrt(HEAD)
V_SCALE = 1.0 / math.sqrt(KPB * BLK)
QK_SCALE = 0.5 * V_SCALE / math.sqrt(HEAD)
GROUP = 6
CLASSES = (160, 192, 224, 256)
ENTRIES = 360
DUMMY_Q, DUMMY_K = 24, 36
VMEM = pl.BlockSpec(memory_space=pltpu.VMEM)
SMEM = pl.BlockSpec(memory_space=pltpu.SMEM)
ANY = pl.BlockSpec(memory_space=pl.ANY)


def place(z, x, y, hi, core):
    return (z * 8 + x * 4 + y % 4) * 4 + hi * 2 + core


DEVICES = [
    (z, x, y, hi, core)
    for z in range(4)
    for x in range(2)
    for y in range(4)
    for hi in range(2)
    for core in range(2)
]


def to_heads(d):
    return [(place(z, x, y, hi, c), place(z, c, y + d, hi, x)) for z, x, y, hi, c in DEVICES]


def from_heads(d):
    return [(j, i) for i, j in to_heads(d)]


OTHER_CORE = [(place(z, x, y, hi, c), place(z, x, y, hi, 1 - c)) for z, x, y, hi, c in DEVICES]
ALONG_Z = [
    (place(z, x, y, hi, c), place(z + 2 * c - 1, x, y, hi, c))
    for z, x, y, hi, c in DEVICES
    if 0 <= z + 2 * c - 1 < 4
]
BACK_Z = [(j, i) for i, j in ALONG_Z]


def nt(a, b):
    return lax.dot_general(a, b, (((1,), (1,)), ((), ())), preferred_element_type=F32)


def nn(a, b):
    return lax.dot_general(a, b, (((1,), (0,)), ((), ())), preferred_element_type=F32)


def tn(a, b):
    return lax.dot_general(a, b, (((0,), (0,)), ((), ())), preferred_element_type=F32)


def split_kernel(at, q, g, k, v, *outs):
    y, x = at[0], at[1]
    for d in range(4):
        lanes = pl.ds(pl.multiple_of(lax.rem(y + d, 4) * HEAD, HEAD), HEAD)

        def put(target, pair, lanes=lanes):
            for n, src in enumerate(pair):
                target[n] = src[:, lanes]

        for first, pair in ((0, (q, g)), (1, (k, v))):

            @pl.when(x == first)
            def _(d=d, pair=pair):
                put(outs[d], pair)

            @pl.when(x != first)
            def _(d=d, pair=pair):
                put(outs[4 + d], pair)


def pair_grads(scores, weight_grad, allowed):
    u = scores * U_SCALE
    t = jnp.tanh(u)
    p = jnp.where(allowed, 1.0 + t, 0.0)
    w = u * p
    slope = p + w * (1.0 - t)
    return w.astype(BF), (weight_grad * slope).astype(BF)


def main_kernel(at, tab, cls, nvd, *refs):
    r1, r2 = refs[0:4], refs[4:8]
    beside, across = refs[8:10]
    dq_own, dk_own, dv_own, beside_out, across_out = refs[10:15]
    qs, gs, ks, vs, dqa, dka, dva, sems = refs[15:]
    core, groups = at[2], at[3]

    def copies(own):
        qg, kv = ((r1, r2), (r2, r1))[own]
        out = []
        for d in range(4):
            rows = pl.ds(3 * d, 3)
            out += [
                (qg[d].at[0], qs.at[rows]),
                (qg[d].at[1], gs.at[rows]),
                (kv[d].at[0], ks.at[rows]),
                (kv[d].at[1], vs.at[rows]),
            ]
        out += [(beside.at[0], ks.at[pl.ds(12, 12)]), (beside.at[1], vs.at[pl.ds(12, 12)])]
        if own == 0:
            out += [(across.at[0], qs.at[pl.ds(12, 12)]), (across.at[1], gs.at[pl.ds(12, 12)])]
        else:
            out += [(across.at[0], ks.at[pl.ds(24, 12)]), (across.at[1], vs.at[pl.ds(24, 12)])]
        return [pltpu.make_async_copy(a, b, sems.at[i]) for i, (a, b) in enumerate(out)]

    for own in range(2):

        @pl.when(core == own)
        def _(own=own):
            for copy in copies(own):
                copy.start()

    dqa[...] = jnp.zeros_like(dqa)
    dka[...] = jnp.zeros_like(dka)
    dva[...] = jnp.zeros_like(dva)
    zero = jnp.zeros((BLK, HEAD), BF)
    qs[DUMMY_Q], gs[DUMMY_Q], ks[DUMMY_K], vs[DUMMY_K] = zero, zero, zero, zero

    for own in range(2):

        @pl.when(core == own)
        def _(own=own):
            for copy in copies(own):
                copy.wait()

    def work(items, rows):
        made = []
        for q, k, mask in items:
            key, value, query, grad = ks[k, :rows], vs[k, :rows], qs[q], gs[q]
            made.append((q, k, mask, key, query, grad, nt(key, query), nt(value, grad)))
        for q, k, mask, key, query, grad, scores, weight_grad in made:
            w, sg = pair_grads(scores, weight_grad, mask)
            dva[k, :rows] += nn(w, grad)
            dka[k, :rows] += nn(sg, query)
            dqa[q] += tn(key, sg)

    def own_group(g, _):
        items = []
        row = lax.broadcasted_iota(jnp.int32, (BLK, BLK), 0)
        col = lax.broadcasted_iota(jnp.int32, (BLK, BLK), 1)
        for i in range(4):
            slot = g * 4 + i
            items.append((slot, slot, (row == col) | ((row < col) & (row < nvd[slot]))))
        work(items, BLK)
        return 0

    lax.fori_loop(0, 3, own_group, 0)

    def group(g, _):
        for c, rows in enumerate(CLASSES):

            @pl.when(cls[g] == c)
            def _(rows=rows):
                row = lax.broadcasted_iota(jnp.int32, (rows, BLK), 0)
                items = []
                for i in range(GROUP):
                    e = tab[g * GROUP + i]
                    items.append((e & 31, (e >> 5) & 63, row < ((e >> 11) & 511)))
                work(items, rows)

        return 0

    lax.fori_loop(0, groups, group, 0)

    def finish(s, _):
        dq_own[s] = dqa[s].T * QK_SCALE
        dk_own[s] = dka[s] * QK_SCALE
        dv_own[s] = dva[s] * V_SCALE
        beside_out[0, s] = (dka[12 + s] * QK_SCALE).astype(BF)
        beside_out[1, s] = (dva[12 + s] * V_SCALE).astype(BF)

        @pl.when(core == 0)
        def _():
            across_out[0, s] = (dqa[12 + s].T * QK_SCALE).astype(BF)
            across_out[1, s] = jnp.zeros((BLK, HEAD), BF)

        @pl.when(core == 1)
        def _():
            across_out[0, s] = (dka[24 + s] * QK_SCALE).astype(BF)
            across_out[1, s] = (dva[24 + s] * V_SCALE).astype(BF)

        return 0

    lax.fori_loop(0, 12, finish, 0)


def sum_kernel(at, dq, dk, dv, beside, across, *outs):
    core = at[2]
    for d in range(4):
        for m in range(3):
            s = 3 * d + m
            near = (beside[0, s].astype(F32), beside[1, s].astype(F32))
            far = (across[0, s].astype(F32), across[1, s].astype(F32))
            first = core == 0
            outs[d][0, m] = (dq[s] + jnp.where(first, far[0], 0.0)).astype(BF)
            outs[d][1, m] = (dk[s] + near[0] + jnp.where(first, 0.0, far[0])).astype(BF)
            outs[d][2, m] = (dv[s] + near[1] + jnp.where(first, 0.0, far[1])).astype(BF)


def join_kernel(at, *refs):
    y = at[0]
    for d in range(4):
        lanes = pl.ds(pl.multiple_of(lax.rem(y + d, 4) * HEAD, HEAD), HEAD)
        for n in range(3):
            refs[4 + n][:, lanes] = refs[d][n]


def call(kernel, outs, ins, scratch=(), limit=48, **kw):
    return pl.pallas_call(
        kernel,
        out_shape=outs,
        in_specs=ins,
        out_specs=[VMEM] * len(outs),
        scratch_shapes=scratch,
        compiler_params=pltpu.CompilerParams(vmem_limit_bytes=limit * 2**20),
        **kw,
    )


def tables(key_blocks, target_counts, z, y, core):
    def slot(t):
        return lax.rem(y + 4 - (t % HALF) // 3, 4) * 3 + t % 3

    own = lax.dynamic_slice(key_blocks, (PLANE * z + HALF * core, 0), (HALF, KPB))
    after = lax.dynamic_slice(key_blocks, (jnp.minimum(PLANE * (z + 1), 84), 0), (HALF, KPB))
    kid = jnp.concatenate([own, after])[:, 1:]
    index = jnp.arange(2 * HALF, dtype=jnp.int32)[:, None]
    q_valid = (index < HALF) | ((core == 0) & (z < 3))
    plane = jnp.maximum(kid, 0) // PLANE
    valid = q_valid & (kid >= 0) & ((core == 1) | (plane == z))
    t = jnp.maximum(kid, 0) - PLANE * plane
    ks = slot(t) + jnp.where(plane == z, jnp.where(t // HALF == core, 0, 12), 24)
    qs = jnp.broadcast_to(slot(index % HALF) + jnp.where(index < HALF, 0, 12), kid.shape)
    ids = jnp.arange(96, dtype=jnp.int32)
    counts = jnp.sum(jnp.where(kid[..., None] == ids, target_counts, 0), -1)
    rows = BLK - counts
    cls = jnp.clip((rows + 31) // 32 - 5, 0, 3)
    value = (qs | (ks << 5) | (rows << 11) | (cls << 20)).reshape(-1)
    order = jnp.where(valid, cls, 4).reshape(-1)
    n = jnp.arange(ENTRIES, dtype=jnp.int32)
    before = (order[None, :] < order[:, None]) | (
        (order[None, :] == order[:, None]) & (n[None, :] < n[:, None])
    )
    rank = jnp.sum(before.astype(jnp.int32), 1)
    total = jnp.sum(valid.astype(jnp.int32))
    tab = jnp.sum(jnp.where(rank[None, :] == n[:, None], value[None, :], 0), 1)
    tab = jnp.where(n < total, tab, DUMMY_Q | (DUMMY_K << 5))
    cls_of = jnp.max((tab >> 20).reshape(-1, GROUP), 1)
    s = jnp.arange(HALF, dtype=jnp.int32)
    block = PLANE * z + HALF * core + lax.rem(y + 4 - s // 3, 4) * 3 + s % 3
    nvd = BLK - jnp.sum(jnp.where(block[:, None] == ids, target_counts, 0), -1)
    return tab, cls_of, nvd, (total + GROUP - 1) // GROUP


def body(queries, keys, values, out_grad, key_blocks, target_counts):
    ctx, tp = lax.axis_index("ctx"), lax.axis_index("tp")
    z, x, y, core = ctx // 8, (ctx // 4) % 2, ctx % 4, tp % 2
    tab, cls, nvd, groups = tables(key_blocks, target_counts, z, y, core)
    at = jnp.stack([y, x, core, groups]).astype(jnp.int32)
    rows = queries.shape[0]
    piece = jax.ShapeDtypeStruct((2, rows, HEAD), BF)
    here = jnp.stack([y, x]).astype(jnp.int32)
    sent = call(split_kernel, [piece] * 8, [SMEM] + [VMEM] * 4, name="split")(
        here, queries, out_grad, keys, values
    )
    got = [lax.ppermute(sent[n], AXES, to_heads(n % 4)) for n in range(8)]
    got = [g.reshape(2, 3, BLK, HEAD) for g in got]
    r1, r2 = jnp.concatenate(got[:4], 1), jnp.concatenate(got[4:], 1)
    across = lax.ppermute(r1, AXES, ALONG_Z)
    beside = lax.ppermute(jnp.where(core == 0, r2, r1), AXES, OTHER_CORE)
    half = jax.ShapeDtypeStruct((HALF, BLK, HEAD), F32)
    two = jax.ShapeDtypeStruct((2, HALF, BLK, HEAD), BF)
    dq, dk, dv, beside_out, across_out = call(
        main_kernel,
        [half, half, half, two, two],
        [SMEM] * 4 + [ANY] * 10,
        [
            pltpu.VMEM((25, BLK, HEAD), BF),
            pltpu.VMEM((25, BLK, HEAD), BF),
            pltpu.VMEM((37, BLK, HEAD), BF),
            pltpu.VMEM((37, BLK, HEAD), BF),
            pltpu.VMEM((25, HEAD, BLK), F32),
            pltpu.VMEM((37, BLK, HEAD), F32),
            pltpu.VMEM((37, BLK, HEAD), F32),
            pltpu.SemaphoreType.DMA((20,)),
        ],
        name="grads",
    )(at, tab, cls, nvd, *got, beside, across)
    beside = lax.ppermute(beside_out, AXES, OTHER_CORE)
    across = lax.ppermute(across_out, AXES, BACK_Z)
    three = jax.ShapeDtypeStruct((3, 3, BLK, HEAD), BF)
    sums = call(sum_kernel, [three] * 4, [SMEM] + [VMEM] * 5, name="sums")(
        at, dq, dk, dv, beside, across
    )
    back = [lax.ppermute(s.reshape(3, rows, HEAD), AXES, from_heads(d)) for d, s in enumerate(sums)]
    out = jax.ShapeDtypeStruct(queries.shape, BF)
    return tuple(call(join_kernel, [out] * 3, [SMEM] + [VMEM] * 4, name="join")(here, *back))


def solution(mesh):
    in_specs = (P("ctx", "tp"),) * 4 + (P(), P())
    return jax.shard_map(
        body, mesh=mesh, in_specs=in_specs, out_specs=(P("ctx", "tp"),) * 3, check_vma=False
    )
```

time: 1450 us -> 192 us (0.13)
  the two profiles are of different devices: /device:TPU:92 before, /device:TPU:7 now
where the time goes in v1:
time: 192 us; the launch traced here: 191 us
  waiting for transfers between devices  75.7 us (39%)
  Pallas kernels  57.2 us (30%)
  starting transfers between devices  43.9 us (23%)
  local copies, waits for them, and re-layouts  6.54 us (3%)
  other arithmetic  5.98 us (3%)
    pallas_call x1, Pallas kernels, body(): call(main_kernel, [half, half, half, two, two], [SMEM] * 4 + [ANY] * 10,...  48.9 us
    ppermute x4, waiting for transfers between devices, body(): lax.ppermute(s.reshape(3, rows, HEAD), AXES, from_heads(d))  27.4 us
    ppermute x8, starting transfers between devices, body(): got = [lax.ppermute(sent[n], AXES, to_heads(n % 4)) for n in range(8)]  22.3 us
    ppermute x1, waiting for transfers between devices, body(): across = lax.ppermute(across_out, AXES, BACK_Z)  18.1 us
    ppermute x8, waiting for transfers between devices, body(): got = [lax.ppermute(sent[n], AXES, to_heads(n % 4)) for n in range(8)]  15.7 us
    ppermute x1, waiting for transfers between devices, body(): across = lax.ppermute(r1, AXES, ALONG_Z)  12.5 us
    ppermute x1, starting transfers between devices, body(): beside = lax.ppermute(beside_out, AXES, OTHER_CORE)  10.6 us
    unnamed x16, local copies, waits for them, and re-layouts  5.96 us
  transfers between devices with their start and end apart: 16, of which 8 were waited for; matrix products, arithmetic and copies ran while one was open for 2% of the time, Pallas kernels for 0%

profile of v1, /device:TPU:7, one launch (start us, length us, event | category | flops | bytes accessed | tf_op | source)
XLA Modules:
  0.0 190.7 jit_solution(2369047541520735726)
XLA Ops:
  0.7 1.1 copy-done.1
  4.1 2.9 %split.1 = (bf16[2,768,128]{2,1,0:T(8,128)(2,1)S(1)}, bf16[2,768,128]{2,1,0:T(8,128)(2,1)S(1)}, bf16[2,768,128]{2,1,0:T(8,128)(2,1)S(1)}, bf16[2,768,128]{2,1,0:...) custom-call(s32[2]{0:T(128)S(1)} %pad_add_fusion.1.at, ...), custom_call_target="tpu_custom_call" | custom-call | tf_op jit(solution)/shard_map/split/pallas_call | solution.py:281
  7.7 1.4 collective-permute-start.1
  9.1 2.6 %collective-permute-start.2 = (bf16[2,768,128]{2,1,0:T(8,128)(2,1)S(1)}, bf16[2,768,128]{2,1,0:T(8,128)(2,1)S(1)}, u32[]{:S(2)}, u32[]{:S(2)}) collective-permute-start(bf16[2,768,128]{2,1,0:T(8,128)(2,1)S(1)} %get-tuple-element.22), channel_id=1, source_target_pairs={{0,8},{1,24},{2,10},{3,26},{4,12},{5,28},{6,14},{7,30},{8,0},{9,16... | collective-permute-start | bytes 1179656 | tf_op jit(solution)/shard_map/ppermute | solution.py:284
  12.8 1.6 collective-permute-start.4
  15.7 14.6 %collective-permute-start.6 = (bf16[2,768,128]{2,1,0:T(8,128)(2,1)}, bf16[2,768,128]{2,1,0:T(8,128)(2,1)S(1)}, u32[]{:S(2)}, u32[]{:S(2)}) collective-permute-start(bf16[2,768,128]{2,1,0:T(8,128)(2,1)} %get-tuple-element.26), channel_id=1, source_target_pairs={{0,8},{1,24},{2,10},{3,26},{4,12},{5,28},{6,14},{7,30},{8,0},{9,16... | collective-permute-start | bytes 1179656 | tf_op jit(solution)/shard_map/ppermute | solution.py:284
  31.6 2.1 %collective-permute-done.5 = bf16[2,768,128]{2,1,0:T(8,128)(2,1)S(1)} collective-permute-done((bf16[2,768,128]{2,1,0:T(8,128)(2,1)}, bf16[2,768,128]{2,1,0:T(8,128)(2,1)S(1)}, u32[]{:S(2)}, u32[]{:S(2)}) %collective-permute-start.5) | collective-permute-done | bytes 393248 | tf_op jit(solution)/shard_map/ppermute | solution.py:284
  33.7 12.7 %collective-permute-done.6 = bf16[2,768,128]{2,1,0:T(8,128)(2,1)S(1)} collective-permute-done((bf16[2,768,128]{2,1,0:T(8,128)(2,1)}, bf16[2,768,128]{2,1,0:T(8,128)(2,1)S(1)}, u32[]{:S(2)}, u32[]{:S(2)}) %collective-permute-start.6) | collective-permute-done | bytes 393248 | tf_op jit(solution)/shard_map/ppermute | solution.py:284
  46.4 1.9 pad_maximum_fusion
  48.3 4.7 %collective-permute-start.9 = (bf16[2,12,256,128]{3,2,1,0:T(8,128)(2,1)}, bf16[2,12,256,128]{3,2,1,0:T(8,128)(2,1)}, u32[]{:S(2)}, u32[]{:S(2)}) collective-permute-start(bf16[2,12,256,128]{3,2,1,0:T(8,128)(2,1)} %get-tuple-element.39), channel_id=1, source_target_pairs={{1,33},{3,35},{5,37},{7,39},{9,41},{11,43},{13,45},{15,47},{17,49}... | collective-permute-start | bytes 4718600 | tf_op jit(solution)/shard_map/ppermute | solution.py:287
  57.0 12.5 %collective-permute-done.9.refs_9_ = bf16[2,12,256,128]{3,2,1,0:T(8,128)(2,1)} collective-permute-done((bf16[2,12,256,128]{3,2,1,0:T(8,128)(2,1)}, bf16[2,12,256,128]{3,2,1,0:T(8,128)(2,1)}, u32[]{:S(2)}, u32[]{:S(2)}) %collective-permute-start.9) | collective-permute-done | bytes 1572896 | tf_op jit(solution)/shard_map/ppermute | solution.py:287
  69.5 48.9 %grads.1 = (f32[12,256,128]{2,1,0:T(8,128)S(1)}, f32[12,256,128]{2,1,0:T(8,128)}, f32[12,256,128]{2,1,0:T(8,128)}, bf16[2,12,256,128]{3,2,1,0:T(8,128)(2,1)}, bf16[2,12,256,128]{3,2,1,0:T(8,128)(2,1)}) custom-call(s32[4]{0:T(128)S(1)} %pad_add_fusion.2.at, s32[360]{0:T(512)S(1)} %fusion.19.tab, s32[60]{0:T(128)S(1)} %shift-right-arithmetic_reduce_fusion.cls, ...), custom_call_target="tpu_custom_call" | custom-call | tf_op jit(solution)/shard_map/grads/pallas_call | solution.py:291
  118.4 10.6 %collective-permute-start.10 = (bf16[2,12,256,128]{3,2,1,0:T(8,128)(2,1)}, bf16[2,12,256,128]{3,2,1,0:T(8,128)(2,1)S(1)}, u32[]{:S(2)}, u32[]{:S(2)}) collective-permute-start(bf16[2,12,256,128]{3,2,1,0:T(8,128)(2,1)} %get-tuple-element.31), channel_id=1, source_target_pairs={{0,1},{1,0},{2,3},{3,2},{4,5},{5,4},{6,7},{7,6},{8,9},{9,8},{10,11... | collective-permute-start | bytes 4718600 | tf_op jit(solution)/shard_map/ppermute | solution.py:307
  128.9 1.3 collective-permute-start.11
  130.2 2.0 %collective-permute-done.10.beside = bf16[2,12,256,128]{3,2,1,0:T(8,128)(2,1)S(1)} collective-permute-done((bf16[2,12,256,128]{3,2,1,0:T(8,128)(2,1)}, bf16[2,12,256,128]{3,2,1,0:T(8,128)(2,1)S(1)}, u32[]{:S(2)}, u32[]{:S(2)}) %collective-permute-start.10) | collective-permute-done | bytes 1572896 | tf_op jit(solution)/shard_map/ppermute | solution.py:307
  132.2 18.1 %collective-permute-done.11.across = bf16[2,12,256,128]{3,2,1,0:T(8,128)(2,1)S(1)} collective-permute-done((bf16[2,12,256,128]{3,2,1,0:T(8,128)(2,1)}, bf16[2,12,256,128]{3,2,1,0:T(8,128)(2,1)S(1)}, u32[]{:S(2)}, u32[]{:S(2)}) %collective-permute-start.11) | collective-permute-done | bytes 1572896 | tf_op jit(solution)/shard_map/ppermute | solution.py:308
  150.3 1.1 copy-done.5
  151.4 1.4 copy-done
  152.9 3.1 %sums.1 = (bf16[3,3,256,128]{3,2,1,0:T(8,128)(2,1)S(1)}, bf16[3,3,256,128]{3,2,1,0:T(8,128)(2,1)S(1)}, bf16[3,3,256,128]{3,2,1,0:T(8,128)(2,1)S(1)}, bf16[3,3,256,128]{3,2,1,0:T(8,128)(2,1)S(1)}) custom-call(s32[4]{0:T(128)S(1)} %pad_add_fusion.2.at, f32[12,256,128]{2,1,0:T(8,128)S(1)} %get-tuple-element.28.dq, f32[12,256,128]{2,1,0:T(8,128)S(1)} %copy-done, ...), custom_call_target="tpu_custom_call" | custom-call | tf_op jit(solution)/shard_map/sums/pallas_call | solution.py:310
  155.9 2.5 %collective-permute-start.13 = (bf16[3,768,128]{2,1,0:T(8,128)(2,1)S(1)}, bf16[3,768,128]{2,1,0:T(8,128)(2,1)S(1)}, u32[]{:S(2)}, u32[]{:S(2)}) collective-permute-start(bf16[3,768,128]{2,1,0:T(8,128)(2,1)S(1)} %bitcast.35), channel_id=1, source_target_pairs={{4,0},{20,1},{6,2},{22,3},{8,4},{24,5},{10,6},{26,7},{12,8},{28,9}... | collective-permute-start | bytes 1769480 | tf_op jit(solution)/shard_map/ppermute | solution.py:313
  159.1 1.8 collective-permute-start.14
  160.9 23.0 %collective-permute-done.13.refs_1_ = bf16[3,768,128]{2,1,0:T(8,128)(2,1)S(1)} collective-permute-done((bf16[3,768,128]{2,1,0:T(8,128)(2,1)S(1)}, bf16[3,768,128]{2,1,0:T(8,128)(2,1)S(1)}, u32[]{:S(2)}, u32[]{:S(2)}) %collective-permute-start.13) | collective-permute-done | bytes 589856 | tf_op jit(solution)/shard_map/ppermute | solution.py:313
  184.0 4.4 %collective-permute-done.15.refs_3_ = bf16[3,768,128]{2,1,0:T(8,128)(2,1)S(1)} collective-permute-done((bf16[3,768,128]{2,1,0:T(8,128)(2,1)S(1)}, bf16[3,768,128]{2,1,0:T(8,128)(2,1)S(1)}, u32[]{:S(2)}, u32[]{:S(2)}) %collective-permute-start.15) | collective-permute-done | bytes 589856 | tf_op jit(solution)/shard_map/ppermute | solution.py:313
  188.4 2.3 %join.1 = (bf16[768,512]{1,0:T(8,128)(2,1)}, bf16[768,512]{1,0:T(8,128)(2,1)}, bf16[768,512]{1,0:T(8,128)(2,1)}) custom-call(s32[2]{0:T(128)S(1)} %pad_add_fusion.1.at, bf16[3,768,128]{2,1,0:T(8,128)(2,1)S(1)} %collective-permute-done.12.refs_0_, bf16[3,768,128]{2,1,0:T(8,128)(2,1)S(1)} %collective-permute-done.13.refs_1_, ...), custom_call_target="tpu_custom_call" | custom-call | tf_op jit(solution)/shard_map/join/pallas_call | solution.py:315
  (50 shorter events, 10.7 us)
Async XLA Ops:
  0.7 1.1 copy-start.1
  1.9 1.1 copy-start.2
  3.0 1.1 copy-start.3
  4.1 26.1 %copy-start.6 = (s32[96,16]{0,1:T(8,128)S(1)}, s32[96,16]{0,1:T(8,128)}, u32[]{:S(2)}) copy-start(s32[96,16]{0,1:T(8,128)} %param.10) | copy-start | bytes 18436
  7.0 7.4 %collective-permute-start = (bf16[2,768,128]{2,1,0:T(8,128)(2,1)S(1)}, bf16[2,768,128]{2,1,0:T(8,128)(2,1)S(1)}, u32[]{:S(2)}, u32[]{:S(2)}) collective-permute-start(bf16[2,768,128]{2,1,0:T(8,128)(2,1)S(1)} %get-tuple-element.20), channel_id=1, source_target_pairs={{0,0},{1,16},{2,2},{3,18},{4,4},{5,20},{6,6},{7,22},{8,8},{9,24},{... | collective-permute-start | bytes 1179656 | tf_op jit(solution)/shard_map/ppermute | solution.py:284
  7.7 8.0 %collective-permute-start.1 = (bf16[2,768,128]{2,1,0:T(8,128)(2,1)S(1)}, bf16[2,768,128]{2,1,0:T(8,128)(2,1)S(1)}, u32[]{:S(2)}, u32[]{:S(2)}) collective-permute-start(bf16[2,768,128]{2,1,0:T(8,128)(2,1)S(1)} %get-tuple-element.21), channel_id=1, source_target_pairs={{0,4},{1,20},{2,6},{3,22},{4,8},{5,24},{6,10},{7,26},{8,12},{9,28}... | collective-permute-start | bytes 1179656 | tf_op jit(solution)/shard_map/ppermute | solution.py:284
  9.1 21.2 %collective-permute-start.2 = (bf16[2,768,128]{2,1,0:T(8,128)(2,1)S(1)}, bf16[2,768,128]{2,1,0:T(8,128)(2,1)S(1)}, u32[]{:S(2)}, u32[]{:S(2)}) collective-permute-start(bf16[2,768,128]{2,1,0:T(8,128)(2,1)S(1)} %get-tuple-element.22), channel_id=1, source_target_pairs={{0,8},{1,24},{2,10},{3,26},{4,12},{5,28},{6,14},{7,30},{8,0},{9,16... | collective-permute-start | bytes 1179656 | tf_op jit(solution)/shard_map/ppermute | solution.py:284
  11.7 19.9 %collective-permute-start.3 = (bf16[2,768,128]{2,1,0:T(8,128)(2,1)}, bf16[2,768,128]{2,1,0:T(8,128)(2,1)S(1)}, u32[]{:S(2)}, u32[]{:S(2)}) collective-permute-start(bf16[2,768,128]{2,1,0:T(8,128)(2,1)} %get-tuple-element.23), channel_id=1, source_target_pairs={{0,12},{1,28},{2,14},{3,30},{4,0},{5,16},{6,2},{7,18},{8,4},{9,20}... | collective-permute-start | bytes 1179656 | tf_op jit(solution)/shard_map/ppermute | solution.py:284
  12.8 18.8 %collective-permute-start.4 = (bf16[2,768,128]{2,1,0:T(8,128)(2,1)}, bf16[2,768,128]{2,1,0:T(8,128)(2,1)S(1)}, u32[]{:S(2)}, u32[]{:S(2)}) collective-permute-start(bf16[2,768,128]{2,1,0:T(8,128)(2,1)} %get-tuple-element.24), channel_id=1, source_target_pairs={{0,0},{1,16},{2,2},{3,18},{4,4},{5,20},{6,6},{7,22},{8,8},{9,24},{... | collective-permute-start | bytes 1179656 | tf_op jit(solution)/shard_map/ppermute | solution.py:284
  14.4 19.3 %collective-permute-start.5 = (bf16[2,768,128]{2,1,0:T(8,128)(2,1)}, bf16[2,768,128]{2,1,0:T(8,128)(2,1)S(1)}, u32[]{:S(2)}, u32[]{:S(2)}) collective-permute-start(bf16[2,768,128]{2,1,0:T(8,128)(2,1)} %get-tuple-element.25), channel_id=1, source_target_pairs={{0,4},{1,20},{2,6},{3,22},{4,8},{5,24},{6,10},{7,26},{8,12},{9,28}... | collective-permute-start | bytes 1179656 | tf_op jit(solution)/shard_map/ppermute | solution.py:284
  15.7 30.7 %collective-permute-start.6 = (bf16[2,768,128]{2,1,0:T(8,128)(2,1)}, bf16[2,768,128]{2,1,0:T(8,128)(2,1)S(1)}, u32[]{:S(2)}, u32[]{:S(2)}) collective-permute-start(bf16[2,768,128]{2,1,0:T(8,128)(2,1)} %get-tuple-element.26), channel_id=1, source_target_pairs={{0,8},{1,24},{2,10},{3,26},{4,12},{5,28},{6,14},{7,30},{8,0},{9,16... | collective-permute-start | bytes 1179656 | tf_op jit(solution)/shard_map/ppermute | solution.py:284
  30.3 16.1 %collective-permute-start.7 = (bf16[2,768,128]{2,1,0:T(8,128)(2,1)S(1)}, bf16[2,768,128]{2,1,0:T(8,128)(2,1)S(1)}, u32[]{:S(2)}, u32[]{:S(2)}) collective-permute-start(bf16[2,768,128]{2,1,0:T(8,128)(2,1)S(1)} %get-tuple-element.27), channel_id=1, source_target_pairs={{0,12},{1,28},{2,14},{3,30},{4,0},{5,16},{6,2},{7,18},{8,4},{9,20}... | collective-permute-start | bytes 1179656 | tf_op jit(solution)/shard_map/ppermute | solution.py:284
  46.4 9.0 %copy-start.7 = (s32[96]{0:T(128)S(1)}, s32[96]{0:T(128)}, u32[]{:S(2)}) copy-start(s32[96]{0:T(128)} %param.11) | copy-start | bytes 1156
  48.3 21.2 %collective-permute-start.9 = (bf16[2,12,256,128]{3,2,1,0:T(8,128)(2,1)}, bf16[2,12,256,128]{3,2,1,0:T(8,128)(2,1)}, u32[]{:S(2)}, u32[]{:S(2)}) collective-permute-start(bf16[2,12,256,128]{3,2,1,0:T(8,128)(2,1)} %get-tuple-element.39), channel_id=1, source_target_pairs={{1,33},{3,35},{5,37},{7,39},{9,41},{11,43},{13,45},{15,47},{17,49}... | collective-permute-start | bytes 4718600 | tf_op jit(solution)/shard_map/ppermute | solution.py:287
  53.0 16.5 %collective-permute-start.8 = (bf16[2,12,256,128]{3,2,1,0:T(8,128)(2,1)}, bf16[2,12,256,128]{3,2,1,0:T(8,128)(2,1)}, u32[]{:S(2)}, u32[]{:S(2)}) collective-permute-start(bf16[2,12,256,128]{3,2,1,0:T(8,128)(2,1)} %get-tuple-element.40), channel_id=1, source_target_pairs={{0,1},{1,0},{2,3},{3,2},{4,5},{5,4},{6,7},{7,6},{8,9},{9,8},{10,11... | collective-permute-start | bytes 4718600 | tf_op jit(solution)/shard_map/ppermute | solution.py:288
  118.4 13.8 %collective-permute-start.10 = (bf16[2,12,256,128]{3,2,1,0:T(8,128)(2,1)}, bf16[2,12,256,128]{3,2,1,0:T(8,128)(2,1)S(1)}, u32[]{:S(2)}, u32[]{:S(2)}) collective-permute-start(bf16[2,12,256,128]{3,2,1,0:T(8,128)(2,1)} %get-tuple-element.31), channel_id=1, source_target_pairs={{0,1},{1,0},{2,3},{3,2},{4,5},{5,4},{6,7},{7,6},{8,9},{9,8},{10,11... | collective-permute-start | bytes 4718600 | tf_op jit(solution)/shard_map/ppermute | solution.py:307
  128.9 21.4 %collective-permute-start.11 = (bf16[2,12,256,128]{3,2,1,0:T(8,128)(2,1)}, bf16[2,12,256,128]{3,2,1,0:T(8,128)(2,1)S(1)}, u32[]{:S(2)}, u32[]{:S(2)}) collective-permute-start(bf16[2,12,256,128]{3,2,1,0:T(8,128)(2,1)} %get-tuple-element.32), channel_id=1, source_target_pairs={{33,1},{35,3},{37,5},{39,7},{41,9},{43,11},{45,13},{47,15},{49,17}... | collective-permute-start | bytes 4718600 | tf_op jit(solution)/shard_map/ppermute | solution.py:308
  132.2 18.1 %copy-start.4 = (bf16[2,12,256,128]{3,2,1,0:T(8,128)(2,1)}, bf16[2,12,256,128]{3,2,1,0:T(8,128)(2,1)S(1)}, u32[]{:S(2)}) copy-start(bf16[2,12,256,128]{3,2,1,0:T(8,128)(2,1)S(1)} %collective-permute-done.10.beside) | copy-start | bytes 4718596
  150.3 1.1 copy-start.5
  151.4 1.4 copy-start
  155.9 28.0 %collective-permute-start.13 = (bf16[3,768,128]{2,1,0:T(8,128)(2,1)S(1)}, bf16[3,768,128]{2,1,0:T(8,128)(2,1)S(1)}, u32[]{:S(2)}, u32[]{:S(2)}) collective-permute-start(bf16[3,768,128]{2,1,0:T(8,128)(2,1)S(1)} %bitcast.35), channel_id=1, source_target_pairs={{4,0},{20,1},{6,2},{22,3},{8,4},{24,5},{10,6},{26,7},{12,8},{28,9}... | collective-permute-start | bytes 1769480 | tf_op jit(solution)/shard_map/ppermute | solution.py:313
  158.4 25.5 %collective-permute-start.12 = (bf16[3,768,128]{2,1,0:T(8,128)(2,1)S(1)}, bf16[3,768,128]{2,1,0:T(8,128)(2,1)S(1)}, u32[]{:S(2)}, u32[]{:S(2)}) collective-permute-start(bf16[3,768,128]{2,1,0:T(8,128)(2,1)S(1)} %bitcast.34), channel_id=1, source_target_pairs={{0,0},{16,1},{2,2},{18,3},{4,4},{20,5},{6,6},{22,7},{8,8},{24,9},{... | collective-permute-start | bytes 1769480 | tf_op jit(solution)/shard_map/ppermute | solution.py:313
  159.1 24.9 %collective-permute-start.14 = (bf16[3,768,128]{2,1,0:T(8,128)(2,1)S(1)}, bf16[3,768,128]{2,1,0:T(8,128)(2,1)S(1)}, u32[]{:S(2)}, u32[]{:S(2)}) collective-permute-start(bf16[3,768,128]{2,1,0:T(8,128)(2,1)S(1)} %bitcast.33), channel_id=1, source_target_pairs={{8,0},{24,1},{10,2},{26,3},{12,4},{28,5},{14,6},{30,7},{0,8},{16,9... | collective-permute-start | bytes 1769480 | tf_op jit(solution)/shard_map/ppermute | solution.py:313
  160.9 27.4 %collective-permute-start.15 = (bf16[3,768,128]{2,1,0:T(8,128)(2,1)S(1)}, bf16[3,768,128]{2,1,0:T(8,128)(2,1)S(1)}, u32[]{:S(2)}, u32[]{:S(2)}) collective-permute-start(bf16[3,768,128]{2,1,0:T(8,128)(2,1)S(1)} %bitcast.32), channel_id=1, source_target_pairs={{12,0},{28,1},{14,2},{30,3},{0,4},{16,5},{2,6},{18,7},{4,8},{20,9}... | collective-permute-start | bytes 1769480 | tf_op jit(solution)/shard_map/ppermute | solution.py:313

commit v2 on v1

v2 whole, which is shorter than its diff:
```python
import functools
import math

import jax
import jax.numpy as jnp
from jax import lax
from jax.experimental import pallas as pl
from jax.experimental.pallas import tpu as pltpu
from jax.sharding import PartitionSpec as P

F32, BF = jnp.float32, jnp.bfloat16
HEAD, BLK, KPB = 128, 256, 16
PLANE, HALF = 24, 12
AXES = ("ctx", "tp")
U_SCALE = 0.5 / math.sqrt(HEAD)
V_SCALE = 1.0 / math.sqrt(KPB * BLK)
QK_SCALE = 0.5 * V_SCALE / math.sqrt(HEAD)
GROUP = 6
CLASSES = (160, 192, 224, 256)
ENTRIES = 180
LISTED = ENTRIES // GROUP
DUMMY = (24, 12)
VMEM = pl.BlockSpec(memory_space=pltpu.VMEM)
SMEM = pl.BlockSpec(memory_space=pltpu.SMEM)
ANY = pl.BlockSpec(memory_space=pl.ANY)


def place(z, x, y, hi, core):
    return (z * 8 + x * 4 + y % 4) * 4 + hi * 2 + core


DEVICES = [
    (z, x, y, hi, core)
    for z in range(4)
    for x in range(2)
    for y in range(4)
    for hi in range(2)
    for core in range(2)
]


def to_heads(d):
    return [(place(z, x, y, hi, c), place(z, c, y + d, hi, x)) for z, x, y, hi, c in DEVICES]


def from_heads(d):
    return [(j, i) for i, j in to_heads(d)]


OTHER_CORE = [(place(z, x, y, hi, c), place(z, x, y, hi, 1 - c)) for z, x, y, hi, c in DEVICES]
TO_FIRST = [(place(z, x, y, hi, 1), place(z, x, y, hi, 0)) for z, x, y, hi, c in DEVICES if c]
TO_SECOND = [(j, i) for i, j in TO_FIRST]
ALONG_Z = [
    (place(z, x, y, hi, c), place(z + 2 * c - 1, x, y, hi, c))
    for z, x, y, hi, c in DEVICES
    if 0 <= z + 2 * c - 1 < 4
]
BACK_Z = [(j, i) for i, j in ALONG_Z]
BACK_Z_SECOND = [(j, i) for j, i in BACK_Z if i % 2]


def nt(a, b):
    return lax.dot_general(a, b, (((1,), (1,)), ((), ())), preferred_element_type=F32)


def nn(a, b):
    return lax.dot_general(a, b, (((1,), (0,)), ((), ())), preferred_element_type=F32)


def tn(a, b):
    return lax.dot_general(a, b, (((0,), (0,)), ((), ())), preferred_element_type=F32)


def split_kernel(first_round, at, q, g, k, v, *refs):
    outs, sems = refs[:4], refs[4]
    y, x = at[0], at[1]

    def copies(pair):
        made = []
        for d in range(4):
            lanes = pl.ds(pl.multiple_of(lax.rem(y + d, 4) * HEAD, HEAD), HEAD)
            for n in range(2):
                made.append(
                    pltpu.make_async_copy(
                        pair[n].at[:, lanes], outs[d].at[n], sems.at[2 * d + n]
                    )
                )
        return made

    for side, pair in ((0, (q, g)), (1, (k, v))):

        @pl.when(x == (side if first_round else 1 - side))
        def _(pair=pair):
            made = copies(pair)
            for copy in made:
                copy.start()
            for copy in made:
                copy.wait()


def gather_kernel(*refs):
    ins, out, sems = refs[:4], refs[4], refs[5]
    made = [
        pltpu.make_async_copy(ins[d], out.at[:, pl.ds(3 * d, 3)], sems.at[d]) for d in range(4)
    ]
    for copy in made:
        copy.start()
    for copy in made:
        copy.wait()


def pair_grads(scores, weight_grad, allowed):
    u = scores * U_SCALE
    t = jnp.tanh(u)
    p = jnp.where(allowed, 1.0 + t, 0.0)
    w = u * p
    slope = p + w * (1.0 - t)
    return w.astype(BF), (weight_grad * slope).astype(BF)


def pairs_kernel(phase, at, tab, cls, nvd, *refs):
    r1, r2 = refs[0:4], refs[4:8]
    extra = refs[8:10] if phase else refs[8:11]
    refs = refs[10:] if phase else refs[11:]
    if phase:
        dq_out, dk_out, dv_out = refs[:3]
        refs = refs[3:]
        qs, gs, ks, vs, dqa, dka, dva, s1, s2, sems = refs
    else:
        p1_out, p2_out, s1_out, s2_out, beside_out = refs[:5]
        qs, gs, ks, vs, dqa, dka, dva, sems = refs[5:]
    core, groups = at[2], at[3 + phase]
    low, high = pl.ds(0, HALF), pl.ds(HALF, HALF)

    def copies(own):
        qg, kv = ((r1, r2), (r2, r1))[own]
        out = []
        for d in range(4):
            rows = pl.ds(3 * d, 3)
            if phase == 1 or own == 1:
                out += [(qg[d].at[0], qs.at[rows]), (qg[d].at[1], gs.at[rows])]
            if phase == 1 or own == 0:
                out += [(kv[d].at[0], ks.at[rows]), (kv[d].at[1], vs.at[rows])]
        if phase == 0:
            across, beside = extra[0], extra[1 + own]
            out += [(beside.at[0], ks.at[high]), (beside.at[1], vs.at[high])]
            if own == 0:
                out += [(across.at[0], qs.at[low]), (across.at[1], gs.at[low])]
            else:
                out += [(across.at[0], ks.at[low]), (across.at[1], vs.at[low])]
        return [pltpu.make_async_copy(a, b, sems.at[i]) for i, (a, b) in enumerate(out)]

    def late():
        return [
            pltpu.make_async_copy(extra[0], s1, sems.at[20]),
            pltpu.make_async_copy(extra[1], s2, sems.at[21]),
        ]

    for own in range(2):

        @pl.when(core == own)
        def _(own=own):
            for copy in copies(own):
                copy.start()

    if phase:
        for copy in late():
            copy.start()
    dqa[...] = jnp.zeros_like(dqa)
    dka[...] = jnp.zeros_like(dka)
    dva[...] = jnp.zeros_like(dva)
    zero = jnp.zeros((BLK, HEAD), BF)
    dummy = DUMMY[phase]
    qs[HALF], gs[HALF], ks[dummy], vs[dummy] = zero, zero, zero, zero

    for own in range(2):

        @pl.when(core == own)
        def _(own=own):
            for copy in copies(own):
                copy.wait()

    def work(items, rows):
        made = []
        for q, k, mask in items:
            key, value, query, grad = ks[k, :rows], vs[k, :rows], qs[q], gs[q]
            made.append((q, k, mask, key, query, grad, nt(key, query), nt(value, grad)))
        for q, k, mask, key, query, grad, scores, weight_grad in made:
            w, sg = pair_grads(scores, weight_grad, mask)
            dva[k, :rows] += nn(w, grad)
            dka[k, :rows] += nn(sg, query)
            dqa[q] += tn(key, sg)

    def own_group(g, _):
        items = []
        row = lax.broadcasted_iota(jnp.int32, (BLK, BLK), 0)
        col = lax.broadcasted_iota(jnp.int32, (BLK, BLK), 1)
        for i in range(4):
            slot = g * 4 + i
            items.append((slot, slot, (row == col) | ((row < col) & (row < nvd[slot]))))
        work(items, BLK)
        return 0

    if phase:
        lax.fori_loop(0, 3, own_group, 0)

    def group(g, _):
        for c, rows in enumerate(CLASSES):

            @pl.when(cls[phase * LISTED + g] == c)
            def _(rows=rows):
                row = lax.broadcasted_iota(jnp.int32, (rows, BLK), 0)
                items = []
                for i in range(GROUP):
                    e = tab[phase * ENTRIES + g * GROUP + i]
                    items.append((e & 15, (e >> 4) & 31, row < ((e >> 9) & 511)))
                work(items, rows)

        return 0

    lax.fori_loop(0, groups, group, 0)

    if phase:
        for copy in late():
            copy.wait()

    def finish(s, _):
        dq, dk, dv = dqa[s].T * QK_SCALE, dka[s] * QK_SCALE, dva[s] * V_SCALE
        if phase:
            dq_out[s] = dq + jnp.where(core == 1, s1[s], 0.0)
            dk_out[s] = dk + jnp.where(core == 0, s1[s], 0.0)
            dv_out[s] = dv + jnp.where(core == 0, s2[s], 0.0)
        else:
            p1_out[s] = jnp.where(core == 0, dq, dk).astype(BF)
            p2_out[s] = dv.astype(BF)
            s1_out[s] = jnp.where(core == 0, dk, dq)
            s2_out[s] = dv
            beside_out[0, s] = (dka[HALF + s] * QK_SCALE).astype(BF)
            beside_out[1, s] = (dva[HALF + s] * V_SCALE).astype(BF)
        return 0

    lax.fori_loop(0, HALF, finish, 0)


def piped(ins, shapes, in_sems, outs, staged, out_sems, compute):
    def coming(d):
        rows = pl.ds(3 * d, 3)
        return [
            pltpu.make_async_copy(
                src.at[:, rows] if four else src.at[rows],
                dst.at[:, rows] if four else dst.at[rows],
                in_sems.at[d, n],
            )
            for n, (src, dst, four) in enumerate(zip(ins, shapes[0], shapes[1]))
        ]

    def going(d):
        return pltpu.make_async_copy(staged.at[d], outs[d], out_sems.at[d])

    for d in range(4):
        for copy in coming(d):
            copy.start()
    for d in range(4):
        for copy in coming(d):
            copy.wait()
        compute(d)
        going(d).start()
    for d in range(4):
        going(d).wait()


def dq_kernel(at, dq, across, o0, o1, o2, o3, dq_v, across_v, staged, in_sems, out_sems):
    first = at[2] == 0

    def compute(d):
        for m in range(3):
            s = 3 * d + m
            far = across_v[s].astype(F32)
            staged[d, m] = (dq_v[s] + jnp.where(first, far, 0.0)).astype(BF)

    piped(
        (dq, across), ((dq_v, across_v), (0, 0)), in_sems, (o0, o1, o2, o3), staged, out_sems, compute
    )


def dkv_kernel(at, *refs):
    ins, outs = refs[:5], refs[5:9]
    bufs, (staged, in_sems, out_sems) = refs[9:14], refs[14:]
    dk, dv, beside, a1, a2 = bufs
    first = at[2] == 0

    def compute(d):
        for m in range(3):
            s = 3 * d + m
            for n, (own, far) in enumerate(((dk, a1), (dv, a2))):
                near = beside[n, s].astype(F32)
                far = jnp.where(first, 0.0, far[s].astype(F32))
                staged[d, n, m] = (own[s] + near + far).astype(BF)

    piped(ins, (bufs, (0, 0, 1, 0, 0)), in_sems, outs, staged, out_sems, compute)


def join_kernel(arrays, at, *refs):
    outs, sems = refs[4 : 4 + arrays], refs[-1]
    made = []
    for d in range(4):
        lanes = pl.ds(pl.multiple_of(lax.rem(at[0] + d, 4) * HEAD, HEAD), HEAD)
        for n in range(arrays):
            made.append(
                pltpu.make_async_copy(
                    refs[d].at[n], outs[n].at[:, lanes], sems.at[d * arrays + n]
                )
            )
    for copy in made:
        copy.start()
    for copy in made:
        copy.wait()


def call(kernel, outs, ins, scratch=(), limit=56, where=ANY, cost=None, **kw):
    return pl.pallas_call(
        kernel,
        out_shape=outs,
        in_specs=ins,
        out_specs=[where] * len(outs),
        scratch_shapes=scratch,
        compiler_params=pltpu.CompilerParams(vmem_limit_bytes=limit * 2**20),
        cost_estimate=cost,
        **kw,
    )


def table(qs, ks, valid, counts, dummy):
    rows = BLK - counts
    cls = jnp.clip((rows + 31) // 32 - 5, 0, 3)
    value = (qs | (ks << 4) | (rows << 9) | (cls << 18)).reshape(-1)
    order = jnp.where(valid, cls, 4).reshape(-1)
    n = jnp.arange(ENTRIES, dtype=jnp.int32)
    before = (order[None, :] < order[:, None]) | (
        (order[None, :] == order[:, None]) & (n[None, :] < n[:, None])
    )
    rank = jnp.sum(before.astype(jnp.int32), 1)
    total = jnp.sum(valid.astype(jnp.int32))
    tab = jnp.sum(jnp.where(rank[None, :] == n[:, None], value[None, :], 0), 1)
    tab = jnp.where(n < total, tab, HALF | (dummy << 4))
    return tab, jnp.max((tab >> 18).reshape(-1, GROUP), 1), (total + GROUP - 1) // GROUP


def tables(key_blocks, target_counts, z, y, core):
    def slot(t):
        return lax.rem(y + 4 - (t % HALF) // 3, 4) * 3 + t % 3

    ids = jnp.arange(96, dtype=jnp.int32)
    own = lax.dynamic_slice(key_blocks, (PLANE * z + HALF * core, 0), (HALF, KPB))[:, 1:]
    after = lax.dynamic_slice(key_blocks, (jnp.minimum(PLANE * (z + 1), 84), 0), (HALF, KPB))[:, 1:]
    qs = jnp.broadcast_to(slot(jnp.arange(HALF, dtype=jnp.int32))[:, None], own.shape)
    made = []
    for phase in range(2):
        kid = own if phase else jnp.where(core == 0, after, own)
        plane = jnp.maximum(kid, 0) // PLANE
        t = jnp.maximum(kid, 0) - PLANE * plane
        same = (plane == z) & (t // HALF == core)
        if phase:
            valid, ks = (kid >= 0) & same, slot(t)
        else:
            valid = (kid >= 0) & jnp.where(core == 0, (z < 3) & (plane == z), ~same)
            other = (plane == z) & (t // HALF != core)
            ks = slot(t) + jnp.where(other, HALF, 0)
        counts = jnp.sum(jnp.where(kid[..., None] == ids, target_counts, 0), -1)
        made.append(table(qs, ks, valid, counts, DUMMY[phase]))
    s = jnp.arange(HALF, dtype=jnp.int32)
    block = PLANE * z + HALF * core + lax.rem(y + 4 - s // 3, 4) * 3 + s % 3
    nvd = BLK - jnp.sum(jnp.where(block[:, None] == ids, target_counts, 0), -1)
    return made, nvd


def pairs_cost(pairs):
    return pl.CostEstimate(
        flops=pairs * 10 * BLK * BLK * HEAD, bytes_accessed=12 * 2**20, transcendentals=pairs * BLK * BLK
    )


def body(queries, keys, values, out_grad, key_blocks, target_counts):
    ctx, tp = lax.axis_index("ctx"), lax.axis_index("tp")
    z, x, y, core = ctx // 8, (ctx // 4) % 2, ctx % 4, tp % 2
    here = jnp.stack([y, x]).astype(jnp.int32)
    rows = queries.shape[0]
    shape = jax.ShapeDtypeStruct
    dma = lambda *n: pltpu.SemaphoreType.DMA(n)

    def split(first_round):
        return call(
            functools.partial(split_kernel, first_round),
            [shape((2, rows, HEAD), BF)] * 4,
            [SMEM] + [ANY] * 4,
            [dma(8)],
            limit=56,
            name="split",
        )(here, queries, out_grad, keys, values)

    def send(pieces, pairs):
        return [lax.ppermute(p, AXES, pairs(d)) for d, p in enumerate(pieces)]

    two = shape((2, HALF, BLK, HEAD), BF)

    def gather(pieces):
        return call(gather_kernel, [two], [ANY] * 4, [dma(4)], limit=56, name="gather")(*pieces)[0]

    def blocks(pieces):
        return [p.reshape(2, 3, BLK, HEAD) for p in pieces]

    r1 = blocks(send(split(True), to_heads))
    r2 = blocks(send(split(False), to_heads))
    all1 = gather(r1)
    across = lax.ppermute(all1, AXES, ALONG_Z)
    to_first = lax.ppermute(all1, AXES, TO_FIRST)
    to_second = lax.ppermute(gather(r2), AXES, TO_SECOND)

    (far, own), nvd = tables(key_blocks, target_counts, z, y, core)
    at = jnp.stack([y, x, core, far[2], own[2]]).astype(jnp.int32)
    tab = jnp.concatenate([far[0], own[0]])
    cls = jnp.concatenate([far[1], own[1]])
    half, half16 = shape((HALF, BLK, HEAD), F32), shape((HALF, BLK, HEAD), BF)

    def scratch(k):
        return [
            pltpu.VMEM((HALF + 1, BLK, HEAD), BF),
            pltpu.VMEM((HALF + 1, BLK, HEAD), BF),
            pltpu.VMEM((k + 1, BLK, HEAD), BF),
            pltpu.VMEM((k + 1, BLK, HEAD), BF),
            pltpu.VMEM((HALF + 1, HEAD, BLK), F32),
            pltpu.VMEM((k + 1, BLK, HEAD), F32),
            pltpu.VMEM((k + 1, BLK, HEAD), F32),
        ]

    p1, p2, s1, s2, beside = call(
        functools.partial(pairs_kernel, 0),
        [half16, half16, half, half, two],
        [SMEM] * 4 + [ANY] * 11,
        scratch(PLANE) + [dma(22)],
        where=VMEM,
        cost=pairs_cost(139),
        name="far",
    )(at, tab, cls, nvd, *r1, *r2, across, to_first, to_second)
    p1 = lax.ppermute(p1, AXES, BACK_Z)
    p2 = lax.ppermute(p2, AXES, BACK_Z_SECOND)
    beside = lax.ppermute(beside, AXES, OTHER_CORE)
    dq, dk, dv = call(
        functools.partial(pairs_kernel, 1),
        [half, half, half],
        [SMEM] * 4 + [ANY] * 10,
        scratch(HALF) + [pltpu.VMEM((HALF, BLK, HEAD), F32)] * 2 + [dma(22)],
        where=VMEM,
        cost=pairs_cost(60),
        name="own",
    )(at, tab, cls, nvd, *r1, *r2, s1, s2)
    v3, v3h = pltpu.VMEM((HALF, BLK, HEAD), F32), pltpu.VMEM((HALF, BLK, HEAD), BF)
    v4 = pltpu.VMEM((2, HALF, BLK, HEAD), BF)
    dq_sent = call(
        dq_kernel,
        [shape((3, BLK, HEAD), BF)] * 4,
        [SMEM] + [ANY] * 2,
        [v3, v3h, pltpu.VMEM((4, 3, BLK, HEAD), BF), dma(4, 2), dma(4)],
        name="dq",
    )(at, dq, p1)
    dq_back = send([p.reshape(1, rows, HEAD) for p in dq_sent], from_heads)
    dkv_sent = call(
        dkv_kernel,
        [shape((2, 3, BLK, HEAD), BF)] * 4,
        [SMEM] + [ANY] * 5,
        [v3, v3, v4, v3h, v3h, pltpu.VMEM((4, 2, 3, BLK, HEAD), BF), dma(4, 5), dma(4)],
        name="dkv",
    )(at, dk, dv, beside, p1, p2)
    dkv_back = send([p.reshape(2, rows, HEAD) for p in dkv_sent], from_heads)
    out = shape(queries.shape, BF)

    def join(pieces, arrays):
        return call(
            functools.partial(join_kernel, arrays),
            [out] * arrays,
            [SMEM] + [ANY] * 4,
            [dma(4 * arrays)],
            limit=56,
            name="join",
        )(here, *pieces)

    return (*join(dq_back, 1), *join(dkv_back, 2))


def solution(mesh):
    in_specs = (P("ctx", "tp"),) * 4 + (P(), P())
    return jax.shard_map(
        body, mesh=mesh, in_specs=in_specs, out_specs=(P("ctx", "tp"),) * 3, check_vma=False
    )
```

time: 192 us -> 451 us (2.35)
  the two profiles are of different devices: /device:TPU:7 before, /device:TPU:0 now
where the time goes in v2:
time: 451 us; the launch traced here: 450 us
  Pallas kernels  339 us (75%)
  waiting for transfers between devices  55.4 us (12%)
  starting transfers between devices  35.6 us (8%)
  local copies, waits for them, and re-layouts  9.13 us (2%)
  other arithmetic  8.16 us (2%)
    pallas_call x2, Pallas kernels, split(): call(functools.partial(split_kernel, first_round), [shape((2, rows, HEAD)...  99 us
    pallas_call x2, Pallas kernels, gather(): call(gather_kernel, [two], [ANY] * 4, [dma(4)], limit=56, name='gather')  97.6 us
    pallas_call x2, Pallas kernels, join(): call(functools.partial(join_kernel, arrays), [out] * arrays, [SMEM] + [AN...  75.1 us
    ppermute x16, waiting for transfers between devices, send(): return [lax.ppermute(p, AXES, pairs(d)) for d, p in enumerate(pieces)]  55.4 us
    pallas_call x1, Pallas kernels, body(): call(functools.partial(pairs_kernel, 0), [half16, half16, half, half, two...  36.6 us
    pallas_call x1, Pallas kernels, body(): call(functools.partial(pairs_kernel, 1), [half, half, half], [SMEM] * 4 +...  22.3 us
    ppermute x16, starting transfers between devices, send(): return [lax.ppermute(p, AXES, pairs(d)) for d, p in enumerate(pieces)]  21.8 us
  transfers between devices with their start and end apart: 22, of which 3 were waited for; matrix products, arithmetic and copies ran while one was open for 2% of the time, Pallas kernels for 45%

profile of v2, /device:TPU:0, one launch (start us, length us, event | category | flops | bytes accessed | tf_op | source)
XLA Modules:
  0.0 449.6 jit_solution(7506810307331762481)
XLA Ops:
  1.3 49.5 %split.3 = (bf16[2,768,128]{2,1,0:T(8,128)(2,1)}, bf16[2,768,128]{2,1,0:T(8,128)(2,1)}, bf16[2,768,128]{2,1,0:T(8,128)(2,1)}, bf16[2,768,128]{2,1,0:T(8,128)(2,1)}) custom-call(s32[2]{0:T(128)} %pad_add_fusion.1.at, bf16[768,512]{1,0:T(8,128)(2,1)} %q.3, bf16[768,512]{1,0:T(8,128)(2,1)} %g.3, bf16[768,512]{1,0:T(8,128)(2,1)} %k.3, bf16[768,512]{1,0:T(8,128)(2,1)} %v.3), custom_call_target="tpu_custom_call" | custom-call | tf_op jit(solution)/shard_map/split/pallas_call | solution.py:392
  50.8 1.7 collective-permute-start.4
  52.5 1.7 collective-permute-start.5
  54.1 49.5 %split.2 = (bf16[2,768,128]{2,1,0:T(8,128)(2,1)}, bf16[2,768,128]{2,1,0:T(8,128)(2,1)}, bf16[2,768,128]{2,1,0:T(8,128)(2,1)}, bf16[2,768,128]{2,1,0:T(8,128)(2,1)}) custom-call(s32[2]{0:T(128)} %pad_add_fusion.1.at, bf16[768,512]{1,0:T(8,128)(2,1)} %q.3, bf16[768,512]{1,0:T(8,128)(2,1)} %g.3, bf16[768,512]{1,0:T(8,128)(2,1)} %k.3, bf16[768,512]{1,0:T(8,128)(2,1)} %v.3), custom_call_target="tpu_custom_call" | custom-call | tf_op jit(solution)/shard_map/split/pallas_call | solution.py:392
  103.6 1.7 collective-permute-start
  105.3 1.6 collective-permute-start.1
  109.3 2.1 collective-permute-start.6
  111.5 24.1 %collective-permute-done.1 = bf16[2,768,128]{2,1,0:T(8,128)(2,1)S(1)} collective-permute-done((bf16[2,768,128]{2,1,0:T(8,128)(2,1)}, bf16[2,768,128]{2,1,0:T(8,128)(2,1)S(1)}, u32[]{:S(2)}, u32[]{:S(2)}) %collective-permute-start.1) | collective-permute-done | bytes 393248 | tf_op jit(solution)/shard_map/ppermute | solution.py:402
  139.1 8.7 %collective-permute-done.3 = bf16[2,768,128]{2,1,0:T(8,128)(2,1)S(1)} collective-permute-done((bf16[2,768,128]{2,1,0:T(8,128)(2,1)}, bf16[2,768,128]{2,1,0:T(8,128)(2,1)S(1)}, u32[]{:S(2)}, u32[]{:S(2)}) %collective-permute-start.3) | collective-permute-done | bytes 393248 | tf_op jit(solution)/shard_map/ppermute | solution.py:402
  148.5 48.8 %gather.2 = bf16[2,12,256,128]{3,2,1,0:T(8,128)(2,1)} custom-call(bf16[2,3,256,128]{3,2,1,0:T(8,128)(2,1)} %bitcast.27, bf16[2,3,256,128]{3,2,1,0:T(8,128)(2,1)} %bitcast.30, bf16[2,3,256,128]{3,2,1,0:T(8,128)(2,1)} %bitcast.33, bf16[2,3,256,128]{3,2,1,0:T(8,128)(2,1)} %bitcast.42), custom_call_target="tpu_custom_call" | custom-call | tf_op jit(solution)/shard_map/gather/pallas_call | solution.py:407
  201.0 48.8 %gather.3 = bf16[2,12,256,128]{3,2,1,0:T(8,128)(2,1)} custom-call(bf16[2,3,256,128]{3,2,1,0:T(8,128)(2,1)} %bitcast.21, bf16[2,3,256,128]{3,2,1,0:T(8,128)(2,1)} %bitcast.24, bf16[2,3,256,128]{3,2,1,0:T(8,128)(2,1)} %bitcast.36, bf16[2,3,256,128]{3,2,1,0:T(8,128)(2,1)} %bitcast.39), custom_call_target="tpu_custom_call" | custom-call | tf_op jit(solution)/shard_map/gather/pallas_call | solution.py:407
  249.7 7.6 %collective-permute-start.10 = (bf16[2,12,256,128]{3,2,1,0:T(8,128)(2,1)}, bf16[2,12,256,128]{3,2,1,0:T(8,128)(2,1)S(1)}, u32[]{:S(2)}, u32[]{:S(2)}) collective-permute-start(bf16[2,12,256,128]{3,2,1,0:T(8,128)(2,1)} %gather.3), channel_id=1, source_target_pairs={{0,1},{2,3},{4,5},{6,7},{8,9},{10,11},{12,13},{14,15},{16,17},{18,... | collective-permute-start | bytes 4718600 | tf_op jit(solution)/shard_map/ppermute | solution.py:417
  264.7 36.6 %far.1 = (bf16[12,256,128]{2,1,0:T(8,128)(2,1)}, bf16[12,256,128]{2,1,0:T(8,128)(2,1)}, f32[12,256,128]{2,1,0:T(8,128)}, f32[12,256,128]{2,1,0:T(8,128)}, bf16[2,12,256,128]{3,2,1,0:T(8,128)(2,1)}) custom-call(s32[5]{0:T(128)} %stack.29.at, s32[360]{0:T(512)} %pad_add_fusion.tab, s32[60]{0:T(128)} %pad_add_fusion.2.cls, s32[12]{0:T(128)} %broadcast_subtract_fusion.nvd, ...), custom_call_target="tpu_custom_call" | custom-call | flops 11660165120 | bytes 12582912 | tf_op jit(solution)/shard_map/far/pallas_call | solution.py:436
  301.4 2.8 collective-permute-start.11
  304.9 22.3 %own.1 = (f32[12,256,128]{2,1,0:T(8,128)}, f32[12,256,128]{2,1,0:T(8,128)}, f32[12,256,128]{2,1,0:T(8,128)}) custom-call(s32[5]{0:T(128)} %stack.29.at, s32[360]{0:T(512)} %pad_add_fusion.tab, s32[60]{0:T(128)} %pad_add_fusion.2.cls, s32[12]{0:T(128)} %broadcast_subtract_fusion.nvd, bf16[2,3,256,128]{3,2,1,0:T(8,128)(2,1)} %bitcast.29, ...), custom_call_target="tpu_custom_call" | custom-call | flops 5033164800 | bytes 12582912 | tf_op jit(solution)/shard_map/own/pallas_call | solution.py:448
  328.2 3.1 dq.1
  332.6 1.6 collective-permute-start.12
  336.1 4.9 %dkv.1 = (bf16[2,3,256,128]{3,2,1,0:T(8,128)(2,1)}, bf16[2,3,256,128]{3,2,1,0:T(8,128)(2,1)}, bf16[2,3,256,128]{3,2,1,0:T(8,128)(2,1)}, bf16[2,3,256,128]{3,2,1,0:T(8,128)(2,1)}) custom-call(s32[5]{0:T(128)} %stack.29.at, f32[12,256,128]{2,1,0:T(8,128)} %get-tuple-element.45.refs_0_, f32[12,256,128]{2,1,0:T(8,128)} %get-tuple-element.46.refs_1_, ...), custom_call_target="tpu_custom_call" | custom-call | tf_op jit(solution)/shard_map/dkv/pallas_call | solution.py:467
  341.0 3.1 collective-permute-start.19
  344.1 1.6 collective-permute-start.18
  347.2 2.1 collective-permute-start.15
  349.3 22.6 %collective-permute-done.15.refs_3_ = bf16[1,768,128]{2,1,0:T(8,128)(2,1)S(1)} collective-permute-done((bf16[1,768,128]{2,1,0:T(8,128)(2,1)S(1)}, bf16[1,768,128]{2,1,0:T(8,128)(2,1)S(1)}, u32[]{:S(2)}, u32[]{:S(2)}) %collective-permute-start.15) | collective-permute-done | bytes 196640 | tf_op jit(solution)/shard_map/ppermute | solution.py:402
  372.5 25.6 %join.2 = bf16[768,512]{1,0:T(8,128)(2,1)} custom-call(s32[2]{0:T(128)} %pad_add_fusion.1.at, bf16[1,768,128]{2,1,0:T(8,128)(2,1)} %copy-done.16, bf16[1,768,128]{2,1,0:T(8,128)(2,1)} %copy-done.15, bf16[1,768,128]{2,1,0:T(8,128)(2,1)} %copy-done.17, bf16[1,768,128]{2,1,0:T(8,128)(2,1)} %copy-done.18), custom_call_target="tpu_custom_call" | custom-call | tf_op jit(solution)/shard_map/join/pallas_call | solution.py:478
  400.0 49.5 %join.3 = (bf16[768,512]{1,0:T(8,128)(2,1)}, bf16[768,512]{1,0:T(8,128)(2,1)}) custom-call(s32[2]{0:T(128)} %pad_add_fusion.1.at, bf16[2,768,128]{2,1,0:T(8,128)(2,1)} %copy-done.12, bf16[2,768,128]{2,1,0:T(8,128)(2,1)} %copy-done.11, bf16[2,768,128]{2,1,0:T(8,128)(2,1)} %copy-done.13, bf16[2,768,128]{2,1,0:T(8,128)(2,1)} %copy-done.14), custom_call_target="tpu_custom_call" | custom-call | tf_op jit(solution)/shard_map/join/pallas_call | solution.py:478
  (106 shorter events, 25.5 us)
Async XLA Ops:
  50.8 147.8 %collective-permute-start.4 = (bf16[2,768,128]{2,1,0:T(8,128)(2,1)}, bf16[2,768,128]{2,1,0:T(8,128)(2,1)S(1)}, u32[]{:S(2)}, u32[]{:S(2)}) collective-permute-start(bf16[2,768,128]{2,1,0:T(8,128)(2,1)} %get-tuple-element.33), channel_id=1, source_target_pairs={{0,0},{1,16},{2,2},{3,18},{4,4},{5,20},{6,6},{7,22},{8,8},{9,24},{... | collective-permute-start | bytes 1179656 | tf_op jit(solution)/shard_map/ppermute | solution.py:402
  52.5 55.9 %copy-start.19 = (s32[96,16]{0,1:T(8,128)S(1)}, s32[96,16]{0,1:T(8,128)}, u32[]{:S(2)}) copy-start(s32[96,16]{0,1:T(8,128)} %param.10) | copy-start | bytes 18436
  52.5 56.2 %copy-start.20 = (s32[96]{0:T(128)S(1)}, s32[96]{0:T(128)}, u32[]{:S(2)}) copy-start(s32[96]{0:T(128)} %param.11) | copy-start | bytes 1156
  52.5 147.5 %collective-permute-start.5 = (bf16[2,768,128]{2,1,0:T(8,128)(2,1)}, bf16[2,768,128]{2,1,0:T(8,128)(2,1)S(1)}, u32[]{:S(2)}, u32[]{:S(2)}) collective-permute-start(bf16[2,768,128]{2,1,0:T(8,128)(2,1)} %get-tuple-element.34), channel_id=1, source_target_pairs={{0,4},{1,20},{2,6},{3,22},{4,8},{5,24},{6,10},{7,26},{8,12},{9,28}... | collective-permute-start | bytes 1179656 | tf_op jit(solution)/shard_map/ppermute | solution.py:402
  103.6 5.7 %collective-permute-start = (bf16[2,768,128]{2,1,0:T(8,128)(2,1)}, bf16[2,768,128]{2,1,0:T(8,128)(2,1)S(1)}, u32[]{:S(2)}, u32[]{:S(2)}) collective-permute-start(bf16[2,768,128]{2,1,0:T(8,128)(2,1)} %get-tuple-element.29), channel_id=1, source_target_pairs={{0,0},{1,16},{2,2},{3,18},{4,4},{5,20},{6,6},{7,22},{8,8},{9,24},{... | collective-permute-start | bytes 1179656 | tf_op jit(solution)/shard_map/ppermute | solution.py:402
  105.3 30.3 %collective-permute-start.1 = (bf16[2,768,128]{2,1,0:T(8,128)(2,1)}, bf16[2,768,128]{2,1,0:T(8,128)(2,1)S(1)}, u32[]{:S(2)}, u32[]{:S(2)}) collective-permute-start(bf16[2,768,128]{2,1,0:T(8,128)(2,1)} %get-tuple-element.30), channel_id=1, source_target_pairs={{0,4},{1,20},{2,6},{3,22},{4,8},{5,24},{6,10},{7,26},{8,12},{9,28}... | collective-permute-start | bytes 1179656 | tf_op jit(solution)/shard_map/ppermute | solution.py:402
  106.9 28.7 %collective-permute-start.2 = (bf16[2,768,128]{2,1,0:T(8,128)(2,1)}, bf16[2,768,128]{2,1,0:T(8,128)(2,1)S(1)}, u32[]{:S(2)}, u32[]{:S(2)}) collective-permute-start(bf16[2,768,128]{2,1,0:T(8,128)(2,1)} %get-tuple-element.31), channel_id=1, source_target_pairs={{0,8},{1,24},{2,10},{3,26},{4,12},{5,28},{6,14},{7,30},{8,0},{9,16... | collective-permute-start | bytes 1179656 | tf_op jit(solution)/shard_map/ppermute | solution.py:402
  109.3 90.6 %collective-permute-start.6 = (bf16[2,768,128]{2,1,0:T(8,128)(2,1)}, bf16[2,768,128]{2,1,0:T(8,128)(2,1)S(1)}, u32[]{:S(2)}, u32[]{:S(2)}) collective-permute-start(bf16[2,768,128]{2,1,0:T(8,128)(2,1)} %get-tuple-element.35), channel_id=1, source_target_pairs={{0,8},{1,24},{2,10},{3,26},{4,12},{5,28},{6,14},{7,30},{8,0},{9,16... | collective-permute-start | bytes 1179656 | tf_op jit(solution)/shard_map/ppermute | solution.py:402
  135.5 64.4 %collective-permute-start.7 = (bf16[2,768,128]{2,1,0:T(8,128)(2,1)}, bf16[2,768,128]{2,1,0:T(8,128)(2,1)S(1)}, u32[]{:S(2)}, u32[]{:S(2)}) collective-permute-start(bf16[2,768,128]{2,1,0:T(8,128)(2,1)} %get-tuple-element.36), channel_id=1, source_target_pairs={{0,12},{1,28},{2,14},{3,30},{4,0},{5,16},{6,2},{7,18},{8,4},{9,20}... | collective-permute-start | bytes 1179656 | tf_op jit(solution)/shard_map/ppermute | solution.py:402
  135.6 12.2 %collective-permute-start.3 = (bf16[2,768,128]{2,1,0:T(8,128)(2,1)}, bf16[2,768,128]{2,1,0:T(8,128)(2,1)S(1)}, u32[]{:S(2)}, u32[]{:S(2)}) collective-permute-start(bf16[2,768,128]{2,1,0:T(8,128)(2,1)} %get-tuple-element.32), channel_id=1, source_target_pairs={{0,12},{1,28},{2,14},{3,30},{4,0},{5,16},{6,2},{7,18},{8,4},{9,20}... | collective-permute-start | bytes 1179656 | tf_op jit(solution)/shard_map/ppermute | solution.py:402
  197.3 66.1 %collective-permute-start.9 = (bf16[2,12,256,128]{3,2,1,0:T(8,128)(2,1)}, bf16[2,12,256,128]{3,2,1,0:T(8,128)(2,1)}, u32[]{:S(2)}, u32[]{:S(2)}) collective-permute-start(bf16[2,12,256,128]{3,2,1,0:T(8,128)(2,1)} %gather.2), channel_id=1, source_target_pairs={{1,0},{3,2},{5,4},{7,6},{9,8},{11,10},{13,12},{15,14},{17,16},{19,... | collective-permute-start | bytes 4718600 | tf_op jit(solution)/shard_map/ppermute | solution.py:416
  198.6 64.8 %collective-permute-start.8 = (bf16[2,12,256,128]{3,2,1,0:T(8,128)(2,1)}, bf16[2,12,256,128]{3,2,1,0:T(8,128)(2,1)}, u32[]{:S(2)}, u32[]{:S(2)}) collective-permute-start(bf16[2,12,256,128]{3,2,1,0:T(8,128)(2,1)} %gather.2), channel_id=1, source_target_pairs={{1,33},{3,35},{5,37},{7,39},{9,41},{11,43},{13,45},{15,47},{17,49}... | collective-permute-start | bytes 4718600 | tf_op jit(solution)/shard_map/ppermute | solution.py:415
  249.7 13.7 %collective-permute-start.10 = (bf16[2,12,256,128]{3,2,1,0:T(8,128)(2,1)}, bf16[2,12,256,128]{3,2,1,0:T(8,128)(2,1)S(1)}, u32[]{:S(2)}, u32[]{:S(2)}) collective-permute-start(bf16[2,12,256,128]{3,2,1,0:T(8,128)(2,1)} %gather.3), channel_id=1, source_target_pairs={{0,1},{2,3},{4,5},{6,7},{8,9},{10,11},{12,13},{14,15},{16,17},{18,... | collective-permute-start | bytes 4718600 | tf_op jit(solution)/shard_map/ppermute | solution.py:417
  301.4 33.3 %collective-permute-start.16 = (bf16[2,12,256,128]{3,2,1,0:T(8,128)(2,1)}, bf16[2,12,256,128]{3,2,1,0:T(8,128)(2,1)S(1)}, u32[]{:S(2)}, u32[]{:S(2)}) collective-permute-start(bf16[2,12,256,128]{3,2,1,0:T(8,128)(2,1)} %get-tuple-element.47), channel_id=1, source_target_pairs={{0,1},{1,0},{2,3},{3,2},{4,5},{5,4},{6,7},{7,6},{8,9},{9,8},{10,11... | collective-permute-start | bytes 4718600 | tf_op jit(solution)/shard_map/ppermute | solution.py:447
  301.4 25.8 %collective-permute-start.11 = (bf16[12,256,128]{2,1,0:T(8,128)(2,1)}, bf16[12,256,128]{2,1,0:T(8,128)(2,1)S(1)}, u32[]{:S(2)}, u32[]{:S(2)}) collective-permute-start(bf16[12,256,128]{2,1,0:T(8,128)(2,1)} %get-tuple-element.40), channel_id=1, source_target_pairs={{33,1},{35,3},{37,5},{39,7},{41,9},{43,11},{45,13},{47,15},{49,17}... | collective-permute-start | bytes 2359304 | tf_op jit(solution)/shard_map/ppermute | solution.py:445
  304.2 30.4 %collective-permute-start.17 = (bf16[12,256,128]{2,1,0:T(8,128)(2,1)}, bf16[12,256,128]{2,1,0:T(8,128)(2,1)S(1)}, u32[]{:S(2)}, u32[]{:S(2)}) collective-permute-start(bf16[12,256,128]{2,1,0:T(8,128)(2,1)} %get-tuple-element.48), channel_id=1, source_target_pairs={{33,1},{35,3},{37,5},{39,7},{41,9},{43,11},{45,13},{47,15},{49,17}... | collective-permute-start | bytes 2359304 | tf_op jit(solution)/shard_map/ppermute | solution.py:446
  331.3 14.4 %collective-permute-start.13 = (bf16[1,768,128]{2,1,0:T(8,128)(2,1)}, bf16[1,768,128]{2,1,0:T(8,128)(2,1)S(1)}, u32[]{:S(2)}, u32[]{:S(2)}) collective-permute-start(bf16[1,768,128]{2,1,0:T(8,128)(2,1)} %bitcast.52), channel_id=1, source_target_pairs={{4,0},{20,1},{6,2},{22,3},{8,4},{24,5},{10,6},{26,7},{12,8},{28,9}... | collective-permute-start | bytes 589832 | tf_op jit(solution)/shard_map/ppermute | solution.py:402
  332.6 13.2 %collective-permute-start.12 = (bf16[1,768,128]{2,1,0:T(8,128)(2,1)}, bf16[1,768,128]{2,1,0:T(8,128)(2,1)S(1)}, u32[]{:S(2)}, u32[]{:S(2)}) collective-permute-start(bf16[1,768,128]{2,1,0:T(8,128)(2,1)} %bitcast.51), channel_id=1, source_target_pairs={{0,0},{16,1},{2,2},{18,3},{4,4},{20,5},{6,6},{22,7},{8,8},{24,9},{... | collective-permute-start | bytes 589832 | tf_op jit(solution)/shard_map/ppermute | solution.py:402
  334.1 13.0 %collective-permute-start.14 = (bf16[1,768,128]{2,1,0:T(8,128)(2,1)}, bf16[1,768,128]{2,1,0:T(8,128)(2,1)S(1)}, u32[]{:S(2)}, u32[]{:S(2)}) collective-permute-start(bf16[1,768,128]{2,1,0:T(8,128)(2,1)} %bitcast.50), channel_id=1, source_target_pairs={{8,0},{24,1},{10,2},{26,3},{12,4},{28,5},{14,6},{30,7},{0,8},{16,9... | collective-permute-start | bytes 589832 | tf_op jit(solution)/shard_map/ppermute | solution.py:402
  341.0 57.2 %collective-permute-start.19 = (bf16[2,768,128]{2,1,0:T(8,128)(2,1)}, bf16[2,768,128]{2,1,0:T(8,128)(2,1)S(1)}, u32[]{:S(2)}, u32[]{:S(2)}) collective-permute-start(bf16[2,768,128]{2,1,0:T(8,128)(2,1)} %bitcast.48), channel_id=1, source_target_pairs={{4,0},{20,1},{6,2},{22,3},{8,4},{24,5},{10,6},{26,7},{12,8},{28,9}... | collective-permute-start | bytes 1179656 | tf_op jit(solution)/shard_map/ppermute | solution.py:402
  344.1 54.1 %collective-permute-start.18 = (bf16[2,768,128]{2,1,0:T(8,128)(2,1)}, bf16[2,768,128]{2,1,0:T(8,128)(2,1)S(1)}, u32[]{:S(2)}, u32[]{:S(2)}) collective-permute-start(bf16[2,768,128]{2,1,0:T(8,128)(2,1)} %bitcast.47), channel_id=1, source_target_pairs={{0,0},{16,1},{2,2},{18,3},{4,4},{20,5},{6,6},{22,7},{8,8},{24,9},{... | collective-permute-start | bytes 1179656 | tf_op jit(solution)/shard_map/ppermute | solution.py:402
  345.7 52.5 %collective-permute-start.20 = (bf16[2,768,128]{2,1,0:T(8,128)(2,1)}, bf16[2,768,128]{2,1,0:T(8,128)(2,1)S(1)}, u32[]{:S(2)}, u32[]{:S(2)}) collective-permute-start(bf16[2,768,128]{2,1,0:T(8,128)(2,1)} %bitcast.46), channel_id=1, source_target_pairs={{8,0},{24,1},{10,2},{26,3},{12,4},{28,5},{14,6},{30,7},{0,8},{16,9... | collective-permute-start | bytes 1179656 | tf_op jit(solution)/shard_map/ppermute | solution.py:402
  345.8 52.5 %collective-permute-start.21 = (bf16[2,768,128]{2,1,0:T(8,128)(2,1)}, bf16[2,768,128]{2,1,0:T(8,128)(2,1)S(1)}, u32[]{:S(2)}, u32[]{:S(2)}) collective-permute-start(bf16[2,768,128]{2,1,0:T(8,128)(2,1)} %bitcast.45), channel_id=1, source_target_pairs={{12,0},{28,1},{14,2},{30,3},{0,4},{16,5},{2,6},{18,7},{4,8},{20,9}... | collective-permute-start | bytes 1179656 | tf_op jit(solution)/shard_map/ppermute | solution.py:402
  347.2 24.7 %collective-permute-start.15 = (bf16[1,768,128]{2,1,0:T(8,128)(2,1)S(1)}, bf16[1,768,128]{2,1,0:T(8,128)(2,1)S(1)}, u32[]{:S(2)}, u32[]{:S(2)}) collective-permute-start(bf16[1,768,128]{2,1,0:T(8,128)(2,1)S(1)} %bitcast.49), channel_id=1, source_target_pairs={{12,0},{28,1},{14,2},{30,3},{0,4},{16,5},{2,6},{18,7},{4,8},{20,9}... | collective-permute-start | bytes 589832 | tf_op jit(solution)/shard_map/ppermute | solution.py:402
  (21 other events, 164.0 us)

commit v3 on v2

--- a/solution.py
+++ b/solution.py
@@ -71,42 +71,39 @@
     return lax.dot_general(a, b, (((0,), (0,)), ((), ())), preferred_element_type=F32)
 
 
+def relay(moves, stage, sems):
+    ins = [
+        pltpu.make_async_copy(src, stage.at[n], sems.at[0, n]) for n, (src, _) in enumerate(moves)
+    ]
+    outs = [
+        pltpu.make_async_copy(stage.at[n], dst, sems.at[1, n]) for n, (_, dst) in enumerate(moves)
+    ]
+    for copy in ins:
+        copy.start()
+    for n, copy in enumerate(ins):
+        copy.wait()
+        outs[n].start()
+    for copy in outs:
+        copy.wait()
+
+
 def split_kernel(first_round, at, q, g, k, v, *refs):
-    outs, sems = refs[:4], refs[4]
+    outs, (stage, sems) = refs[-6:-2], refs[-2:]
     y, x = at[0], at[1]
-
-    def copies(pair):
-        made = []
-        for d in range(4):
-            lanes = pl.ds(pl.multiple_of(lax.rem(y + d, 4) * HEAD, HEAD), HEAD)
-            for n in range(2):
-                made.append(
-                    pltpu.make_async_copy(
-                        pair[n].at[:, lanes], outs[d].at[n], sems.at[2 * d + n]
-                    )
-                )
-        return made
-
     for side, pair in ((0, (q, g)), (1, (k, v))):
 
         @pl.when(x == (side if first_round else 1 - side))
         def _(pair=pair):
-            made = copies(pair)
-            for copy in made:
-                copy.start()
-            for copy in made:
-                copy.wait()
+            moves = []
+            for d in range(4):
+                lanes = pl.ds(pl.multiple_of(lax.rem(y + d, 4) * HEAD, HEAD), HEAD)
+                moves += [(pair[n].at[:, lanes], outs[d].at[n]) for n in range(2)]
+            relay(moves, stage, sems)
 
 
 def gather_kernel(*refs):
-    ins, out, sems = refs[:4], refs[4], refs[5]
-    made = [
-        pltpu.make_async_copy(ins[d], out.at[:, pl.ds(3 * d, 3)], sems.at[d]) for d in range(4)
-    ]
-    for copy in made:
-        copy.start()
-    for copy in made:
-        copy.wait()
+    ins, out, stage, sems = refs[:4], *refs[4:]
+    relay([(ins[d], out.at[:, pl.ds(3 * d, 3)]) for d in range(4)], stage, sems)
 
 
 def pair_grads(scores, weight_grad, allowed):
@@ -301,20 +298,12 @@
 
 
 def join_kernel(arrays, at, *refs):
-    outs, sems = refs[4 : 4 + arrays], refs[-1]
-    made = []
+    outs, (stage, sems) = refs[4 : 4 + arrays], refs[-2:]
+    moves = []
     for d in range(4):
         lanes = pl.ds(pl.multiple_of(lax.rem(at[0] + d, 4) * HEAD, HEAD), HEAD)
-        for n in range(arrays):
-            made.append(
-                pltpu.make_async_copy(
-                    refs[d].at[n], outs[n].at[:, lanes], sems.at[d * arrays + n]
-                )
-            )
-    for copy in made:
-        copy.start()
-    for copy in made:
-        copy.wait()
+        moves += [(refs[d].at[n], outs[n].at[:, lanes]) for n in range(arrays)]
+    relay(moves, stage, sems)
 
 
 def call(kernel, outs, ins, scratch=(), limit=56, where=ANY, cost=None, **kw):
@@ -388,29 +377,33 @@
     shape = jax.ShapeDtypeStruct
     dma = lambda *n: pltpu.SemaphoreType.DMA(n)
 
-    def split(first_round):
+    def split(first_round, *behind):
         return call(
             functools.partial(split_kernel, first_round),
             [shape((2, rows, HEAD), BF)] * 4,
-            [SMEM] + [ANY] * 4,
-            [dma(8)],
+            [SMEM] + [ANY] * (4 + len(behind)),
+            [pltpu.VMEM((8, rows, HEAD), BF), dma(2, 8)],
             limit=56,
             name="split",
-        )(here, queries, out_grad, keys, values)
+        )(here, queries, out_grad, keys, values, *behind)
 
     def send(pieces, pairs):
         return [lax.ppermute(p, AXES, pairs(d)) for d, p in enumerate(pieces)]
 
     two = shape((2, HALF, BLK, HEAD), BF)
 
+    stage = pltpu.VMEM((4, 2, 3, BLK, HEAD), BF)
+
     def gather(pieces):
-        return call(gather_kernel, [two], [ANY] * 4, [dma(4)], limit=56, name="gather")(*pieces)[0]
+        return call(gather_kernel, [two], [ANY] * 4, [stage, dma(2, 4)], limit=56, name="gather")(*pieces)[0]
 
     def blocks(pieces):
         return [p.reshape(2, 3, BLK, HEAD) for p in pieces]
 
-    r1 = blocks(send(split(True), to_heads))
-    r2 = blocks(send(split(False), to_heads))
+    sent1 = split(True)
+    sent2 = split(False, sent1[0])
+    r1 = blocks(send(sent1, to_heads))
+    r2 = blocks(send(sent2, to_heads))
     all1 = gather(r1)
     across = lax.ppermute(all1, AXES, ALONG_Z)
     to_first = lax.ppermute(all1, AXES, TO_FIRST)
@@ -479,7 +472,7 @@
             functools.partial(join_kernel, arrays),
             [out] * arrays,
             [SMEM] + [ANY] * 4,
-            [dma(4 * arrays)],
+            [pltpu.VMEM((4 * arrays, rows, HEAD), BF), dma(2, 4 * arrays)],
             limit=56,
             name="join",
         )(here, *pieces)

time: 451 us -> 181 us (0.40)
  Pallas kernels: 339 us -> 83.5 us
  waiting for transfers between devices: 55.4 us -> 42.7 us
    pallas_call x2, Pallas kernels: 97.6 us -> 4.5 us  [gather(): call(gather_kernel, [two], [ANY] * 4, [stage, dma(2, 4)], limit=56, name=...]
    pallas_call x2, Pallas kernels: 99 us -> 6.04 us  [split(): call(functools.partial(split_kernel, first_round), [shape((2, rows, HEAD)...]
    pallas_call x2, Pallas kernels: 75.1 us -> 5.58 us  [join(): call(functools.partial(join_kernel, arrays), [out] * arrays, [SMEM] + [AN...]
    ppermute x16, waiting for transfers between devices: 55.4 us -> 38.9 us  [send(): return [lax.ppermute(p, AXES, pairs(d)) for d, p in enumerate(pieces)]]
    ppermute x1, starting transfers between devices: 7.65 us -> 1.39 us  [body(): to_second = lax.ppermute(gather(r2), AXES, TO_SECOND)]
  transfers between devices with their start and end apart: 22 -> 22, of which waited for: 3 -> 5; matrix products, arithmetic and copies ran while one was open for 2% -> 5% of each run, Pallas kernels for 45% -> 23%
where the time goes in v3:
time: 181 us; the launch traced here: 178 us
  Pallas kernels  83.5 us (46%)
  waiting for transfers between devices  42.7 us (24%)
  starting transfers between devices  33.2 us (18%)
  other arithmetic  8.13 us (4%)
  local copies, waits for them, and re-layouts  7.76 us (4%)
  between operations  2.61 us (1%)
    ppermute x16, waiting for transfers between devices, send(): return [lax.ppermute(p, AXES, pairs(d)) for d, p in enumerate(pieces)]  38.9 us
    pallas_call x1, Pallas kernels, body(): call(functools.partial(pairs_kernel, 0), [half16, half16, half, half, two...  36.3 us
    ppermute x16, starting transfers between devices, send(): return [lax.ppermute(p, AXES, pairs(d)) for d, p in enumerate(pieces)]  24.8 us
    pallas_call x1, Pallas kernels, body(): call(functools.partial(pairs_kernel, 1), [half, half, half], [SMEM] * 4 +...  23.1 us
    unnamed x48, local copies, waits for them, and re-layouts  6.49 us
    pallas_call x2, Pallas kernels, split(): call(functools.partial(split_kernel, first_round), [shape((2, rows, HEAD)...  6.04 us
    pallas_call x2, Pallas kernels, join(): call(functools.partial(join_kernel, arrays), [out] * arrays, [SMEM] + [AN...  5.58 us
    pallas_call x1, Pallas kernels, body(): call(dkv_kernel, [shape((2, 3, BLK, HEAD), BF)] * 4, [SMEM] + [ANY] * 5,...  4.91 us
  transfers between devices with their start and end apart: 22, of which 5 were waited for; matrix products, arithmetic and copies ran while one was open for 5% of the time, Pallas kernels for 23%

profile of v3, /device:TPU:0, one launch (start us, length us, event | category | flops | bytes accessed | tf_op | source)
XLA Modules:
  0.0 177.9 jit_solution(972440478390314834)
XLA Ops:
  1.3 3.0 %split.2 = (bf16[2,768,128]{2,1,0:T(8,128)(2,1)}, bf16[2,768,128]{2,1,0:T(8,128)(2,1)}, bf16[2,768,128]{2,1,0:T(8,128)(2,1)}, bf16[2,768,128]{2,1,0:T(8,128)(2,1)}) custom-call(s32[2]{0:T(128)} %pad_add_fusion.1.at, bf16[768,512]{1,0:T(8,128)(2,1)} %q.3, bf16[768,512]{1,0:T(8,128)(2,1)} %g.3, bf16[768,512]{1,0:T(8,128)(2,1)} %k.3, bf16[768,512]{1,0:T(8,128)(2,1)} %v.3), custom_call_target="tpu_custom_call" | custom-call | tf_op jit(solution)/shard_map/split/pallas_call | solution.py:381
  4.3 1.7 collective-permute-start.1
  6.0 2.9 %collective-permute-start.2 = (bf16[2,768,128]{2,1,0:T(8,128)(2,1)}, bf16[2,768,128]{2,1,0:T(8,128)(2,1)S(1)}, u32[]{:S(2)}, u32[]{:S(2)}) collective-permute-start(bf16[2,768,128]{2,1,0:T(8,128)(2,1)} %get-tuple-element.31), channel_id=1, source_target_pairs={{0,8},{1,24},{2,10},{3,26},{4,12},{5,28},{6,14},{7,30},{8,0},{9,16... | collective-permute-start | bytes 1179656 | tf_op jit(solution)/shard_map/ppermute | solution.py:391
  10.3 1.8 collective-permute-start
  12.0 3.1 %split.3 = (bf16[2,768,128]{2,1,0:T(8,128)(2,1)}, bf16[2,768,128]{2,1,0:T(8,128)(2,1)}, bf16[2,768,128]{2,1,0:T(8,128)(2,1)}, bf16[2,768,128]{2,1,0:T(8,128)(2,1)}) custom-call(s32[2]{0:T(128)} %pad_add_fusion.1.at, bf16[768,512]{1,0:T(8,128)(2,1)} %q.3, bf16[768,512]{1,0:T(8,128)(2,1)} %g.3, bf16[768,512]{1,0:T(8,128)(2,1)} %k.3, bf16[768,512]{1,0:T(8,128)(2,1)} %v.3, ...), custom_call_target="tpu_custom_call" | custom-call | tf_op jit(solution)/shard_map/split/pallas_call | solution.py:381
  15.1 1.7 collective-permute-start.4
  17.7 4.2 %collective-permute-done.1 = bf16[2,768,128]{2,1,0:T(8,128)(2,1)S(1)} collective-permute-done((bf16[2,768,128]{2,1,0:T(8,128)(2,1)}, bf16[2,768,128]{2,1,0:T(8,128)(2,1)S(1)}, u32[]{:S(2)}, u32[]{:S(2)}) %collective-permute-start.1) | collective-permute-done | bytes 393248 | tf_op jit(solution)/shard_map/ppermute | solution.py:391
  22.4 5.1 %collective-permute-done.2 = bf16[2,768,128]{2,1,0:T(8,128)(2,1)S(1)} collective-permute-done((bf16[2,768,128]{2,1,0:T(8,128)(2,1)}, bf16[2,768,128]{2,1,0:T(8,128)(2,1)S(1)}, u32[]{:S(2)}, u32[]{:S(2)}) %collective-permute-start.2) | collective-permute-done | bytes 393248 | tf_op jit(solution)/shard_map/ppermute | solution.py:391
  28.4 2.5 %collective-permute-start.7 = (bf16[2,768,128]{2,1,0:T(8,128)(2,1)}, bf16[2,768,128]{2,1,0:T(8,128)(2,1)S(1)}, u32[]{:S(2)}, u32[]{:S(2)}) collective-permute-start(bf16[2,768,128]{2,1,0:T(8,128)(2,1)} %get-tuple-element.36), channel_id=1, source_target_pairs={{0,12},{1,28},{2,14},{3,30},{4,0},{5,16},{6,2},{7,18},{8,4},{9,20}... | collective-permute-start | bytes 1179656 | tf_op jit(solution)/shard_map/ppermute | solution.py:391
  35.1 2.2 %gather.2 = bf16[2,12,256,128]{3,2,1,0:T(8,128)(2,1)} custom-call(bf16[2,3,256,128]{3,2,1,0:T(8,128)(2,1)} %bitcast.30, bf16[2,3,256,128]{3,2,1,0:T(8,128)(2,1)} %bitcast.21, bf16[2,3,256,128]{3,2,1,0:T(8,128)(2,1)} %bitcast.24, bf16[2,3,256,128]{3,2,1,0:T(8,128)(2,1)} %bitcast.27), custom_call_target="tpu_custom_call" | custom-call | tf_op jit(solution)/shard_map/gather/pallas_call | solution.py:398
  39.9 6.9 %collective-permute-done.6 = bf16[2,768,128]{2,1,0:T(8,128)(2,1)S(1)} collective-permute-done((bf16[2,768,128]{2,1,0:T(8,128)(2,1)}, bf16[2,768,128]{2,1,0:T(8,128)(2,1)S(1)}, u32[]{:S(2)}, u32[]{:S(2)}) %collective-permute-start.6) | collective-permute-done | bytes 393248 | tf_op jit(solution)/shard_map/ppermute | solution.py:391
  47.8 2.3 %gather.3 = bf16[2,12,256,128]{3,2,1,0:T(8,128)(2,1)} custom-call(bf16[2,3,256,128]{3,2,1,0:T(8,128)(2,1)} %bitcast.33, bf16[2,3,256,128]{3,2,1,0:T(8,128)(2,1)} %bitcast.36, bf16[2,3,256,128]{3,2,1,0:T(8,128)(2,1)} %bitcast.39, bf16[2,3,256,128]{3,2,1,0:T(8,128)(2,1)} %bitcast.42), custom_call_target="tpu_custom_call" | custom-call | tf_op jit(solution)/shard_map/gather/pallas_call | solution.py:398
  57.5 3.8 %collective-permute-done.8.refs_8_ = bf16[2,12,256,128]{3,2,1,0:T(8,128)(2,1)} collective-permute-done((bf16[2,12,256,128]{3,2,1,0:T(8,128)(2,1)}, bf16[2,12,256,128]{3,2,1,0:T(8,128)(2,1)}, u32[]{:S(2)}, u32[]{:S(2)}) %collective-permute-start.8) | collective-permute-done | bytes 1572896 | tf_op jit(solution)/shard_map/ppermute | solution.py:408
  61.2 36.3 %far.1 = (bf16[12,256,128]{2,1,0:T(8,128)(2,1)}, bf16[12,256,128]{2,1,0:T(8,128)(2,1)}, f32[12,256,128]{2,1,0:T(8,128)}, f32[12,256,128]{2,1,0:T(8,128)}, bf16[2,12,256,128]{3,2,1,0:T(8,128)(2,1)}) custom-call(s32[5]{0:T(128)} %stack.29.at, s32[360]{0:T(512)} %pad_add_fusion.tab, s32[60]{0:T(128)} %pad_add_fusion.2.cls, s32[12]{0:T(128)} %broadcast_subtract_fusion.nvd, ...), custom_call_target="tpu_custom_call" | custom-call | flops 11660165120 | bytes 12582912 | tf_op jit(solution)/shard_map/far/pallas_call | solution.py:429
  97.6 3.7 %collective-permute-start.11 = (bf16[12,256,128]{2,1,0:T(8,128)(2,1)}, bf16[12,256,128]{2,1,0:T(8,128)(2,1)S(1)}, u32[]{:S(2)}, u32[]{:S(2)}) collective-permute-start(bf16[12,256,128]{2,1,0:T(8,128)(2,1)} %get-tuple-element.40), channel_id=1, source_target_pairs={{33,1},{35,3},{37,5},{39,7},{41,9},{43,11},{45,13},{47,15},{49,17}... | collective-permute-start | bytes 2359304 | tf_op jit(solution)/shard_map/ppermute | solution.py:438
  102.0 23.1 %own.1 = (f32[12,256,128]{2,1,0:T(8,128)}, f32[12,256,128]{2,1,0:T(8,128)}, f32[12,256,128]{2,1,0:T(8,128)}) custom-call(s32[5]{0:T(128)} %stack.29.at, s32[360]{0:T(512)} %pad_add_fusion.tab, s32[60]{0:T(128)} %pad_add_fusion.2.cls, s32[12]{0:T(128)} %broadcast_subtract_fusion.nvd, bf16[2,3,256,128]{3,2,1,0:T(8,128)(2,1)} %bitcast.32, ...), custom_call_target="tpu_custom_call" | custom-call | flops 5033164800 | bytes 12582912 | tf_op jit(solution)/shard_map/own/pallas_call | solution.py:441
  126.0 3.1 %dq.1 = (bf16[3,256,128]{2,1,0:T(8,128)(2,1)}, bf16[3,256,128]{2,1,0:T(8,128)(2,1)}, bf16[3,256,128]{2,1,0:T(8,128)(2,1)}, bf16[3,256,128]{2,1,0:T(8,128)(2,1)}) custom-call(s32[5]{0:T(128)} %stack.29.at, f32[12,256,128]{2,1,0:T(8,128)} %get-tuple-element.39.dq, bf16[12,256,128]{2,1,0:T(8,128)(2,1)} %copy-done), custom_call_target="tpu_custom_call" | custom-call | tf_op jit(solution)/shard_map/dq/pallas_call | solution.py:452
  133.8 4.9 %dkv.1 = (bf16[2,3,256,128]{3,2,1,0:T(8,128)(2,1)}, bf16[2,3,256,128]{3,2,1,0:T(8,128)(2,1)}, bf16[2,3,256,128]{3,2,1,0:T(8,128)(2,1)}, bf16[2,3,256,128]{3,2,1,0:T(8,128)(2,1)}) custom-call(s32[5]{0:T(128)} %stack.29.at, f32[12,256,128]{2,1,0:T(8,128)} %get-tuple-element.45.refs_0_, f32[12,256,128]{2,1,0:T(8,128)} %get-tuple-element.46.refs_1_, ...), custom_call_target="tpu_custom_call" | custom-call | tf_op jit(solution)/shard_map/dkv/pallas_call | solution.py:460
  138.7 3.2 %collective-permute-start.19 = (bf16[2,768,128]{2,1,0:T(8,128)(2,1)}, bf16[2,768,128]{2,1,0:T(8,128)(2,1)S(1)}, u32[]{:S(2)}, u32[]{:S(2)}) collective-permute-start(bf16[2,768,128]{2,1,0:T(8,128)(2,1)} %bitcast.48), channel_id=1, source_target_pairs={{4,0},{20,1},{6,2},{22,3},{8,4},{24,5},{10,6},{26,7},{12,8},{28,9}... | collective-permute-start | bytes 1179656 | tf_op jit(solution)/shard_map/ppermute | solution.py:391
  141.9 1.6 collective-permute-start.18
  144.6 2.5 %collective-permute-start.15 = (bf16[1,768,128]{2,1,0:T(8,128)(2,1)S(1)}, bf16[1,768,128]{2,1,0:T(8,128)(2,1)S(1)}, u32[]{:S(2)}, u32[]{:S(2)}) collective-permute-start(bf16[1,768,128]{2,1,0:T(8,128)(2,1)S(1)} %bitcast.49), channel_id=1, source_target_pairs={{12,0},{28,1},{14,2},{30,3},{0,4},{16,5},{2,6},{18,7},{4,8},{20,9}... | collective-permute-start | bytes 589832 | tf_op jit(solution)/shard_map/ppermute | solution.py:391
  147.1 22.6 %collective-permute-done.15.refs_3_ = bf16[1,768,128]{2,1,0:T(8,128)(2,1)S(1)} collective-permute-done((bf16[1,768,128]{2,1,0:T(8,128)(2,1)S(1)}, bf16[1,768,128]{2,1,0:T(8,128)(2,1)S(1)}, u32[]{:S(2)}, u32[]{:S(2)}) %collective-permute-start.15) | collective-permute-done | bytes 196640 | tf_op jit(solution)/shard_map/ppermute | solution.py:391
  170.4 2.6 %join.2 = bf16[768,512]{1,0:T(8,128)(2,1)} custom-call(s32[2]{0:T(128)} %pad_add_fusion.1.at, bf16[1,768,128]{2,1,0:T(8,128)(2,1)} %copy-done.16, bf16[1,768,128]{2,1,0:T(8,128)(2,1)} %copy-done.15, bf16[1,768,128]{2,1,0:T(8,128)(2,1)} %copy-done.17, bf16[1,768,128]{2,1,0:T(8,128)(2,1)} %copy-done.18), custom_call_target="tpu_custom_call" | custom-call | tf_op jit(solution)/shard_map/join/pallas_call | solution.py:471
  174.8 3.0 %join.3 = (bf16[768,512]{1,0:T(8,128)(2,1)}, bf16[768,512]{1,0:T(8,128)(2,1)}) custom-call(s32[2]{0:T(128)} %pad_add_fusion.1.at, bf16[2,768,128]{2,1,0:T(8,128)(2,1)} %copy-done.12, bf16[2,768,128]{2,1,0:T(8,128)(2,1)} %copy-done.11, bf16[2,768,128]{2,1,0:T(8,128)(2,1)} %copy-done.13, bf16[2,768,128]{2,1,0:T(8,128)(2,1)} %copy-done.14), custom_call_target="tpu_custom_call" | custom-call | tf_op jit(solution)/shard_map/join/pallas_call | solution.py:471
  (106 shorter events, 27.5 us)
Async XLA Ops:
  4.3 17.7 %collective-permute-start.1 = (bf16[2,768,128]{2,1,0:T(8,128)(2,1)}, bf16[2,768,128]{2,1,0:T(8,128)(2,1)S(1)}, u32[]{:S(2)}, u32[]{:S(2)}) collective-permute-start(bf16[2,768,128]{2,1,0:T(8,128)(2,1)} %get-tuple-element.30), channel_id=1, source_target_pairs={{0,4},{1,20},{2,6},{3,22},{4,8},{5,24},{6,10},{7,26},{8,12},{9,28}... | collective-permute-start | bytes 1179656 | tf_op jit(solution)/shard_map/ppermute | solution.py:391
  6.0 21.6 %collective-permute-start.2 = (bf16[2,768,128]{2,1,0:T(8,128)(2,1)}, bf16[2,768,128]{2,1,0:T(8,128)(2,1)S(1)}, u32[]{:S(2)}, u32[]{:S(2)}) collective-permute-start(bf16[2,768,128]{2,1,0:T(8,128)(2,1)} %get-tuple-element.31), channel_id=1, source_target_pairs={{0,8},{1,24},{2,10},{3,26},{4,12},{5,28},{6,14},{7,30},{8,0},{9,16... | collective-permute-start | bytes 1179656 | tf_op jit(solution)/shard_map/ppermute | solution.py:391
  8.9 19.4 %collective-permute-start.3 = (bf16[2,768,128]{2,1,0:T(8,128)(2,1)}, bf16[2,768,128]{2,1,0:T(8,128)(2,1)S(1)}, u32[]{:S(2)}, u32[]{:S(2)}) collective-permute-start(bf16[2,768,128]{2,1,0:T(8,128)(2,1)} %get-tuple-element.32), channel_id=1, source_target_pairs={{0,12},{1,28},{2,14},{3,30},{4,0},{5,16},{6,2},{7,18},{8,4},{9,20}... | collective-permute-start | bytes 1179656 | tf_op jit(solution)/shard_map/ppermute | solution.py:391
  10.3 24.0 %collective-permute-start = (bf16[2,768,128]{2,1,0:T(8,128)(2,1)}, bf16[2,768,128]{2,1,0:T(8,128)(2,1)S(1)}, u32[]{:S(2)}, u32[]{:S(2)}) collective-permute-start(bf16[2,768,128]{2,1,0:T(8,128)(2,1)} %get-tuple-element.29.refs_0_), channel_id=1, source_target_pairs={{0,0},{1,16},{2,2},{3,18},{4,4},{5,20},{6,6},{7,22},{8,8},{9,24},{... | collective-permute-start | bytes 1179656 | tf_op jit(solution)/shard_map/ppermute | solution.py:391
  15.1 23.5 %collective-permute-start.4 = (bf16[2,768,128]{2,1,0:T(8,128)(2,1)}, bf16[2,768,128]{2,1,0:T(8,128)(2,1)S(1)}, u32[]{:S(2)}, u32[]{:S(2)}) collective-permute-start(bf16[2,768,128]{2,1,0:T(8,128)(2,1)} %get-tuple-element.33), channel_id=1, source_target_pairs={{0,0},{1,16},{2,2},{3,18},{4,4},{5,20},{6,6},{7,22},{8,8},{9,24},{... | collective-permute-start | bytes 1179656 | tf_op jit(solution)/shard_map/ppermute | solution.py:391
  22.0 17.9 %collective-permute-start.5 = (bf16[2,768,128]{2,1,0:T(8,128)(2,1)}, bf16[2,768,128]{2,1,0:T(8,128)(2,1)S(1)}, u32[]{:S(2)}, u32[]{:S(2)}) collective-permute-start(bf16[2,768,128]{2,1,0:T(8,128)(2,1)} %get-tuple-element.34), channel_id=1, source_target_pairs={{0,4},{1,20},{2,6},{3,22},{4,8},{5,24},{6,10},{7,26},{8,12},{9,28}... | collective-permute-start | bytes 1179656 | tf_op jit(solution)/shard_map/ppermute | solution.py:391
  27.6 19.3 %collective-permute-start.6 = (bf16[2,768,128]{2,1,0:T(8,128)(2,1)}, bf16[2,768,128]{2,1,0:T(8,128)(2,1)S(1)}, u32[]{:S(2)}, u32[]{:S(2)}) collective-permute-start(bf16[2,768,128]{2,1,0:T(8,128)(2,1)} %get-tuple-element.35), channel_id=1, source_target_pairs={{0,8},{1,24},{2,10},{3,26},{4,12},{5,28},{6,14},{7,30},{8,0},{9,16... | collective-permute-start | bytes 1179656 | tf_op jit(solution)/shard_map/ppermute | solution.py:391
  28.4 18.5 %collective-permute-start.7 = (bf16[2,768,128]{2,1,0:T(8,128)(2,1)}, bf16[2,768,128]{2,1,0:T(8,128)(2,1)S(1)}, u32[]{:S(2)}, u32[]{:S(2)}) collective-permute-start(bf16[2,768,128]{2,1,0:T(8,128)(2,1)} %get-tuple-element.36), channel_id=1, source_target_pairs={{0,12},{1,28},{2,14},{3,30},{4,0},{5,16},{6,2},{7,18},{8,4},{9,20}... | collective-permute-start | bytes 1179656 | tf_op jit(solution)/shard_map/ppermute | solution.py:391
  37.3 20.2 %collective-permute-start.9 = (bf16[2,12,256,128]{3,2,1,0:T(8,128)(2,1)}, bf16[2,12,256,128]{3,2,1,0:T(8,128)(2,1)}, u32[]{:S(2)}, u32[]{:S(2)}) collective-permute-start(bf16[2,12,256,128]{3,2,1,0:T(8,128)(2,1)} %gather.2), channel_id=1, source_target_pairs={{1,0},{3,2},{5,4},{7,6},{9,8},{11,10},{13,12},{15,14},{17,16},{19,... | collective-permute-start | bytes 4718600 | tf_op jit(solution)/shard_map/ppermute | solution.py:409
  38.6 22.6 %collective-permute-start.8 = (bf16[2,12,256,128]{3,2,1,0:T(8,128)(2,1)}, bf16[2,12,256,128]{3,2,1,0:T(8,128)(2,1)}, u32[]{:S(2)}, u32[]{:S(2)}) collective-permute-start(bf16[2,12,256,128]{3,2,1,0:T(8,128)(2,1)} %gather.2), channel_id=1, source_target_pairs={{1,33},{3,35},{5,37},{7,39},{9,41},{11,43},{13,45},{15,47},{17,49}... | collective-permute-start | bytes 4718600 | tf_op jit(solution)/shard_map/ppermute | solution.py:408
  50.0 7.4 %collective-permute-start.10 = (bf16[2,12,256,128]{3,2,1,0:T(8,128)(2,1)}, bf16[2,12,256,128]{3,2,1,0:T(8,128)(2,1)S(1)}, u32[]{:S(2)}, u32[]{:S(2)}) collective-permute-start(bf16[2,12,256,128]{3,2,1,0:T(8,128)(2,1)} %gather.3), channel_id=1, source_target_pairs={{0,1},{2,3},{4,5},{6,7},{8,9},{10,11},{12,13},{14,15},{16,17},{18,... | collective-permute-start | bytes 4718600 | tf_op jit(solution)/shard_map/ppermute | solution.py:410
  97.5 34.8 %collective-permute-start.16 = (bf16[2,12,256,128]{3,2,1,0:T(8,128)(2,1)}, bf16[2,12,256,128]{3,2,1,0:T(8,128)(2,1)S(1)}, u32[]{:S(2)}, u32[]{:S(2)}) collective-permute-start(bf16[2,12,256,128]{3,2,1,0:T(8,128)(2,1)} %get-tuple-element.47), channel_id=1, source_target_pairs={{0,1},{1,0},{2,3},{3,2},{4,5},{5,4},{6,7},{7,6},{8,9},{9,8},{10,11... | collective-permute-start | bytes 4718600 | tf_op jit(solution)/shard_map/ppermute | solution.py:440
  97.6 27.5 %collective-permute-start.11 = (bf16[12,256,128]{2,1,0:T(8,128)(2,1)}, bf16[12,256,128]{2,1,0:T(8,128)(2,1)S(1)}, u32[]{:S(2)}, u32[]{:S(2)}) collective-permute-start(bf16[12,256,128]{2,1,0:T(8,128)(2,1)} %get-tuple-element.40), channel_id=1, source_target_pairs={{33,1},{35,3},{37,5},{39,7},{41,9},{43,11},{45,13},{47,15},{49,17}... | collective-permute-start | bytes 2359304 | tf_op jit(solution)/shard_map/ppermute | solution.py:438
  101.3 31.1 %collective-permute-start.17 = (bf16[12,256,128]{2,1,0:T(8,128)(2,1)}, bf16[12,256,128]{2,1,0:T(8,128)(2,1)S(1)}, u32[]{:S(2)}, u32[]{:S(2)}) collective-permute-start(bf16[12,256,128]{2,1,0:T(8,128)(2,1)} %get-tuple-element.48), channel_id=1, source_target_pairs={{33,1},{35,3},{37,5},{39,7},{41,9},{43,11},{45,13},{47,15},{49,17}... | collective-permute-start | bytes 2359304 | tf_op jit(solution)/shard_map/ppermute | solution.py:439
  129.1 14.4 %collective-permute-start.13 = (bf16[1,768,128]{2,1,0:T(8,128)(2,1)}, bf16[1,768,128]{2,1,0:T(8,128)(2,1)S(1)}, u32[]{:S(2)}, u32[]{:S(2)}) collective-permute-start(bf16[1,768,128]{2,1,0:T(8,128)(2,1)} %bitcast.52), channel_id=1, source_target_pairs={{4,0},{20,1},{6,2},{22,3},{8,4},{24,5},{10,6},{26,7},{12,8},{28,9}... | collective-permute-start | bytes 589832 | tf_op jit(solution)/shard_map/ppermute | solution.py:391
  130.0 13.6 %collective-permute-start.12 = (bf16[1,768,128]{2,1,0:T(8,128)(2,1)}, bf16[1,768,128]{2,1,0:T(8,128)(2,1)S(1)}, u32[]{:S(2)}, u32[]{:S(2)}) collective-permute-start(bf16[1,768,128]{2,1,0:T(8,128)(2,1)} %bitcast.51), channel_id=1, source_target_pairs={{0,0},{16,1},{2,2},{18,3},{4,4},{20,5},{6,6},{22,7},{8,8},{24,9},{... | collective-permute-start | bytes 589832 | tf_op jit(solution)/shard_map/ppermute | solution.py:391
  131.5 13.0 %collective-permute-start.14 = (bf16[1,768,128]{2,1,0:T(8,128)(2,1)}, bf16[1,768,128]{2,1,0:T(8,128)(2,1)S(1)}, u32[]{:S(2)}, u32[]{:S(2)}) collective-permute-start(bf16[1,768,128]{2,1,0:T(8,128)(2,1)} %bitcast.50), channel_id=1, source_target_pairs={{8,0},{24,1},{10,2},{26,3},{12,4},{28,5},{14,6},{30,7},{0,8},{16,9... | collective-permute-start | bytes 589832 | tf_op jit(solution)/shard_map/ppermute | solution.py:391
  138.7 34.3 %collective-permute-start.19 = (bf16[2,768,128]{2,1,0:T(8,128)(2,1)}, bf16[2,768,128]{2,1,0:T(8,128)(2,1)S(1)}, u32[]{:S(2)}, u32[]{:S(2)}) collective-permute-start(bf16[2,768,128]{2,1,0:T(8,128)(2,1)} %bitcast.48), channel_id=1, source_target_pairs={{4,0},{20,1},{6,2},{22,3},{8,4},{24,5},{10,6},{26,7},{12,8},{28,9}... | collective-permute-start | bytes 1179656 | tf_op jit(solution)/shard_map/ppermute | solution.py:391
  141.9 31.1 %collective-permute-start.18 = (bf16[2,768,128]{2,1,0:T(8,128)(2,1)}, bf16[2,768,128]{2,1,0:T(8,128)(2,1)S(1)}, u32[]{:S(2)}, u32[]{:S(2)}) collective-permute-start(bf16[2,768,128]{2,1,0:T(8,128)(2,1)} %bitcast.47), channel_id=1, source_target_pairs={{0,0},{16,1},{2,2},{18,3},{4,4},{20,5},{6,6},{22,7},{8,8},{24,9},{... | collective-permute-start | bytes 1179656 | tf_op jit(solution)/shard_map/ppermute | solution.py:391
  143.5 26.2 %copy-start.15 = (bf16[1,768,128]{2,1,0:T(8,128)(2,1)}, bf16[1,768,128]{2,1,0:T(8,128)(2,1)S(1)}, u32[]{:S(2)}) copy-start(bf16[1,768,128]{2,1,0:T(8,128)(2,1)S(1)} %collective-permute-done.13.refs_1_) | copy-start | bytes 589828
  143.6 29.5 %collective-permute-start.20 = (bf16[2,768,128]{2,1,0:T(8,128)(2,1)}, bf16[2,768,128]{2,1,0:T(8,128)(2,1)S(1)}, u32[]{:S(2)}, u32[]{:S(2)}) collective-permute-start(bf16[2,768,128]{2,1,0:T(8,128)(2,1)} %bitcast.46), channel_id=1, source_target_pairs={{8,0},{24,1},{10,2},{26,3},{12,4},{28,5},{14,6},{30,7},{0,8},{16,9... | collective-permute-start | bytes 1179656 | tf_op jit(solution)/shard_map/ppermute | solution.py:391
  143.6 26.1 %copy-start.16 = (bf16[1,768,128]{2,1,0:T(8,128)(2,1)}, bf16[1,768,128]{2,1,0:T(8,128)(2,1)S(1)}, u32[]{:S(2)}) copy-start(bf16[1,768,128]{2,1,0:T(8,128)(2,1)S(1)} %collective-permute-done.12.refs_0_) | copy-start | bytes 589828
  143.6 29.5 %collective-permute-start.21 = (bf16[2,768,128]{2,1,0:T(8,128)(2,1)}, bf16[2,768,128]{2,1,0:T(8,128)(2,1)S(1)}, u32[]{:S(2)}, u32[]{:S(2)}) collective-permute-start(bf16[2,768,128]{2,1,0:T(8,128)(2,1)} %bitcast.45), channel_id=1, source_target_pairs={{12,0},{28,1},{14,2},{30,3},{0,4},{16,5},{2,6},{18,7},{4,8},{20,9}... | collective-permute-start | bytes 1179656 | tf_op jit(solution)/shard_map/ppermute | solution.py:391
  144.6 25.1 %collective-permute-start.15 = (bf16[1,768,128]{2,1,0:T(8,128)(2,1)S(1)}, bf16[1,768,128]{2,1,0:T(8,128)(2,1)S(1)}, u32[]{:S(2)}, u32[]{:S(2)}) collective-permute-start(bf16[1,768,128]{2,1,0:T(8,128)(2,1)S(1)} %bitcast.49), channel_id=1, source_target_pairs={{12,0},{28,1},{14,2},{30,3},{0,4},{16,5},{2,6},{18,7},{4,8},{20,9}... | collective-permute-start | bytes 589832 | tf_op jit(solution)/shard_map/ppermute | solution.py:391
  (21 other events, 102.9 us)

commit v4 on v3

v4 whole, which is shorter than its diff:
```python
import functools
import math

import jax
import jax.numpy as jnp
from jax import lax
from jax.experimental import pallas as pl
from jax.experimental.pallas import tpu as pltpu
from jax.sharding import PartitionSpec as P

F32, BF = jnp.float32, jnp.bfloat16
HEAD, BLK, KPB = 128, 256, 16
PLANE, HALF = 24, 12
AXES = ("ctx", "tp")
U_SCALE = 0.5 / math.sqrt(HEAD)
V_SCALE = 1.0 / math.sqrt(KPB * BLK)
QK_SCALE = 0.5 * V_SCALE / math.sqrt(HEAD)
GROUP = 6
CLASSES = (160, 192, 224, 256)
SPOTS = 256
MOST = 10
DUMMY = (24, 12)
VMEM = pl.BlockSpec(memory_space=pltpu.VMEM)
SMEM = pl.BlockSpec(memory_space=pltpu.SMEM)
ANY = pl.BlockSpec(memory_space=pl.ANY)


def place(z, x, y, hi, core):
    return (z * 8 + x * 4 + y % 4) * 4 + hi * 2 + core


DEVICES = [
    (z, x, y, hi, core)
    for z in range(4)
    for x in range(2)
    for y in range(4)
    for hi in range(2)
    for core in range(2)
]


def to_heads(d):
    return [(place(z, x, y, hi, c), place(z, c, y + d, hi, x)) for z, x, y, hi, c in DEVICES]


def from_heads(d):
    return [(j, i) for i, j in to_heads(d)]


OTHER_CORE = [(place(z, x, y, hi, c), place(z, x, y, hi, 1 - c)) for z, x, y, hi, c in DEVICES]
ALONG_Z = [
    (place(z, x, y, hi, c), place(z + 2 * c - 1, x, y, hi, c))
    for z, x, y, hi, c in DEVICES
    if 0 <= z + 2 * c - 1 < 4
]
BACK_Z = [(j, i) for i, j in ALONG_Z]
BACK_Z_SECOND = [(j, i) for j, i in BACK_Z if i % 2]


def nt(a, b):
    return lax.dot_general(a, b, (((1,), (1,)), ((), ())), preferred_element_type=F32)


def nn(a, b):
    return lax.dot_general(a, b, (((1,), (0,)), ((), ())), preferred_element_type=F32)


def tn(a, b):
    return lax.dot_general(a, b, (((0,), (0,)), ((), ())), preferred_element_type=F32)


def relay(moves, stage, sems):
    ins = [
        pltpu.make_async_copy(src, stage.at[n], sems.at[0, n]) for n, (src, _) in enumerate(moves)
    ]
    outs = [
        pltpu.make_async_copy(stage.at[n], dst, sems.at[1, n]) for n, (_, dst) in enumerate(moves)
    ]
    for copy in ins:
        copy.start()
    for n, copy in enumerate(ins):
        copy.wait()
        outs[n].start()
    for copy in outs:
        copy.wait()


def split_kernel(first_round, at, q, g, k, v, *refs):
    outs, (stage, sems) = refs[-6:-2], refs[-2:]
    y, x = at[0], at[1]
    for side, pair in ((0, (q, g)), (1, (k, v))):

        @pl.when(x == (side if first_round else 1 - side))
        def _(pair=pair):
            moves = []
            for d in range(4):
                lanes = pl.ds(pl.multiple_of(lax.rem(y + d, 4) * HEAD, HEAD), HEAD)
                moves += [(pair[n].at[:, lanes], outs[d].at[n]) for n in range(2)]
            relay(moves, stage, sems)


def gather_kernel(*refs):
    ins, (out, stage, sems) = refs[:4], refs[-3:]
    relay([(ins[d], out.at[:, pl.ds(3 * d, 3)]) for d in range(4)], stage, sems)


def gather_keys_kernel(at, *refs):
    ins, (most, rest, stage, sems) = refs[:8], refs[8:]
    for own, pieces in ((0, ins[4:]), (1, ins[:4])):

        @pl.when(at[2] == own)
        def _(pieces=pieces):
            moves = []
            for d in range(4):
                for m in range(3):
                    b = 3 * d + m
                    to = most.at[:, b] if b < MOST else rest.at[:, b - MOST]
                    moves.append((pieces[d].at[:, m], to))
            relay(moves, stage, sems)


def pair_grads(scores, weight_grad, allowed):
    u = scores * U_SCALE
    t = jnp.tanh(u)
    p = jnp.where(allowed, 1.0 + t, 0.0)
    w = u * p
    slope = p + w * (1.0 - t)
    return w.astype(BF), (weight_grad * slope).astype(BF)


def pairs_kernel(phase, at, tab, *refs):
    r1, r2 = refs[0:4], refs[4:8]
    extra = refs[8:10] if phase else refs[8:11]
    refs = refs[10:] if phase else refs[11:]
    if phase:
        outs, refs = refs[:3], refs[3:]
        (*made, s1, s2), refs = refs[:5], refs[5:]
    else:
        outs, refs = refs[:4], refs[4:]
        made, refs = refs[:5], refs[5:]
    qs, gs, ks, vs, dqa, dka, dva, sems = refs
    core, groups = at[2], (tab[phase, SPOTS - 1] + GROUP - 1) // GROUP

    def copies(own):
        qg, kv = ((r1, r2), (r2, r1))[own]
        out = []
        for d in range(4):
            rows = pl.ds(3 * d, 3)
            if phase == 1 or own == 1:
                out += [(qg[d].at[0], qs.at[rows]), (qg[d].at[1], gs.at[rows])]
            if phase == 1 or own == 0:
                out += [(kv[d].at[0], ks.at[rows]), (kv[d].at[1], vs.at[rows])]
        if phase == 0:
            across, most, rest = extra
            to = (ks, vs) if own else (qs, gs)
            for n in range(2):
                out.append((across.at[n], to[n].at[pl.ds(0, HALF)]))
                out.append((most.at[n], (ks, vs)[n].at[pl.ds(HALF, MOST)]))
                out.append((rest.at[n], (ks, vs)[n].at[pl.ds(HALF + MOST, HALF - MOST)]))
        return [pltpu.make_async_copy(a, b, sems.at[i]) for i, (a, b) in enumerate(out)]

    def late():
        return [
            pltpu.make_async_copy(extra[0], s1, sems.at[42]),
            pltpu.make_async_copy(extra[1], s2, sems.at[43]),
        ]

    for own in range(2):

        @pl.when(core == own)
        def _(own=own):
            for copy in copies(own):
                copy.start()

    if phase:
        for copy in late():
            copy.start()
    dqa[...] = jnp.zeros_like(dqa)
    dka[...] = jnp.zeros_like(dka)
    dva[...] = jnp.zeros_like(dva)
    zero = jnp.zeros((BLK, HEAD), BF)
    dummy = DUMMY[phase]
    qs[HALF], gs[HALF], ks[dummy], vs[dummy] = zero, zero, zero, zero

    for own in range(2):

        @pl.when(core == own)
        def _(own=own):
            for copy in copies(own):
                copy.wait()

    def work(items, rows):
        made = []
        for q, k, mask in items:
            key, value, query, grad = ks[k, :rows], vs[k, :rows], qs[q], gs[q]
            made.append((q, k, mask, key, query, grad, nt(key, query), nt(value, grad)))
        for q, k, mask, key, query, grad, scores, weight_grad in made:
            w, sg = pair_grads(scores, weight_grad, mask)
            dva[k, :rows] += nn(w, grad)
            dka[k, :rows] += nn(sg, query)
            dqa[q] += tn(key, sg)

    def own_group(g, _):
        items = []
        row = lax.broadcasted_iota(jnp.int32, (BLK, BLK), 0)
        col = lax.broadcasted_iota(jnp.int32, (BLK, BLK), 1)
        for i in range(4):
            slot = g * 4 + i
            items.append((slot, slot, (row == col) | ((row < col) & (row < tab[2, slot]))))
        work(items, BLK)
        return 0

    if phase:
        lax.fori_loop(0, 3, own_group, 0)

    def group(g, _):
        for c, rows in enumerate(CLASSES):

            @pl.when((tab[phase, g * GROUP + GROUP - 1] >> 18) == c)
            def _(rows=rows):
                row = lax.broadcasted_iota(jnp.int32, (rows, BLK), 0)
                items = []
                for i in range(GROUP):
                    e = tab[phase, g * GROUP + i]
                    items.append((e & 15, (e >> 4) & 31, row < ((e >> 9) & 511)))
                work(items, rows)

        return 0

    lax.fori_loop(0, groups, group, 0)

    if phase:
        for copy in late():
            copy.wait()

    def finish(s):
        dq, dk, dv = dqa[s].T * QK_SCALE, dka[s] * QK_SCALE, dva[s] * V_SCALE
        if phase:
            before, last = s1[s].astype(F32), s2[s].astype(F32)
            made[0][s] = (dq + jnp.where(core == 1, before, 0.0)).astype(BF)
            made[1][s] = (dk + jnp.where(core == 0, before, 0.0)).astype(BF)
            made[2][s] = (dv + jnp.where(core == 0, last, 0.0)).astype(BF)
        else:
            made[0][s] = jnp.where(core == 0, dq, dk).astype(BF)
            made[1][s] = dv.astype(BF)
            made[2][s] = jnp.where(core == 0, dk, dq).astype(BF)
            made[3][s] = (dka[HALF + s] * QK_SCALE).astype(BF)
            made[4][s] = (dva[HALF + s] * V_SCALE).astype(BF)

    targets = outs if phase else (outs[0], outs[1], outs[2], outs[3].at[0], outs[3].at[1])
    going = []
    for part in range(4):
        lax.fori_loop(3 * part, 3 * part + 3, lambda s, _: (finish(s), 0)[1], 0)
        rows = pl.ds(3 * part, 3)
        for n, (src, dst) in enumerate(zip(made, targets)):
            going.append(
                pltpu.make_async_copy(src.at[rows], dst.at[rows], sems.at[5 * part + n])
            )
            going[-1].start()
    for copy in going:
        copy.wait()


def piped(ins, shapes, in_sems, outs, staged, out_sems, compute):
    def coming(d):
        rows = pl.ds(3 * d, 3)
        return [
            pltpu.make_async_copy(
                src.at[:, rows] if four else src.at[rows],
                dst.at[:, rows] if four else dst.at[rows],
                in_sems.at[d, n],
            )
            for n, (src, dst, four) in enumerate(zip(ins, shapes[0], shapes[1]))
        ]

    def going(d):
        return pltpu.make_async_copy(staged.at[d], outs[d], out_sems.at[d])

    for d in range(4):
        for copy in coming(d):
            copy.start()
    for d in range(4):
        for copy in coming(d):
            copy.wait()
        compute(d)
        going(d).start()
    for d in range(4):
        going(d).wait()


def sum_kernel(at, *refs):
    ins, outs = refs[:6], refs[6:10]
    bufs, (staged, in_sems, out_sems) = refs[10:16], refs[16:]
    dq, dk, dv, beside, a1, a2 = bufs
    first = at[2] == 0

    def compute(d):
        for m in range(3):
            s = 3 * d + m
            far = a1[s].astype(F32)
            last = jnp.where(first, 0.0, a2[s].astype(F32))
            staged[d, 0, m] = (dq[s].astype(F32) + jnp.where(first, far, 0.0)).astype(BF)
            far = jnp.where(first, 0.0, far)
            staged[d, 1, m] = (dk[s].astype(F32) + beside[0, s].astype(F32) + far).astype(BF)
            staged[d, 2, m] = (dv[s].astype(F32) + beside[1, s].astype(F32) + last).astype(BF)

    piped(ins, (bufs, (0, 0, 0, 1, 0, 0)), in_sems, outs, staged, out_sems, compute)


def join_kernel(arrays, at, *refs):
    outs, (stage, sems) = refs[4 : 4 + arrays], refs[-2:]
    moves = []
    for d in range(4):
        lanes = pl.ds(pl.multiple_of(lax.rem(at[0] + d, 4) * HEAD, HEAD), HEAD)
        moves += [(refs[d].at[n], outs[n].at[:, lanes]) for n in range(arrays)]
    relay(moves, stage, sems)


def call(kernel, outs, ins, scratch=(), limit=56, where=ANY, cost=None, **kw):
    return pl.pallas_call(
        kernel,
        out_shape=outs,
        in_specs=ins,
        out_specs=[where] * len(outs),
        scratch_shapes=scratch,
        compiler_params=pltpu.CompilerParams(vmem_limit_bytes=limit * 2**20),
        cost_estimate=cost,
        **kw,
    )


def table_kernel(at, counts, rows, out):
    y, core, z = at[0], at[2], at[3]
    shape = rows.shape[1:]
    lane = lax.broadcasted_iota(jnp.int32, shape, 1)
    line = lax.broadcasted_iota(jnp.int32, shape, 0)
    spot = lax.broadcasted_iota(jnp.int32, (shape[0], SPOTS), 1)
    ahead = (
        lax.broadcasted_iota(jnp.int32, (128, 128), 0)
        < lax.broadcasted_iota(jnp.int32, (128, 128), 1)
    ).astype(F32)
    above = (
        lax.broadcasted_iota(jnp.int32, (shape[0], shape[0]), 1)
        < lax.broadcasted_iota(jnp.int32, (shape[0], shape[0]), 0)
    ).astype(F32)

    def at_least(a, *bounds):
        return sum((a >= b).astype(jnp.int32) for b in bounds)

    def slot(u):
        third = at_least(u, 3, 6, 9)
        return ((y - third) & 3) * 3 + u - 3 * third

    def place_values(rank, value, columns):
        made = jnp.zeros((shape[0], SPOTS), jnp.int32)
        for j in columns:
            made += jnp.where(rank[:, j : j + 1] == spot, value[:, j : j + 1], 0)
        return jnp.sum(made, 0, keepdims=True)

    for phase in range(2):
        kid = rows[0] if phase else jnp.where(core == 0, rows[1], rows[0])
        kept = jnp.zeros(shape, jnp.int32)
        for k in range(4 * PLANE):
            kept = jnp.where(kid == k, BLK - counts[k], kept)
        plane = at_least(kid, PLANE, 2 * PLANE, 3 * PLANE)
        t = kid - PLANE * plane
        half = at_least(t, HALF)
        listed = (
            at_least(kid, 0) * at_least(lane, 1) * (1 - at_least(lane, KPB)) * (1 - at_least(line, HALF))
        )
        here, same = (plane == z).astype(jnp.int32), (half == core).astype(jnp.int32)
        ks = slot(t - HALF * half)
        if phase:
            valid = listed * here * same
        else:
            above_it = (z < 3).astype(jnp.int32)
            valid = listed * jnp.where(core == 0, here * above_it, 1 - here * same)
            ks = ks + HALF * here * (1 - same)
        cls = jnp.clip(((kept + 31) >> 5) - 5, 0, 3)
        value = slot(line) | (ks << 4) | (kept << 9) | (cls << 18)
        rank, total = jnp.full(shape, -1, jnp.int32), 0
        for c in range(4):
            mine = valid * (cls == c).astype(jnp.int32)
            ones = mine.astype(F32)
            before = nn(ones, ahead) + jnp.sum(nn(above, ones), 1, keepdims=True)
            rank = jnp.where(mine > 0, total + before.astype(jnp.int32), rank)
            total = total + jnp.sum(mine)
        made = place_values(rank, value, range(1, KPB))
        first = spot[:1]
        made = jnp.where(first < total, made, HALF | (DUMMY[phase] << 4) | (3 << 18))
        out[phase : phase + 1] = jnp.where(first == SPOTS - 1, total, made)
        if phase:
            out[2:3] = place_values(jnp.where(line < HALF, slot(line), -1), kept, (0,))


def pairs_cost(pairs):
    return pl.CostEstimate(
        flops=pairs * 10 * BLK * BLK * HEAD, bytes_accessed=12 * 2**20, transcendentals=pairs * BLK * BLK
    )


def body(queries, keys, values, out_grad, key_blocks, target_counts):
    ctx, tp = lax.axis_index("ctx"), lax.axis_index("tp")
    z, x, y, core = ctx // 8, (ctx // 4) % 2, ctx % 4, tp % 2
    at = jnp.stack([y, x, core, z]).astype(jnp.int32)
    rows = queries.shape[0]
    shape = jax.ShapeDtypeStruct
    dma = lambda *n: pltpu.SemaphoreType.DMA(n)
    own = lax.dynamic_slice(key_blocks, (PLANE * z + HALF * core, 0), (HALF, KPB))
    after = lax.dynamic_slice(key_blocks, (jnp.minimum(PLANE * (z + 1), 84), 0), (HALF, KPB))
    lists = jnp.pad(jnp.stack([own, after]), ((0, 0), (0, 4), (0, 128 - KPB)), constant_values=-1)
    tab = call(
        table_kernel,
        [shape((3, SPOTS), jnp.int32)],
        [SMEM, SMEM, VMEM],
        where=VMEM,
        name="table",
    )(at, target_counts, lists)[0]
    half = shape((HALF, BLK, HEAD), BF)

    def split(first_round, *behind):
        return call(
            functools.partial(split_kernel, first_round),
            [shape((2, rows, HEAD), BF)] * 4,
            [SMEM] + [ANY] * (4 + len(behind)),
            [pltpu.VMEM((8, rows, HEAD), BF), dma(2, 8)],
            limit=56,
            name="split",
        )(at, queries, out_grad, keys, values, *behind)

    def send(pieces, pairs):
        return [lax.ppermute(p, AXES, pairs(d)) for d, p in enumerate(pieces)]

    two = shape((2, HALF, BLK, HEAD), BF)


    def blocks(pieces):
        return [p.reshape(2, 3, BLK, HEAD) for p in pieces]

    sent1 = split(True)
    sent2 = split(False, sent1[0], tab)
    r1 = blocks(send(sent1, to_heads))
    r2 = blocks(send(sent2, to_heads))
    first = call(
        gather_kernel,
        [two],
        [ANY] * 5,
        [pltpu.VMEM((4, 2, 3, BLK, HEAD), BF), dma(2, 4)],
        name="gather",
    )(*r1, sent2[0])[0]
    across = lax.ppermute(first, AXES, ALONG_Z)
    near = call(
        gather_keys_kernel,
        [shape((2, n, BLK, HEAD), BF) for n in (MOST, HALF - MOST)],
        [SMEM] + [ANY] * 8,
        [pltpu.VMEM((HALF, 2, BLK, HEAD), BF), dma(2, HALF)],
        name="gather_keys",
    )(at, *r1, *r2)
    near = [lax.ppermute(n, AXES, OTHER_CORE) for n in near]

    def scratch(k):
        return [
            pltpu.VMEM((HALF + 1, BLK, HEAD), BF),
            pltpu.VMEM((HALF + 1, BLK, HEAD), BF),
            pltpu.VMEM((k + 1, BLK, HEAD), BF),
            pltpu.VMEM((k + 1, BLK, HEAD), BF),
            pltpu.VMEM((HALF + 1, HEAD, BLK), F32),
            pltpu.VMEM((k + 1, BLK, HEAD), F32),
            pltpu.VMEM((k + 1, BLK, HEAD), F32),
        ]

    parts = [pltpu.VMEM((HALF, BLK, HEAD), BF)] * 5
    p1, p2, s1, beside = call(
        functools.partial(pairs_kernel, 0),
        [half, half, half, two],
        [SMEM] * 2 + [ANY] * 11,
        parts + scratch(PLANE) + [dma(44)],
        cost=pairs_cost(139),
        name="far",
    )(at, tab, *r1, *r2, across, *near)
    s2 = p2
    p1 = lax.ppermute(p1, AXES, BACK_Z)
    p2 = lax.ppermute(p2, AXES, BACK_Z_SECOND)
    beside = lax.ppermute(beside, AXES, OTHER_CORE)
    dq, dk, dv = call(
        functools.partial(pairs_kernel, 1),
        [half, half, half],
        [SMEM] * 2 + [ANY] * 10,
        parts + scratch(HALF) + [dma(44)],
        cost=pairs_cost(60),
        name="own",
    )(at, tab, *r1, *r2, s1, s2)
    v3, v4 = pltpu.VMEM((HALF, BLK, HEAD), BF), pltpu.VMEM((2, HALF, BLK, HEAD), BF)
    sums = call(
        sum_kernel,
        [shape((3, 3, BLK, HEAD), BF)] * 4,
        [SMEM] + [ANY] * 6,
        [v3, v3, v3, v4, v3, v3, pltpu.VMEM((4, 3, 3, BLK, HEAD), BF), dma(4, 6), dma(4)],
        name="sums",
    )(at, dq, dk, dv, beside, p1, p2)
    back = send([p.reshape(3, rows, HEAD) for p in sums], from_heads)
    out = shape(queries.shape, BF)
    return tuple(
        call(
            functools.partial(join_kernel, 3),
            [out] * 3,
            [SMEM] + [ANY] * 4,
            [pltpu.VMEM((12, rows, HEAD), BF), dma(2, 12)],
            name="join",
        )(at, *back)
    )


def solution(mesh):
    in_specs = (P("ctx", "tp"),) * 4 + (P(), P())
    return jax.shard_map(
        body, mesh=mesh, in_specs=in_specs, out_specs=(P("ctx", "tp"),) * 3, check_vma=False
    )
```

time: 181 us -> 162 us (0.90)
  other arithmetic: 8.13 us -> 0.68 us
  starting transfers between devices: 33.2 us -> 26.2 us
  Pallas kernels: 83.5 us -> 77.9 us
  waiting for transfers between devices: 42.7 us -> 48 us
    pallas_call x8 -> x7, Pallas kernels: 77.5 us -> 71.7 us  [the longest x1 35.4 us: body(): call(functools.partial(pairs_kernel, 0), [half, half, half, two], [SMEM]...]
    reduce_sum x8 -> x0, other arithmetic: 2.67 us -> none  [the longest x2 1.29 us: table(): total = jnp.sum(valid.astype(jnp.int32))]
    ppermute x16 -> x12, waiting for transfers between devices: 38.9 us -> 41.6 us  [send(): return [lax.ppermute(p, AXES, pairs(d)) for d, p in enumerate(pieces)]]
    ppermute x3, waiting for transfers between devices: 3.77 us -> 6.42 us  [the longest x1 3.31 us: body(): across = lax.ppermute(first, AXES, ALONG_Z)]
    ppermute x16 -> x12, starting transfers between devices: 24.8 us -> 22.1 us  [send(): return [lax.ppermute(p, AXES, pairs(d)) for d, p in enumerate(pieces)]]
    ppermute x1, starting transfers between devices: 3.65 us -> 1.34 us  [body(): p1 = lax.ppermute(p1, AXES, BACK_Z)]
    ppermute x3, starting transfers between devices: 3.97 us -> 1.87 us  [the longest x1 1.29 us: body(): across = lax.ppermute(first, AXES, ALONG_Z)]
    unnamed x48 -> x38, local copies, waits for them, and re-layouts: 6.49 us -> 5.39 us
  transfers between devices with their start and end apart: 22 -> 18, of which waited for: 5 -> 7; matrix products, arithmetic and copies ran while one was open for 5% -> 1% of each run, Pallas kernels for 23% -> 20%
where the time goes in v4:
time: 162 us; the launch traced here: 160 us
  Pallas kernels  77.9 us (48%)
  waiting for transfers between devices  48 us (30%)
  starting transfers between devices  26.2 us (16%)
  local copies, waits for them, and re-layouts  6.24 us (4%)
    ppermute x12, waiting for transfers between devices, send(): return [lax.ppermute(p, AXES, pairs(d)) for d, p in enumerate(pieces)]  41.6 us
    pallas_call x1, Pallas kernels, body(): call(functools.partial(pairs_kernel, 0), [half, half, half, two], [SMEM]...  35.4 us
    ppermute x12, starting transfers between devices, send(): return [lax.ppermute(p, AXES, pairs(d)) for d, p in enumerate(pieces)]  22.1 us
    pallas_call x1, Pallas kernels, body(): call(functools.partial(pairs_kernel, 1), [half, half, half], [SMEM] * 2 +...  21.1 us
    pallas_call x2, Pallas kernels, split(): call(functools.partial(split_kernel, first_round), [shape((2, rows, HEAD)...  6.16 us
    unnamed x38, local copies, waits for them, and re-layouts  5.39 us
    pallas_call x1, Pallas kernels, body(): call(sum_kernel, [shape((3, 3, BLK, HEAD), BF)] * 4, [SMEM] + [ANY] * 6,...  4.81 us
    ppermute x1, waiting for transfers between devices, body(): across = lax.ppermute(first, AXES, ALONG_Z)  3.31 us
  transfers between devices with their start and end apart: 18, of which 7 were waited for; matrix products, arithmetic and copies ran while one was open for 1% of the time, Pallas kernels for 20%

profile of v4, /device:TPU:0, one launch (start us, length us, event | category | flops | bytes accessed | tf_op | source)
XLA Modules:
  0.0 160.0 jit_solution(2331301758698808451)
XLA Ops:
  1.3 3.1 %split.2 = (bf16[2,768,128]{2,1,0:T(8,128)(2,1)}, bf16[2,768,128]{2,1,0:T(8,128)(2,1)}, bf16[2,768,128]{2,1,0:T(8,128)(2,1)}, bf16[2,768,128]{2,1,0:T(8,128)(2,1)}) custom-call(s32[4]{0:T(128)} %pad_add_fusion.1.at, bf16[768,512]{1,0:T(8,128)(2,1)} %q.3, bf16[768,512]{1,0:T(8,128)(2,1)} %g.3, bf16[768,512]{1,0:T(8,128)(2,1)} %k.3, bf16[768,512]{1,0:T(8,128)(2,1)} %v.3), custom_call_target="tpu_custom_call" | custom-call | tf_op jit(solution)/shard_map/split/pallas_call | solution.py:422
  4.5 1.7 %collective-permute-start.1 = (bf16[2,768,128]{2,1,0:T(8,128)(2,1)}, bf16[2,768,128]{2,1,0:T(8,128)(2,1)S(1)}, u32[]{:S(2)}, u32[]{:S(2)}) collective-permute-start(bf16[2,768,128]{2,1,0:T(8,128)(2,1)} %get-tuple-element.25), channel_id=1, source_target_pairs={{0,4},{1,20},{2,6},{3,22},{4,8},{5,24},{6,10},{7,26},{8,12},{9,28}... | collective-permute-start | bytes 1179656 | tf_op jit(solution)/shard_map/ppermute | solution.py:432
  6.2 2.9 %collective-permute-start.2 = (bf16[2,768,128]{2,1,0:T(8,128)(2,1)}, bf16[2,768,128]{2,1,0:T(8,128)(2,1)S(1)}, u32[]{:S(2)}, u32[]{:S(2)}) collective-permute-start(bf16[2,768,128]{2,1,0:T(8,128)(2,1)} %get-tuple-element.26), channel_id=1, source_target_pairs={{0,8},{1,24},{2,10},{3,26},{4,12},{5,28},{6,14},{7,30},{8,0},{9,16... | collective-permute-start | bytes 1179656 | tf_op jit(solution)/shard_map/ppermute | solution.py:432
  10.5 1.6 %collective-permute-start = (bf16[2,768,128]{2,1,0:T(8,128)(2,1)}, bf16[2,768,128]{2,1,0:T(8,128)(2,1)S(1)}, u32[]{:S(2)}, u32[]{:S(2)}) collective-permute-start(bf16[2,768,128]{2,1,0:T(8,128)(2,1)} %get-tuple-element.24.refs_0_), channel_id=1, source_target_pairs={{0,0},{1,16},{2,2},{3,18},{4,4},{5,20},{6,6},{7,22},{8,8},{9,24},{... | collective-permute-start | bytes 1179656 | tf_op jit(solution)/shard_map/ppermute | solution.py:432
  13.0 1.9 %table.1.refs_1_.tab = s32[3,256]{1,0:T(4,128)} custom-call(s32[4]{0:T(128)} %pad_add_fusion.1.at, s32[96]{0:T(128)} %counts.1, s32[2,16,128]{2,1,0:T(8,128)} %pad.4.rows), custom_call_target="tpu_custom_call" | custom-call | tf_op jit(solution)/shard_map/table/pallas_call | solution.py:412
  14.9 3.0 %split.3 = (bf16[2,768,128]{2,1,0:T(8,128)(2,1)}, bf16[2,768,128]{2,1,0:T(8,128)(2,1)}, bf16[2,768,128]{2,1,0:T(8,128)(2,1)}, bf16[2,768,128]{2,1,0:T(8,128)(2,1)}) custom-call(s32[4]{0:T(128)} %pad_add_fusion.1.at, bf16[768,512]{1,0:T(8,128)(2,1)} %q.3, bf16[768,512]{1,0:T(8,128)(2,1)} %g.3, bf16[768,512]{1,0:T(8,128)(2,1)} %k.3, bf16[768,512]{1,0:T(8,128)(2,1)} %v.3, ...), custom_call_target="tpu_custom_call" | custom-call | tf_op jit(solution)/shard_map/split/pallas_call | solution.py:422
  18.7 3.5 %collective-permute-done.1 = bf16[2,768,128]{2,1,0:T(8,128)(2,1)S(1)} collective-permute-done((bf16[2,768,128]{2,1,0:T(8,128)(2,1)}, bf16[2,768,128]{2,1,0:T(8,128)(2,1)S(1)}, u32[]{:S(2)}, u32[]{:S(2)}) %collective-permute-start.1) | collective-permute-done | bytes 393248 | tf_op jit(solution)/shard_map/ppermute | solution.py:432
  22.2 6.3 %collective-permute-start.6 = (bf16[2,768,128]{2,1,0:T(8,128)(2,1)}, bf16[2,768,128]{2,1,0:T(8,128)(2,1)S(1)}, u32[]{:S(2)}, u32[]{:S(2)}) collective-permute-start(bf16[2,768,128]{2,1,0:T(8,128)(2,1)} %get-tuple-element.30), channel_id=1, source_target_pairs={{0,8},{1,24},{2,10},{3,26},{4,12},{5,28},{6,14},{7,30},{8,0},{9,16... | collective-permute-start | bytes 1179656 | tf_op jit(solution)/shard_map/ppermute | solution.py:432
  28.5 1.7 %collective-permute-start.4 = (bf16[2,768,128]{2,1,0:T(8,128)(2,1)}, bf16[2,768,128]{2,1,0:T(8,128)(2,1)S(1)}, u32[]{:S(2)}, u32[]{:S(2)}) collective-permute-start(bf16[2,768,128]{2,1,0:T(8,128)(2,1)} %get-tuple-element.28.refs_4_), channel_id=1, source_target_pairs={{0,0},{1,16},{2,2},{3,18},{4,4},{5,20},{6,6},{7,22},{8,8},{9,24},{... | collective-permute-start | bytes 1179656 | tf_op jit(solution)/shard_map/ppermute | solution.py:432
  30.9 2.2 %gather.1 = bf16[2,12,256,128]{3,2,1,0:T(8,128)(2,1)} custom-call(bf16[2,3,256,128]{3,2,1,0:T(8,128)(2,1)} %bitcast.30, bf16[2,3,256,128]{3,2,1,0:T(8,128)(2,1)} %bitcast.18, bf16[2,3,256,128]{3,2,1,0:T(8,128)(2,1)} %bitcast.22, bf16[2,3,256,128]{3,2,1,0:T(8,128)(2,1)} %bitcast.26, bf16[2,768,128]{2,1,0:T(8,128)(2,1)} %get-tuple-element.28.refs_4_), custom_call_target="tpu_custom_call" | custom-call | tf_op jit(solution)/shard_map/gather/pallas_call | solution.py:444
  34.4 5.4 %collective-permute-done.5 = bf16[2,768,128]{2,1,0:T(8,128)(2,1)S(1)} collective-permute-done((bf16[2,768,128]{2,1,0:T(8,128)(2,1)}, bf16[2,768,128]{2,1,0:T(8,128)(2,1)S(1)}, u32[]{:S(2)}, u32[]{:S(2)}) %collective-permute-start.5) | collective-permute-done | bytes 393248 | tf_op jit(solution)/shard_map/ppermute | solution.py:432
  39.8 4.8 %collective-permute-done.6 = bf16[2,768,128]{2,1,0:T(8,128)(2,1)S(1)} collective-permute-done((bf16[2,768,128]{2,1,0:T(8,128)(2,1)}, bf16[2,768,128]{2,1,0:T(8,128)(2,1)S(1)}, u32[]{:S(2)}, u32[]{:S(2)}) %collective-permute-start.6) | collective-permute-done | bytes 393248 | tf_op jit(solution)/shard_map/ppermute | solution.py:432
  45.6 3.0 %gather_keys.1 = (bf16[2,10,256,128]{3,2,1,0:T(8,128)(2,1)}, bf16[2,2,256,128]{3,2,1,0:T(8,128)(2,1)}) custom-call(s32[4]{0:T(128)} %pad_add_fusion.1.at, bf16[2,3,256,128]{3,2,1,0:T(8,128)(2,1)} %bitcast.31, bf16[2,3,256,128]{3,2,1,0:T(8,128)(2,1)} %bitcast.19, bf16[2,3,256,128]{3,2,1,0:T(8,128)(2,1)} %bitcast.23, bf16[2,3,256,128]{3,2,1,0:T(8,128)(2,1)} %bitcast.27, ...), custom_call_target="tpu_custom_call" | custom-call | tf_op jit(solution)/shard_map/gather_keys/pallas_call | solution.py:452
  49.2 3.1 %collective-permute-done.10.refs_10_ = bf16[2,2,256,128]{3,2,1,0:T(8,128)(2,1)S(1)} collective-permute-done((bf16[2,2,256,128]{3,2,1,0:T(8,128)(2,1)}, bf16[2,2,256,128]{3,2,1,0:T(8,128)(2,1)S(1)}, u32[]{:S(2)}, u32[]{:S(2)}) %collective-permute-start.10) | collective-permute-done | bytes 262176 | tf_op jit(solution)/shard_map/ppermute | solution.py:459
  52.3 3.3 %collective-permute-done.8.refs_8_ = bf16[2,12,256,128]{3,2,1,0:T(8,128)(2,1)S(1)} collective-permute-done((bf16[2,12,256,128]{3,2,1,0:T(8,128)(2,1)}, bf16[2,12,256,128]{3,2,1,0:T(8,128)(2,1)S(1)}, u32[]{:S(2)}, u32[]{:S(2)}) %collective-permute-start.8) | collective-permute-done | bytes 1572896 | tf_op jit(solution)/shard_map/ppermute | solution.py:451
  56.8 35.4 %far.1 = (bf16[12,256,128]{2,1,0:T(8,128)(2,1)}, bf16[12,256,128]{2,1,0:T(8,128)(2,1)}, bf16[12,256,128]{2,1,0:T(8,128)(2,1)}, bf16[2,12,256,128]{3,2,1,0:T(8,128)(2,1)}) custom-call(s32[4]{0:T(128)} %pad_add_fusion.1.at, s32[3,256]{1,0:T(4,128)} %table.1.refs_1_.tab, bf16[2,3,256,128]{3,2,1,0:T(8,128)(2,1)} %bitcast.32, bf16[2,3,256,128]{3,2,1,0:T(8,128)(2,1)} %bitcast.20, ...), custom_call_target="tpu_custom_call" | custom-call | flops 11660165120 | bytes 12582912 | tf_op jit(solution)/shard_map/far/pallas_call | solution.py:473
  94.3 21.1 %own.1 = (bf16[12,256,128]{2,1,0:T(8,128)(2,1)}, bf16[12,256,128]{2,1,0:T(8,128)(2,1)}, bf16[12,256,128]{2,1,0:T(8,128)(2,1)}) custom-call(s32[4]{0:T(128)} %pad_add_fusion.1.at, s32[3,256]{1,0:T(4,128)} %table.1.refs_1_.tab, bf16[2,3,256,128]{3,2,1,0:T(8,128)(2,1)} %bitcast.33, bf16[2,3,256,128]{3,2,1,0:T(8,128)(2,1)} %bitcast.21, ...), custom_call_target="tpu_custom_call" | custom-call | flops 5033164800 | bytes 12582912 | tf_op jit(solution)/shard_map/own/pallas_call | solution.py:485
  117.2 4.8 %sums.1 = (bf16[3,3,256,128]{3,2,1,0:T(8,128)(2,1)}, bf16[3,3,256,128]{3,2,1,0:T(8,128)(2,1)}, bf16[3,3,256,128]{3,2,1,0:T(8,128)(2,1)}, bf16[3,3,256,128]{3,2,1,0:T(8,128)(2,1)}) custom-call(s32[4]{0:T(128)} %pad_add_fusion.1.at, bf16[12,256,128]{2,1,0:T(8,128)(2,1)} %get-tuple-element.36.refs_0_, bf16[12,256,128]{2,1,0:T(8,128)(2,1)} %get-tuple-element.37.refs_1_, ...), custom_call_target="tpu_custom_call" | custom-call | tf_op jit(solution)/shard_map/sums/pallas_call | solution.py:494
  122.0 1.5 collective-permute-start.15
  123.5 1.7 %collective-permute-start.14 = (bf16[3,768,128]{2,1,0:T(8,128)(2,1)}, bf16[3,768,128]{2,1,0:T(8,128)(2,1)S(1)}, u32[]{:S(2)}, u32[]{:S(2)}) collective-permute-start(bf16[3,768,128]{2,1,0:T(8,128)(2,1)} %bitcast.50), channel_id=1, source_target_pairs={{0,0},{16,1},{2,2},{18,3},{4,4},{20,5},{6,6},{22,7},{8,8},{24,9},{... | collective-permute-start | bytes 1769480 | tf_op jit(solution)/shard_map/ppermute | solution.py:432
  125.2 2.6 %collective-permute-start.16 = (bf16[3,768,128]{2,1,0:T(8,128)(2,1)}, bf16[3,768,128]{2,1,0:T(8,128)(2,1)S(1)}, u32[]{:S(2)}, u32[]{:S(2)}) collective-permute-start(bf16[3,768,128]{2,1,0:T(8,128)(2,1)} %bitcast.49), channel_id=1, source_target_pairs={{8,0},{24,1},{10,2},{26,3},{12,4},{28,5},{14,6},{30,7},{0,8},{16,9... | collective-permute-start | bytes 1769480 | tf_op jit(solution)/shard_map/ppermute | solution.py:432
  127.8 9.9 %collective-permute-done.15.refs_1_ = bf16[3,768,128]{2,1,0:T(8,128)(2,1)S(1)} collective-permute-done((bf16[3,768,128]{2,1,0:T(8,128)(2,1)}, bf16[3,768,128]{2,1,0:T(8,128)(2,1)S(1)}, u32[]{:S(2)}, u32[]{:S(2)}) %collective-permute-start.15) | collective-permute-done | bytes 589856 | tf_op jit(solution)/shard_map/ppermute | solution.py:432
  137.8 17.9 %collective-permute-done.17.refs_3_ = bf16[3,768,128]{2,1,0:T(8,128)(2,1)S(1)} collective-permute-done((bf16[3,768,128]{2,1,0:T(8,128)(2,1)}, bf16[3,768,128]{2,1,0:T(8,128)(2,1)S(1)}, u32[]{:S(2)}, u32[]{:S(2)}) %collective-permute-start.17) | collective-permute-done | bytes 589856 | tf_op jit(solution)/shard_map/ppermute | solution.py:432
  156.6 3.3 %join.1 = (bf16[768,512]{1,0:T(8,128)(2,1)}, bf16[768,512]{1,0:T(8,128)(2,1)}, bf16[768,512]{1,0:T(8,128)(2,1)}) custom-call(s32[4]{0:T(128)} %pad_add_fusion.1.at, bf16[3,768,128]{2,1,0:T(8,128)(2,1)} %copy-done.8, bf16[3,768,128]{2,1,0:T(8,128)(2,1)} %copy-done.7, bf16[3,768,128]{2,1,0:T(8,128)(2,1)} %copy-done.9, bf16[3,768,128]{2,1,0:T(8,128)(2,1)} %copy-done.10), custom_call_target="tpu_custom_call" | custom-call | tf_op jit(solution)/shard_map/join/pallas_call | solution.py:504
  (65 shorter events, 13.1 us)
Async XLA Ops:
  1.3 10.8 %copy-start.15 = (s32[96,16]{0,1:T(8,128)S(1)}, s32[96,16]{0,1:T(8,128)}, u32[]{:S(2)}) copy-start(s32[96,16]{0,1:T(8,128)} %param.10) | copy-start | bytes 18436
  4.5 17.7 %collective-permute-start.1 = (bf16[2,768,128]{2,1,0:T(8,128)(2,1)}, bf16[2,768,128]{2,1,0:T(8,128)(2,1)S(1)}, u32[]{:S(2)}, u32[]{:S(2)}) collective-permute-start(bf16[2,768,128]{2,1,0:T(8,128)(2,1)} %get-tuple-element.25), channel_id=1, source_target_pairs={{0,4},{1,20},{2,6},{3,22},{4,8},{5,24},{6,10},{7,26},{8,12},{9,28}... | collective-permute-start | bytes 1179656 | tf_op jit(solution)/shard_map/ppermute | solution.py:432
  6.2 22.2 %collective-permute-start.2 = (bf16[2,768,128]{2,1,0:T(8,128)(2,1)}, bf16[2,768,128]{2,1,0:T(8,128)(2,1)S(1)}, u32[]{:S(2)}, u32[]{:S(2)}) collective-permute-start(bf16[2,768,128]{2,1,0:T(8,128)(2,1)} %get-tuple-element.26), channel_id=1, source_target_pairs={{0,8},{1,24},{2,10},{3,26},{4,12},{5,28},{6,14},{7,30},{8,0},{9,16... | collective-permute-start | bytes 1179656 | tf_op jit(solution)/shard_map/ppermute | solution.py:432
  9.1 19.4 %collective-permute-start.3 = (bf16[2,768,128]{2,1,0:T(8,128)(2,1)}, bf16[2,768,128]{2,1,0:T(8,128)(2,1)S(1)}, u32[]{:S(2)}, u32[]{:S(2)}) collective-permute-start(bf16[2,768,128]{2,1,0:T(8,128)(2,1)} %get-tuple-element.27), channel_id=1, source_target_pairs={{0,12},{1,28},{2,14},{3,30},{4,0},{5,16},{6,2},{7,18},{8,4},{9,20}... | collective-permute-start | bytes 1179656 | tf_op jit(solution)/shard_map/ppermute | solution.py:432
  10.5 19.7 %collective-permute-start = (bf16[2,768,128]{2,1,0:T(8,128)(2,1)}, bf16[2,768,128]{2,1,0:T(8,128)(2,1)S(1)}, u32[]{:S(2)}, u32[]{:S(2)}) collective-permute-start(bf16[2,768,128]{2,1,0:T(8,128)(2,1)} %get-tuple-element.24.refs_0_), channel_id=1, source_target_pairs={{0,0},{1,16},{2,2},{3,18},{4,4},{5,20},{6,6},{7,22},{8,8},{9,24},{... | collective-permute-start | bytes 1179656 | tf_op jit(solution)/shard_map/ppermute | solution.py:432
  17.9 21.9 %collective-permute-start.5 = (bf16[2,768,128]{2,1,0:T(8,128)(2,1)}, bf16[2,768,128]{2,1,0:T(8,128)(2,1)S(1)}, u32[]{:S(2)}, u32[]{:S(2)}) collective-permute-start(bf16[2,768,128]{2,1,0:T(8,128)(2,1)} %get-tuple-element.29), channel_id=1, source_target_pairs={{0,4},{1,20},{2,6},{3,22},{4,8},{5,24},{6,10},{7,26},{8,12},{9,28}... | collective-permute-start | bytes 1179656 | tf_op jit(solution)/shard_map/ppermute | solution.py:432
  22.2 8.0 %copy-start.1 = (bf16[2,768,128]{2,1,0:T(8,128)(2,1)}, bf16[2,768,128]{2,1,0:T(8,128)(2,1)S(1)}, u32[]{:S(2)}) copy-start(bf16[2,768,128]{2,1,0:T(8,128)(2,1)S(1)} %collective-permute-done.1) | copy-start | bytes 1179652
  22.2 22.4 %collective-permute-start.6 = (bf16[2,768,128]{2,1,0:T(8,128)(2,1)}, bf16[2,768,128]{2,1,0:T(8,128)(2,1)S(1)}, u32[]{:S(2)}, u32[]{:S(2)}) collective-permute-start(bf16[2,768,128]{2,1,0:T(8,128)(2,1)} %get-tuple-element.30), channel_id=1, source_target_pairs={{0,8},{1,24},{2,10},{3,26},{4,12},{5,28},{6,14},{7,30},{8,0},{9,16... | collective-permute-start | bytes 1179656 | tf_op jit(solution)/shard_map/ppermute | solution.py:432
  28.5 16.2 %collective-permute-start.7 = (bf16[2,768,128]{2,1,0:T(8,128)(2,1)}, bf16[2,768,128]{2,1,0:T(8,128)(2,1)S(1)}, u32[]{:S(2)}, u32[]{:S(2)}) collective-permute-start(bf16[2,768,128]{2,1,0:T(8,128)(2,1)} %get-tuple-element.31), channel_id=1, source_target_pairs={{0,12},{1,28},{2,14},{3,30},{4,0},{5,16},{6,2},{7,18},{8,4},{9,20}... | collective-permute-start | bytes 1179656 | tf_op jit(solution)/shard_map/ppermute | solution.py:432
  28.5 16.1 %collective-permute-start.4 = (bf16[2,768,128]{2,1,0:T(8,128)(2,1)}, bf16[2,768,128]{2,1,0:T(8,128)(2,1)S(1)}, u32[]{:S(2)}, u32[]{:S(2)}) collective-permute-start(bf16[2,768,128]{2,1,0:T(8,128)(2,1)} %get-tuple-element.28.refs_4_), channel_id=1, source_target_pairs={{0,0},{1,16},{2,2},{3,18},{4,4},{5,20},{6,6},{7,22},{8,8},{9,24},{... | collective-permute-start | bytes 1179656 | tf_op jit(solution)/shard_map/ppermute | solution.py:432
  33.1 22.5 %collective-permute-start.8 = (bf16[2,12,256,128]{3,2,1,0:T(8,128)(2,1)}, bf16[2,12,256,128]{3,2,1,0:T(8,128)(2,1)S(1)}, u32[]{:S(2)}, u32[]{:S(2)}) collective-permute-start(bf16[2,12,256,128]{3,2,1,0:T(8,128)(2,1)} %gather.1), channel_id=1, source_target_pairs={{1,33},{3,35},{5,37},{7,39},{9,41},{11,43},{13,45},{15,47},{17,49}... | collective-permute-start | bytes 4718600 | tf_op jit(solution)/shard_map/ppermute | solution.py:451
  39.8 4.8 %copy-start.11 = (bf16[2,768,128]{2,1,0:T(8,128)(2,1)}, bf16[2,768,128]{2,1,0:T(8,128)(2,1)S(1)}, u32[]{:S(2)}) copy-start(bf16[2,768,128]{2,1,0:T(8,128)(2,1)S(1)} %collective-permute-done.5) | copy-start | bytes 1179652
  48.6 3.7 %collective-permute-start.9 = (bf16[2,10,256,128]{3,2,1,0:T(8,128)(2,1)}, bf16[2,10,256,128]{3,2,1,0:T(8,128)(2,1)S(1)}, u32[]{:S(2)}, u32[]{:S(2)}) collective-permute-start(bf16[2,10,256,128]{3,2,1,0:T(8,128)(2,1)} %get-tuple-element.32), channel_id=1, source_target_pairs={{0,1},{1,0},{2,3},{3,2},{4,5},{5,4},{6,7},{7,6},{8,9},{9,8},{10,11... | collective-permute-start | bytes 3932168 | tf_op jit(solution)/shard_map/ppermute | solution.py:459
  48.7 3.6 %collective-permute-start.10 = (bf16[2,2,256,128]{3,2,1,0:T(8,128)(2,1)}, bf16[2,2,256,128]{3,2,1,0:T(8,128)(2,1)S(1)}, u32[]{:S(2)}, u32[]{:S(2)}) collective-permute-start(bf16[2,2,256,128]{3,2,1,0:T(8,128)(2,1)} %get-tuple-element.33), channel_id=1, source_target_pairs={{0,1},{1,0},{2,3},{3,2},{4,5},{5,4},{6,7},{7,6},{8,9},{9,8},{10,11... | collective-permute-start | bytes 786440 | tf_op jit(solution)/shard_map/ppermute | solution.py:459
  92.2 23.3 %collective-permute-start.11 = (bf16[2,12,256,128]{3,2,1,0:T(8,128)(2,1)}, bf16[2,12,256,128]{3,2,1,0:T(8,128)(2,1)S(1)}, u32[]{:S(2)}, u32[]{:S(2)}) collective-permute-start(bf16[2,12,256,128]{3,2,1,0:T(8,128)(2,1)} %get-tuple-element.39), channel_id=1, source_target_pairs={{0,1},{1,0},{2,3},{3,2},{4,5},{5,4},{6,7},{7,6},{8,9},{9,8},{10,11... | collective-permute-start | bytes 4718600 | tf_op jit(solution)/shard_map/ppermute | solution.py:484
  92.3 23.2 %collective-permute-start.12 = (bf16[12,256,128]{2,1,0:T(8,128)(2,1)}, bf16[12,256,128]{2,1,0:T(8,128)(2,1)S(1)}, u32[]{:S(2)}, u32[]{:S(2)}) collective-permute-start(bf16[12,256,128]{2,1,0:T(8,128)(2,1)} %get-tuple-element.40), channel_id=1, source_target_pairs={{33,1},{35,3},{37,5},{39,7},{41,9},{43,11},{45,13},{47,15},{49,17}... | collective-permute-start | bytes 2359304 | tf_op jit(solution)/shard_map/ppermute | solution.py:482
  93.6 21.9 %collective-permute-start.13 = (bf16[12,256,128]{2,1,0:T(8,128)(2,1)}, bf16[12,256,128]{2,1,0:T(8,128)(2,1)S(1)}, u32[]{:S(2)}, u32[]{:S(2)}) collective-permute-start(bf16[12,256,128]{2,1,0:T(8,128)(2,1)} %get-tuple-element.35.refs_9_), channel_id=1, source_target_pairs={{33,1},{35,3},{37,5},{39,7},{41,9},{43,11},{45,13},{47,15},{49,17}... | collective-permute-start | bytes 2359304 | tf_op jit(solution)/shard_map/ppermute | solution.py:483
  122.0 15.8 %collective-permute-start.15 = (bf16[3,768,128]{2,1,0:T(8,128)(2,1)}, bf16[3,768,128]{2,1,0:T(8,128)(2,1)S(1)}, u32[]{:S(2)}, u32[]{:S(2)}) collective-permute-start(bf16[3,768,128]{2,1,0:T(8,128)(2,1)} %bitcast.51), channel_id=1, source_target_pairs={{4,0},{20,1},{6,2},{22,3},{8,4},{24,5},{10,6},{26,7},{12,8},{28,9}... | collective-permute-start | bytes 1769480 | tf_op jit(solution)/shard_map/ppermute | solution.py:432
  123.5 14.3 %collective-permute-start.14 = (bf16[3,768,128]{2,1,0:T(8,128)(2,1)}, bf16[3,768,128]{2,1,0:T(8,128)(2,1)S(1)}, u32[]{:S(2)}, u32[]{:S(2)}) collective-permute-start(bf16[3,768,128]{2,1,0:T(8,128)(2,1)} %bitcast.50), channel_id=1, source_target_pairs={{0,0},{16,1},{2,2},{18,3},{4,4},{20,5},{6,6},{22,7},{8,8},{24,9},{... | collective-permute-start | bytes 1769480 | tf_op jit(solution)/shard_map/ppermute | solution.py:432
  125.2 12.6 %collective-permute-start.16 = (bf16[3,768,128]{2,1,0:T(8,128)(2,1)}, bf16[3,768,128]{2,1,0:T(8,128)(2,1)S(1)}, u32[]{:S(2)}, u32[]{:S(2)}) collective-permute-start(bf16[3,768,128]{2,1,0:T(8,128)(2,1)} %bitcast.49), channel_id=1, source_target_pairs={{8,0},{24,1},{10,2},{26,3},{12,4},{28,5},{14,6},{30,7},{0,8},{16,9... | collective-permute-start | bytes 1769480 | tf_op jit(solution)/shard_map/ppermute | solution.py:432
  127.8 27.9 %collective-permute-start.17 = (bf16[3,768,128]{2,1,0:T(8,128)(2,1)}, bf16[3,768,128]{2,1,0:T(8,128)(2,1)S(1)}, u32[]{:S(2)}, u32[]{:S(2)}) collective-permute-start(bf16[3,768,128]{2,1,0:T(8,128)(2,1)} %bitcast.48), channel_id=1, source_target_pairs={{12,0},{28,1},{14,2},{30,3},{0,4},{16,5},{2,6},{18,7},{4,8},{20,9}... | collective-permute-start | bytes 1769480 | tf_op jit(solution)/shard_map/ppermute | solution.py:432
  137.8 18.0 %copy-start.7 = (bf16[3,768,128]{2,1,0:T(8,128)(2,1)}, bf16[3,768,128]{2,1,0:T(8,128)(2,1)S(1)}, u32[]{:S(2)}) copy-start(bf16[3,768,128]{2,1,0:T(8,128)(2,1)S(1)} %collective-permute-done.15.refs_1_) | copy-start | bytes 1769476
  137.8 18.0 %copy-start.8 = (bf16[3,768,128]{2,1,0:T(8,128)(2,1)}, bf16[3,768,128]{2,1,0:T(8,128)(2,1)S(1)}, u32[]{:S(2)}) copy-start(bf16[3,768,128]{2,1,0:T(8,128)(2,1)S(1)} %collective-permute-done.14.refs_0_) | copy-start | bytes 1769476
  137.8 18.0 %copy-start.9 = (bf16[3,768,128]{2,1,0:T(8,128)(2,1)}, bf16[3,768,128]{2,1,0:T(8,128)(2,1)S(1)}, u32[]{:S(2)}) copy-start(bf16[3,768,128]{2,1,0:T(8,128)(2,1)S(1)} %collective-permute-done.16.refs_2_) | copy-start | bytes 1769476
  (13 other events, 19.0 us)

commit v5 on v4

--- a/solution.py
+++ b/solution.py
@@ -15,7 +15,7 @@
 U_SCALE = 0.5 / math.sqrt(HEAD)
 V_SCALE = 1.0 / math.sqrt(KPB * BLK)
 QK_SCALE = 0.5 * V_SCALE / math.sqrt(HEAD)
-GROUP = 6
+GROUP = (8, 6)
 CLASSES = (160, 192, 224, 256)
 SPOTS = 256
 MOST = 10
@@ -122,7 +122,9 @@
 def pair_grads(scores, weight_grad, allowed):
     u = scores * U_SCALE
     t = jnp.tanh(u)
-    p = jnp.where(allowed, 1.0 + t, 0.0)
+    p = 1.0 + t
+    if allowed is not None:
+        p = jnp.where(allowed, p, 0.0)
     w = u * p
     slope = p + w * (1.0 - t)
     return w.astype(BF), (weight_grad * slope).astype(BF)
@@ -139,7 +141,8 @@
         outs, refs = refs[:4], refs[4:]
         made, refs = refs[:5], refs[5:]
     qs, gs, ks, vs, dqa, dka, dva, sems = refs
-    core, groups = at[2], (tab[phase, SPOTS - 1] + GROUP - 1) // GROUP
+    core, size = at[2], GROUP[phase]
+    groups = (tab[phase, SPOTS - 1] + size - 1) // size
 
     def copies(own):
         qg, kv = ((r1, r2), (r2, r1))[own]
@@ -190,39 +193,59 @@
                 copy.wait()
 
     def work(items, rows):
-        made = []
-        for q, k, mask in items:
+        def scores(item):
+            q, k, mask = item
             key, value, query, grad = ks[k, :rows], vs[k, :rows], qs[q], gs[q]
-            made.append((q, k, mask, key, query, grad, nt(key, query), nt(value, grad)))
-        for q, k, mask, key, query, grad, scores, weight_grad in made:
-            w, sg = pair_grads(scores, weight_grad, mask)
+            return q, k, mask, key, query, grad, nt(key, query), nt(value, grad)
+
+        def grads(q, k, mask, key, query, grad, score, weight_grad):
+            made = [
+                pair_grads(score[lo:hi], weight_grad[lo:hi], mask(lo, hi))
+                for lo, hi in ((0, 128), (128, rows))
+            ]
+            w, sg = (jnp.concatenate(parts) for parts in zip(*made))
             dva[k, :rows] += nn(w, grad)
             dka[k, :rows] += nn(sg, query)
             dqa[q] += tn(key, sg)
 
+        ahead = scores(items[0])
+        for item in (*items[1:], None):
+            now, ahead = ahead, None if item is None else scores(item)
+            grads(*now)
+
     def own_group(g, _):
-        items = []
-        row = lax.broadcasted_iota(jnp.int32, (BLK, BLK), 0)
-        col = lax.broadcasted_iota(jnp.int32, (BLK, BLK), 1)
-        for i in range(4):
-            slot = g * 4 + i
-            items.append((slot, slot, (row == col) | ((row < col) & (row < tab[2, slot]))))
-        work(items, BLK)
+        def mask_of(slot):
+            def mask(lo, hi):
+                row = lo + lax.broadcasted_iota(jnp.int32, (hi - lo, BLK), 0)
+                col = lax.broadcasted_iota(jnp.int32, (hi - lo, BLK), 1)
+                return (row == col) | ((row < col) & (row < tab[2, slot]))
+
+            return mask
+
+        slots = [g * 6 + i for i in range(6)]
+        work([(slot, slot, mask_of(slot)) for slot in slots], BLK)
         return 0
 
     if phase:
-        lax.fori_loop(0, 3, own_group, 0)
+        lax.fori_loop(0, 2, own_group, 0)
+
+    def mask_from(kept):
+        def mask(lo, hi):
+            if lo == 0:
+                return None
+            return lo + lax.broadcasted_iota(jnp.int32, (hi - lo, BLK), 0) < kept
+
+        return mask
 
     def group(g, _):
         for c, rows in enumerate(CLASSES):
 
-            @pl.when((tab[phase, g * GROUP + GROUP - 1] >> 18) == c)
+            @pl.when((tab[phase, g * size + size - 1] >> 18) == c)
             def _(rows=rows):
-                row = lax.broadcasted_iota(jnp.int32, (rows, BLK), 0)
                 items = []
-                for i in range(GROUP):
-                    e = tab[phase, g * GROUP + i]
-                    items.append((e & 15, (e >> 4) & 31, row < ((e >> 9) & 511)))
+                for i in range(size):
+                    e = tab[phase, g * size + i]
+                    items.append((e & 15, (e >> 4) & 31, mask_from((e >> 9) & 511)))
                 work(items, rows)
 
         return 0
@@ -476,6 +499,7 @@
         [SMEM] * 2 + [ANY] * 11,
         parts + scratch(PLANE) + [dma(44)],
         cost=pairs_cost(139),
+        limit=56,
         name="far",
     )(at, tab, *r1, *r2, across, *near)
     s2 = p2
@@ -488,6 +512,7 @@
         [SMEM] * 2 + [ANY] * 10,
         parts + scratch(HALF) + [dma(44)],
         cost=pairs_cost(60),
+        limit=56,
         name="own",
     )(at, tab, *r1, *r2, s1, s2)
     v3, v4 = pltpu.VMEM((HALF, BLK, HEAD), BF), pltpu.VMEM((2, HALF, BLK, HEAD), BF)
@@ -496,6 +521,7 @@
         [shape((3, 3, BLK, HEAD), BF)] * 4,
         [SMEM] + [ANY] * 6,
         [v3, v3, v3, v4, v3, v3, pltpu.VMEM((4, 3, 3, BLK, HEAD), BF), dma(4, 6), dma(4)],
+        limit=56,
         name="sums",
     )(at, dq, dk, dv, beside, p1, p2)
     back = send([p.reshape(3, rows, HEAD) for p in sums], from_heads)

time: 162 us -> 157 us (0.969)
  Pallas kernels: 77.9 us -> 70.2 us
  starting transfers between devices: 26.2 us -> 28.4 us
    pallas_call x1, Pallas kernels: 35.4 us -> 29.4 us  [body(): call(functools.partial(pairs_kernel, 0), [half, half, half, two], [SMEM]...]
    ppermute x1, starting transfers between devices: 1.34 us -> 3.35 us  [body(): p1 = lax.ppermute(p1, AXES, BACK_Z)]
    pallas_call x1, Pallas kernels: 21.1 us -> 19.3 us  [body(): call(functools.partial(pairs_kernel, 1), [half, half, half], [SMEM] * 2 +...]
  transfers between devices with their start and end apart: 18 -> 18, of which waited for: 7 -> 7; matrix products, arithmetic and copies ran while one was open for 1% -> 1% of each run, Pallas kernels for 20% -> 19%
where the time goes in v5:
time: 157 us; the launch traced here: 155 us
  Pallas kernels  70.2 us (45%)
  waiting for transfers between devices  48.1 us (31%)
  starting transfers between devices  28.4 us (18%)
  local copies, waits for them, and re-layouts  6.24 us (4%)
    ppermute x12, waiting for transfers between devices, send(): return [lax.ppermute(p, AXES, pairs(d)) for d, p in enumerate(pieces)]  41.6 us
    pallas_call x1, Pallas kernels, body(): call(functools.partial(pairs_kernel, 0), [half, half, half, two], [SMEM]...  29.4 us
    ppermute x12, starting transfers between devices, send(): return [lax.ppermute(p, AXES, pairs(d)) for d, p in enumerate(pieces)]  22.2 us
    pallas_call x1, Pallas kernels, body(): call(functools.partial(pairs_kernel, 1), [half, half, half], [SMEM] * 2 +...  19.3 us
    pallas_call x2, Pallas kernels, split(): call(functools.partial(split_kernel, first_round), [shape((2, rows, HEAD)...  6.16 us
    unnamed x38, local copies, waits for them, and re-layouts  5.39 us
    pallas_call x1, Pallas kernels, body(): call(sum_kernel, [shape((3, 3, BLK, HEAD), BF)] * 4, [SMEM] + [ANY] * 6,...  4.81 us
    ppermute x1, starting transfers between devices, body(): p1 = lax.ppermute(p1, AXES, BACK_Z)  3.35 us
  transfers between devices with their start and end apart: 18, of which 7 were waited for; matrix products, arithmetic and copies ran while one was open for 1% of the time, Pallas kernels for 19%

profile of v5, /device:TPU:0, one launch (start us, length us, event | category | flops | bytes accessed | tf_op | source)
XLA Modules:
  0.0 154.6 jit_solution(4689232107632136239)
XLA Ops:
  1.3 3.1 %split.2 = (bf16[2,768,128]{2,1,0:T(8,128)(2,1)}, bf16[2,768,128]{2,1,0:T(8,128)(2,1)}, bf16[2,768,128]{2,1,0:T(8,128)(2,1)}, bf16[2,768,128]{2,1,0:T(8,128)(2,1)}) custom-call(s32[4]{0:T(128)} %pad_add_fusion.1.at, bf16[768,512]{1,0:T(8,128)(2,1)} %q.3, bf16[768,512]{1,0:T(8,128)(2,1)} %g.3, bf16[768,512]{1,0:T(8,128)(2,1)} %k.3, bf16[768,512]{1,0:T(8,128)(2,1)} %v.3), custom_call_target="tpu_custom_call" | custom-call | tf_op jit(solution)/shard_map/split/pallas_call | solution.py:445
  4.5 1.7 %collective-permute-start.1 = (bf16[2,768,128]{2,1,0:T(8,128)(2,1)}, bf16[2,768,128]{2,1,0:T(8,128)(2,1)S(1)}, u32[]{:S(2)}, u32[]{:S(2)}) collective-permute-start(bf16[2,768,128]{2,1,0:T(8,128)(2,1)} %get-tuple-element.25), channel_id=1, source_target_pairs={{0,4},{1,20},{2,6},{3,22},{4,8},{5,24},{6,10},{7,26},{8,12},{9,28}... | collective-permute-start | bytes 1179656 | tf_op jit(solution)/shard_map/ppermute | solution.py:455
  6.2 2.9 %collective-permute-start.2 = (bf16[2,768,128]{2,1,0:T(8,128)(2,1)}, bf16[2,768,128]{2,1,0:T(8,128)(2,1)S(1)}, u32[]{:S(2)}, u32[]{:S(2)}) collective-permute-start(bf16[2,768,128]{2,1,0:T(8,128)(2,1)} %get-tuple-element.26), channel_id=1, source_target_pairs={{0,8},{1,24},{2,10},{3,26},{4,12},{5,28},{6,14},{7,30},{8,0},{9,16... | collective-permute-start | bytes 1179656 | tf_op jit(solution)/shard_map/ppermute | solution.py:455
  10.5 1.6 %collective-permute-start = (bf16[2,768,128]{2,1,0:T(8,128)(2,1)}, bf16[2,768,128]{2,1,0:T(8,128)(2,1)S(1)}, u32[]{:S(2)}, u32[]{:S(2)}) collective-permute-start(bf16[2,768,128]{2,1,0:T(8,128)(2,1)} %get-tuple-element.24.refs_0_), channel_id=1, source_target_pairs={{0,0},{1,16},{2,2},{3,18},{4,4},{5,20},{6,6},{7,22},{8,8},{9,24},{... | collective-permute-start | bytes 1179656 | tf_op jit(solution)/shard_map/ppermute | solution.py:455
  13.0 1.9 %table.1.refs_1_.tab = s32[3,256]{1,0:T(4,128)} custom-call(s32[4]{0:T(128)} %pad_add_fusion.1.at, s32[96]{0:T(128)} %counts.1, s32[2,16,128]{2,1,0:T(8,128)} %pad.4.rows), custom_call_target="tpu_custom_call" | custom-call | tf_op jit(solution)/shard_map/table/pallas_call | solution.py:435
  14.9 3.0 %split.3 = (bf16[2,768,128]{2,1,0:T(8,128)(2,1)}, bf16[2,768,128]{2,1,0:T(8,128)(2,1)}, bf16[2,768,128]{2,1,0:T(8,128)(2,1)}, bf16[2,768,128]{2,1,0:T(8,128)(2,1)}) custom-call(s32[4]{0:T(128)} %pad_add_fusion.1.at, bf16[768,512]{1,0:T(8,128)(2,1)} %q.3, bf16[768,512]{1,0:T(8,128)(2,1)} %g.3, bf16[768,512]{1,0:T(8,128)(2,1)} %k.3, bf16[768,512]{1,0:T(8,128)(2,1)} %v.3, ...), custom_call_target="tpu_custom_call" | custom-call | tf_op jit(solution)/shard_map/split/pallas_call | solution.py:445
  18.7 3.5 %collective-permute-done.1 = bf16[2,768,128]{2,1,0:T(8,128)(2,1)S(1)} collective-permute-done((bf16[2,768,128]{2,1,0:T(8,128)(2,1)}, bf16[2,768,128]{2,1,0:T(8,128)(2,1)S(1)}, u32[]{:S(2)}, u32[]{:S(2)}) %collective-permute-start.1) | collective-permute-done | bytes 393248 | tf_op jit(solution)/shard_map/ppermute | solution.py:455
  22.2 6.3 %collective-permute-start.6 = (bf16[2,768,128]{2,1,0:T(8,128)(2,1)}, bf16[2,768,128]{2,1,0:T(8,128)(2,1)S(1)}, u32[]{:S(2)}, u32[]{:S(2)}) collective-permute-start(bf16[2,768,128]{2,1,0:T(8,128)(2,1)} %get-tuple-element.30), channel_id=1, source_target_pairs={{0,8},{1,24},{2,10},{3,26},{4,12},{5,28},{6,14},{7,30},{8,0},{9,16... | collective-permute-start | bytes 1179656 | tf_op jit(solution)/shard_map/ppermute | solution.py:455
  28.5 1.7 %collective-permute-start.4 = (bf16[2,768,128]{2,1,0:T(8,128)(2,1)}, bf16[2,768,128]{2,1,0:T(8,128)(2,1)S(1)}, u32[]{:S(2)}, u32[]{:S(2)}) collective-permute-start(bf16[2,768,128]{2,1,0:T(8,128)(2,1)} %get-tuple-element.28.refs_4_), channel_id=1, source_target_pairs={{0,0},{1,16},{2,2},{3,18},{4,4},{5,20},{6,6},{7,22},{8,8},{9,24},{... | collective-permute-start | bytes 1179656 | tf_op jit(solution)/shard_map/ppermute | solution.py:455
  30.9 2.2 %gather.1 = bf16[2,12,256,128]{3,2,1,0:T(8,128)(2,1)} custom-call(bf16[2,3,256,128]{3,2,1,0:T(8,128)(2,1)} %bitcast.30, bf16[2,3,256,128]{3,2,1,0:T(8,128)(2,1)} %bitcast.18, bf16[2,3,256,128]{3,2,1,0:T(8,128)(2,1)} %bitcast.22, bf16[2,3,256,128]{3,2,1,0:T(8,128)(2,1)} %bitcast.26, bf16[2,768,128]{2,1,0:T(8,128)(2,1)} %get-tuple-element.28.refs_4_), custom_call_target="tpu_custom_call" | custom-call | tf_op jit(solution)/shard_map/gather/pallas_call | solution.py:467
  34.4 5.4 %collective-permute-done.5 = bf16[2,768,128]{2,1,0:T(8,128)(2,1)S(1)} collective-permute-done((bf16[2,768,128]{2,1,0:T(8,128)(2,1)}, bf16[2,768,128]{2,1,0:T(8,128)(2,1)S(1)}, u32[]{:S(2)}, u32[]{:S(2)}) %collective-permute-start.5) | collective-permute-done | bytes 393248 | tf_op jit(solution)/shard_map/ppermute | solution.py:455
  39.8 4.8 %collective-permute-done.6 = bf16[2,768,128]{2,1,0:T(8,128)(2,1)S(1)} collective-permute-done((bf16[2,768,128]{2,1,0:T(8,128)(2,1)}, bf16[2,768,128]{2,1,0:T(8,128)(2,1)S(1)}, u32[]{:S(2)}, u32[]{:S(2)}) %collective-permute-start.6) | collective-permute-done | bytes 393248 | tf_op jit(solution)/shard_map/ppermute | solution.py:455
  45.6 3.0 %gather_keys.1 = (bf16[2,10,256,128]{3,2,1,0:T(8,128)(2,1)}, bf16[2,2,256,128]{3,2,1,0:T(8,128)(2,1)}) custom-call(s32[4]{0:T(128)} %pad_add_fusion.1.at, bf16[2,3,256,128]{3,2,1,0:T(8,128)(2,1)} %bitcast.31, bf16[2,3,256,128]{3,2,1,0:T(8,128)(2,1)} %bitcast.19, bf16[2,3,256,128]{3,2,1,0:T(8,128)(2,1)} %bitcast.23, bf16[2,3,256,128]{3,2,1,0:T(8,128)(2,1)} %bitcast.27, ...), custom_call_target="tpu_custom_call" | custom-call | tf_op jit(solution)/shard_map/gather_keys/pallas_call | solution.py:475
  49.2 3.1 %collective-permute-done.10.refs_10_ = bf16[2,2,256,128]{3,2,1,0:T(8,128)(2,1)S(1)} collective-permute-done((bf16[2,2,256,128]{3,2,1,0:T(8,128)(2,1)}, bf16[2,2,256,128]{3,2,1,0:T(8,128)(2,1)S(1)}, u32[]{:S(2)}, u32[]{:S(2)}) %collective-permute-start.10) | collective-permute-done | bytes 262176 | tf_op jit(solution)/shard_map/ppermute | solution.py:482
  52.3 3.3 %collective-permute-done.8.refs_8_ = bf16[2,12,256,128]{3,2,1,0:T(8,128)(2,1)S(1)} collective-permute-done((bf16[2,12,256,128]{3,2,1,0:T(8,128)(2,1)}, bf16[2,12,256,128]{3,2,1,0:T(8,128)(2,1)S(1)}, u32[]{:S(2)}, u32[]{:S(2)}) %collective-permute-start.8) | collective-permute-done | bytes 1572896 | tf_op jit(solution)/shard_map/ppermute | solution.py:474
  56.8 29.4 %far.1 = (bf16[12,256,128]{2,1,0:T(8,128)(2,1)}, bf16[12,256,128]{2,1,0:T(8,128)(2,1)}, bf16[12,256,128]{2,1,0:T(8,128)(2,1)}, bf16[2,12,256,128]{3,2,1,0:T(8,128)(2,1)}) custom-call(s32[4]{0:T(128)} %pad_add_fusion.1.at, s32[3,256]{1,0:T(4,128)} %table.1.refs_1_.tab, bf16[2,3,256,128]{3,2,1,0:T(8,128)(2,1)} %bitcast.32, bf16[2,3,256,128]{3,2,1,0:T(8,128)(2,1)} %bitcast.20, ...), custom_call_target="tpu_custom_call" | custom-call | flops 11660165120 | bytes 12582912 | tf_op jit(solution)/shard_map/far/pallas_call | solution.py:496
  86.4 3.4 %collective-permute-start.12 = (bf16[12,256,128]{2,1,0:T(8,128)(2,1)}, bf16[12,256,128]{2,1,0:T(8,128)(2,1)S(1)}, u32[]{:S(2)}, u32[]{:S(2)}) collective-permute-start(bf16[12,256,128]{2,1,0:T(8,128)(2,1)} %get-tuple-element.40), channel_id=1, source_target_pairs={{33,1},{35,3},{37,5},{39,7},{41,9},{43,11},{45,13},{47,15},{49,17}... | collective-permute-start | bytes 2359304 | tf_op jit(solution)/shard_map/ppermute | solution.py:506
  90.6 19.3 %own.1 = (bf16[12,256,128]{2,1,0:T(8,128)(2,1)}, bf16[12,256,128]{2,1,0:T(8,128)(2,1)}, bf16[12,256,128]{2,1,0:T(8,128)(2,1)}) custom-call(s32[4]{0:T(128)} %pad_add_fusion.1.at, s32[3,256]{1,0:T(4,128)} %table.1.refs_1_.tab, bf16[2,3,256,128]{3,2,1,0:T(8,128)(2,1)} %bitcast.33, bf16[2,3,256,128]{3,2,1,0:T(8,128)(2,1)} %bitcast.21, ...), custom_call_target="tpu_custom_call" | custom-call | flops 5033164800 | bytes 12582912 | tf_op jit(solution)/shard_map/own/pallas_call | solution.py:509
  111.7 4.8 %sums.1 = (bf16[3,3,256,128]{3,2,1,0:T(8,128)(2,1)}, bf16[3,3,256,128]{3,2,1,0:T(8,128)(2,1)}, bf16[3,3,256,128]{3,2,1,0:T(8,128)(2,1)}, bf16[3,3,256,128]{3,2,1,0:T(8,128)(2,1)}) custom-call(s32[4]{0:T(128)} %pad_add_fusion.1.at, bf16[12,256,128]{2,1,0:T(8,128)(2,1)} %get-tuple-element.36.refs_0_, bf16[12,256,128]{2,1,0:T(8,128)(2,1)} %get-tuple-element.37.refs_1_, ...), custom_call_target="tpu_custom_call" | custom-call | tf_op jit(solution)/shard_map/sums/pallas_call | solution.py:519
  118.0 1.7 %collective-permute-start.14 = (bf16[3,768,128]{2,1,0:T(8,128)(2,1)}, bf16[3,768,128]{2,1,0:T(8,128)(2,1)S(1)}, u32[]{:S(2)}, u32[]{:S(2)}) collective-permute-start(bf16[3,768,128]{2,1,0:T(8,128)(2,1)} %bitcast.50), channel_id=1, source_target_pairs={{0,0},{16,1},{2,2},{18,3},{4,4},{20,5},{6,6},{22,7},{8,8},{24,9},{... | collective-permute-start | bytes 1769480 | tf_op jit(solution)/shard_map/ppermute | solution.py:455
  119.8 2.6 %collective-permute-start.16 = (bf16[3,768,128]{2,1,0:T(8,128)(2,1)}, bf16[3,768,128]{2,1,0:T(8,128)(2,1)S(1)}, u32[]{:S(2)}, u32[]{:S(2)}) collective-permute-start(bf16[3,768,128]{2,1,0:T(8,128)(2,1)} %bitcast.49), channel_id=1, source_target_pairs={{8,0},{24,1},{10,2},{26,3},{12,4},{28,5},{14,6},{30,7},{0,8},{16,9... | collective-permute-start | bytes 1769480 | tf_op jit(solution)/shard_map/ppermute | solution.py:455
  122.3 9.1 %collective-permute-done.15.refs_1_ = bf16[3,768,128]{2,1,0:T(8,128)(2,1)S(1)} collective-permute-done((bf16[3,768,128]{2,1,0:T(8,128)(2,1)}, bf16[3,768,128]{2,1,0:T(8,128)(2,1)S(1)}, u32[]{:S(2)}, u32[]{:S(2)}) %collective-permute-start.15) | collective-permute-done | bytes 589856 | tf_op jit(solution)/shard_map/ppermute | solution.py:455
  131.5 18.8 %collective-permute-done.17.refs_3_ = bf16[3,768,128]{2,1,0:T(8,128)(2,1)S(1)} collective-permute-done((bf16[3,768,128]{2,1,0:T(8,128)(2,1)}, bf16[3,768,128]{2,1,0:T(8,128)(2,1)S(1)}, u32[]{:S(2)}, u32[]{:S(2)}) %collective-permute-start.17) | collective-permute-done | bytes 589856 | tf_op jit(solution)/shard_map/ppermute | solution.py:455
  151.1 3.3 %join.1 = (bf16[768,512]{1,0:T(8,128)(2,1)}, bf16[768,512]{1,0:T(8,128)(2,1)}, bf16[768,512]{1,0:T(8,128)(2,1)}) custom-call(s32[4]{0:T(128)} %pad_add_fusion.1.at, bf16[3,768,128]{2,1,0:T(8,128)(2,1)} %copy-done.8, bf16[3,768,128]{2,1,0:T(8,128)(2,1)} %copy-done.7, bf16[3,768,128]{2,1,0:T(8,128)(2,1)} %copy-done.9, bf16[3,768,128]{2,1,0:T(8,128)(2,1)} %copy-done.10), custom_call_target="tpu_custom_call" | custom-call | tf_op jit(solution)/shard_map/join/pallas_call | solution.py:530
  (65 shorter events, 13.5 us)
Async XLA Ops:
  1.3 10.8 %copy-start.15 = (s32[96,16]{0,1:T(8,128)S(1)}, s32[96,16]{0,1:T(8,128)}, u32[]{:S(2)}) copy-start(s32[96,16]{0,1:T(8,128)} %param.10) | copy-start | bytes 18436
  4.5 17.7 %collective-permute-start.1 = (bf16[2,768,128]{2,1,0:T(8,128)(2,1)}, bf16[2,768,128]{2,1,0:T(8,128)(2,1)S(1)}, u32[]{:S(2)}, u32[]{:S(2)}) collective-permute-start(bf16[2,768,128]{2,1,0:T(8,128)(2,1)} %get-tuple-element.25), channel_id=1, source_target_pairs={{0,4},{1,20},{2,6},{3,22},{4,8},{5,24},{6,10},{7,26},{8,12},{9,28}... | collective-permute-start | bytes 1179656 | tf_op jit(solution)/shard_map/ppermute | solution.py:455
  6.2 22.2 %collective-permute-start.2 = (bf16[2,768,128]{2,1,0:T(8,128)(2,1)}, bf16[2,768,128]{2,1,0:T(8,128)(2,1)S(1)}, u32[]{:S(2)}, u32[]{:S(2)}) collective-permute-start(bf16[2,768,128]{2,1,0:T(8,128)(2,1)} %get-tuple-element.26), channel_id=1, source_target_pairs={{0,8},{1,24},{2,10},{3,26},{4,12},{5,28},{6,14},{7,30},{8,0},{9,16... | collective-permute-start | bytes 1179656 | tf_op jit(solution)/shard_map/ppermute | solution.py:455
  9.1 19.4 %collective-permute-start.3 = (bf16[2,768,128]{2,1,0:T(8,128)(2,1)}, bf16[2,768,128]{2,1,0:T(8,128)(2,1)S(1)}, u32[]{:S(2)}, u32[]{:S(2)}) collective-permute-start(bf16[2,768,128]{2,1,0:T(8,128)(2,1)} %get-tuple-element.27), channel_id=1, source_target_pairs={{0,12},{1,28},{2,14},{3,30},{4,0},{5,16},{6,2},{7,18},{8,4},{9,20}... | collective-permute-start | bytes 1179656 | tf_op jit(solution)/shard_map/ppermute | solution.py:455
  10.5 19.7 %collective-permute-start = (bf16[2,768,128]{2,1,0:T(8,128)(2,1)}, bf16[2,768,128]{2,1,0:T(8,128)(2,1)S(1)}, u32[]{:S(2)}, u32[]{:S(2)}) collective-permute-start(bf16[2,768,128]{2,1,0:T(8,128)(2,1)} %get-tuple-element.24.refs_0_), channel_id=1, source_target_pairs={{0,0},{1,16},{2,2},{3,18},{4,4},{5,20},{6,6},{7,22},{8,8},{9,24},{... | collective-permute-start | bytes 1179656 | tf_op jit(solution)/shard_map/ppermute | solution.py:455
  17.9 21.9 %collective-permute-start.5 = (bf16[2,768,128]{2,1,0:T(8,128)(2,1)}, bf16[2,768,128]{2,1,0:T(8,128)(2,1)S(1)}, u32[]{:S(2)}, u32[]{:S(2)}) collective-permute-start(bf16[2,768,128]{2,1,0:T(8,128)(2,1)} %get-tuple-element.29), channel_id=1, source_target_pairs={{0,4},{1,20},{2,6},{3,22},{4,8},{5,24},{6,10},{7,26},{8,12},{9,28}... | collective-permute-start | bytes 1179656 | tf_op jit(solution)/shard_map/ppermute | solution.py:455
  22.2 8.0 %copy-start.1 = (bf16[2,768,128]{2,1,0:T(8,128)(2,1)}, bf16[2,768,128]{2,1,0:T(8,128)(2,1)S(1)}, u32[]{:S(2)}) copy-start(bf16[2,768,128]{2,1,0:T(8,128)(2,1)S(1)} %collective-permute-done.1) | copy-start | bytes 1179652
  22.2 22.4 %collective-permute-start.6 = (bf16[2,768,128]{2,1,0:T(8,128)(2,1)}, bf16[2,768,128]{2,1,0:T(8,128)(2,1)S(1)}, u32[]{:S(2)}, u32[]{:S(2)}) collective-permute-start(bf16[2,768,128]{2,1,0:T(8,128)(2,1)} %get-tuple-element.30), channel_id=1, source_target_pairs={{0,8},{1,24},{2,10},{3,26},{4,12},{5,28},{6,14},{7,30},{8,0},{9,16... | collective-permute-start | bytes 1179656 | tf_op jit(solution)/shard_map/ppermute | solution.py:455
  28.5 16.2 %collective-permute-start.7 = (bf16[2,768,128]{2,1,0:T(8,128)(2,1)}, bf16[2,768,128]{2,1,0:T(8,128)(2,1)S(1)}, u32[]{:S(2)}, u32[]{:S(2)}) collective-permute-start(bf16[2,768,128]{2,1,0:T(8,128)(2,1)} %get-tuple-element.31), channel_id=1, source_target_pairs={{0,12},{1,28},{2,14},{3,30},{4,0},{5,16},{6,2},{7,18},{8,4},{9,20}... | collective-permute-start | bytes 1179656 | tf_op jit(solution)/shard_map/ppermute | solution.py:455
  28.5 16.1 %collective-permute-start.4 = (bf16[2,768,128]{2,1,0:T(8,128)(2,1)}, bf16[2,768,128]{2,1,0:T(8,128)(2,1)S(1)}, u32[]{:S(2)}, u32[]{:S(2)}) collective-permute-start(bf16[2,768,128]{2,1,0:T(8,128)(2,1)} %get-tuple-element.28.refs_4_), channel_id=1, source_target_pairs={{0,0},{1,16},{2,2},{3,18},{4,4},{5,20},{6,6},{7,22},{8,8},{9,24},{... | collective-permute-start | bytes 1179656 | tf_op jit(solution)/shard_map/ppermute | solution.py:455
  33.1 22.5 %collective-permute-start.8 = (bf16[2,12,256,128]{3,2,1,0:T(8,128)(2,1)}, bf16[2,12,256,128]{3,2,1,0:T(8,128)(2,1)S(1)}, u32[]{:S(2)}, u32[]{:S(2)}) collective-permute-start(bf16[2,12,256,128]{3,2,1,0:T(8,128)(2,1)} %gather.1), channel_id=1, source_target_pairs={{1,33},{3,35},{5,37},{7,39},{9,41},{11,43},{13,45},{15,47},{17,49}... | collective-permute-start | bytes 4718600 | tf_op jit(solution)/shard_map/ppermute | solution.py:474
  39.8 4.8 %copy-start.11 = (bf16[2,768,128]{2,1,0:T(8,128)(2,1)}, bf16[2,768,128]{2,1,0:T(8,128)(2,1)S(1)}, u32[]{:S(2)}) copy-start(bf16[2,768,128]{2,1,0:T(8,128)(2,1)S(1)} %collective-permute-done.5) | copy-start | bytes 1179652
  48.6 3.7 %collective-permute-start.9 = (bf16[2,10,256,128]{3,2,1,0:T(8,128)(2,1)}, bf16[2,10,256,128]{3,2,1,0:T(8,128)(2,1)S(1)}, u32[]{:S(2)}, u32[]{:S(2)}) collective-permute-start(bf16[2,10,256,128]{3,2,1,0:T(8,128)(2,1)} %get-tuple-element.32), channel_id=1, source_target_pairs={{0,1},{1,0},{2,3},{3,2},{4,5},{5,4},{6,7},{7,6},{8,9},{9,8},{10,11... | collective-permute-start | bytes 3932168 | tf_op jit(solution)/shard_map/ppermute | solution.py:482
  48.7 3.6 %collective-permute-start.10 = (bf16[2,2,256,128]{3,2,1,0:T(8,128)(2,1)}, bf16[2,2,256,128]{3,2,1,0:T(8,128)(2,1)S(1)}, u32[]{:S(2)}, u32[]{:S(2)}) collective-permute-start(bf16[2,2,256,128]{3,2,1,0:T(8,128)(2,1)} %get-tuple-element.33), channel_id=1, source_target_pairs={{0,1},{1,0},{2,3},{3,2},{4,5},{5,4},{6,7},{7,6},{8,9},{9,8},{10,11... | collective-permute-start | bytes 786440 | tf_op jit(solution)/shard_map/ppermute | solution.py:482
  86.3 23.7 %collective-permute-start.11 = (bf16[2,12,256,128]{3,2,1,0:T(8,128)(2,1)}, bf16[2,12,256,128]{3,2,1,0:T(8,128)(2,1)S(1)}, u32[]{:S(2)}, u32[]{:S(2)}) collective-permute-start(bf16[2,12,256,128]{3,2,1,0:T(8,128)(2,1)} %get-tuple-element.39), channel_id=1, source_target_pairs={{0,1},{1,0},{2,3},{3,2},{4,5},{5,4},{6,7},{7,6},{8,9},{9,8},{10,11... | collective-permute-start | bytes 4718600 | tf_op jit(solution)/shard_map/ppermute | solution.py:508
  86.4 23.6 %collective-permute-start.12 = (bf16[12,256,128]{2,1,0:T(8,128)(2,1)}, bf16[12,256,128]{2,1,0:T(8,128)(2,1)S(1)}, u32[]{:S(2)}, u32[]{:S(2)}) collective-permute-start(bf16[12,256,128]{2,1,0:T(8,128)(2,1)} %get-tuple-element.40), channel_id=1, source_target_pairs={{33,1},{35,3},{37,5},{39,7},{41,9},{43,11},{45,13},{47,15},{49,17}... | collective-permute-start | bytes 2359304 | tf_op jit(solution)/shard_map/ppermute | solution.py:506
  89.7 20.3 %collective-permute-start.13 = (bf16[12,256,128]{2,1,0:T(8,128)(2,1)}, bf16[12,256,128]{2,1,0:T(8,128)(2,1)S(1)}, u32[]{:S(2)}, u32[]{:S(2)}) collective-permute-start(bf16[12,256,128]{2,1,0:T(8,128)(2,1)} %get-tuple-element.35.refs_9_), channel_id=1, source_target_pairs={{33,1},{35,3},{37,5},{39,7},{41,9},{43,11},{45,13},{47,15},{49,17}... | collective-permute-start | bytes 2359304 | tf_op jit(solution)/shard_map/ppermute | solution.py:507
  116.5 15.0 %collective-permute-start.15 = (bf16[3,768,128]{2,1,0:T(8,128)(2,1)}, bf16[3,768,128]{2,1,0:T(8,128)(2,1)S(1)}, u32[]{:S(2)}, u32[]{:S(2)}) collective-permute-start(bf16[3,768,128]{2,1,0:T(8,128)(2,1)} %bitcast.51), channel_id=1, source_target_pairs={{4,0},{20,1},{6,2},{22,3},{8,4},{24,5},{10,6},{26,7},{12,8},{28,9}... | collective-permute-start | bytes 1769480 | tf_op jit(solution)/shard_map/ppermute | solution.py:455
  118.0 13.4 %collective-permute-start.14 = (bf16[3,768,128]{2,1,0:T(8,128)(2,1)}, bf16[3,768,128]{2,1,0:T(8,128)(2,1)S(1)}, u32[]{:S(2)}, u32[]{:S(2)}) collective-permute-start(bf16[3,768,128]{2,1,0:T(8,128)(2,1)} %bitcast.50), channel_id=1, source_target_pairs={{0,0},{16,1},{2,2},{18,3},{4,4},{20,5},{6,6},{22,7},{8,8},{24,9},{... | collective-permute-start | bytes 1769480 | tf_op jit(solution)/shard_map/ppermute | solution.py:455
  119.8 11.7 %collective-permute-start.16 = (bf16[3,768,128]{2,1,0:T(8,128)(2,1)}, bf16[3,768,128]{2,1,0:T(8,128)(2,1)S(1)}, u32[]{:S(2)}, u32[]{:S(2)}) collective-permute-start(bf16[3,768,128]{2,1,0:T(8,128)(2,1)} %bitcast.49), channel_id=1, source_target_pairs={{8,0},{24,1},{10,2},{26,3},{12,4},{28,5},{14,6},{30,7},{0,8},{16,9... | collective-permute-start | bytes 1769480 | tf_op jit(solution)/shard_map/ppermute | solution.py:455
  122.3 28.0 %collective-permute-start.17 = (bf16[3,768,128]{2,1,0:T(8,128)(2,1)}, bf16[3,768,128]{2,1,0:T(8,128)(2,1)S(1)}, u32[]{:S(2)}, u32[]{:S(2)}) collective-permute-start(bf16[3,768,128]{2,1,0:T(8,128)(2,1)} %bitcast.48), channel_id=1, source_target_pairs={{12,0},{28,1},{14,2},{30,3},{0,4},{16,5},{2,6},{18,7},{4,8},{20,9}... | collective-permute-start | bytes 1769480 | tf_op jit(solution)/shard_map/ppermute | solution.py:455
  131.5 18.9 %copy-start.7 = (bf16[3,768,128]{2,1,0:T(8,128)(2,1)}, bf16[3,768,128]{2,1,0:T(8,128)(2,1)S(1)}, u32[]{:S(2)}) copy-start(bf16[3,768,128]{2,1,0:T(8,128)(2,1)S(1)} %collective-permute-done.15.refs_1_) | copy-start | bytes 1769476
  131.5 18.9 %copy-start.8 = (bf16[3,768,128]{2,1,0:T(8,128)(2,1)}, bf16[3,768,128]{2,1,0:T(8,128)(2,1)S(1)}, u32[]{:S(2)}) copy-start(bf16[3,768,128]{2,1,0:T(8,128)(2,1)S(1)} %collective-permute-done.14.refs_0_) | copy-start | bytes 1769476
  131.5 18.9 %copy-start.9 = (bf16[3,768,128]{2,1,0:T(8,128)(2,1)}, bf16[3,768,128]{2,1,0:T(8,128)(2,1)S(1)}, u32[]{:S(2)}) copy-start(bf16[3,768,128]{2,1,0:T(8,128)(2,1)S(1)} %collective-permute-done.16.refs_2_) | copy-start | bytes 1769476
  (13 other events, 19.0 us)

commit v6 on v5

--- a/solution.py
+++ b/solution.py
@@ -54,7 +54,6 @@
     if 0 <= z + 2 * c - 1 < 4
 ]
 BACK_Z = [(j, i) for i, j in ALONG_Z]
-BACK_Z_SECOND = [(j, i) for j, i in BACK_Z if i % 2]
 
 
 def nt(a, b):
@@ -138,7 +137,7 @@
         outs, refs = refs[:3], refs[3:]
         (*made, s1, s2), refs = refs[:5], refs[5:]
     else:
-        outs, refs = refs[:4], refs[4:]
+        outs, refs = refs[:3], refs[3:]
         made, refs = refs[:5], refs[5:]
     qs, gs, ks, vs, dqa, dka, dva, sems = refs
     core, size = at[2], GROUP[phase]
@@ -165,7 +164,7 @@
     def late():
         return [
             pltpu.make_async_copy(extra[0], s1, sems.at[42]),
-            pltpu.make_async_copy(extra[1], s2, sems.at[43]),
+            pltpu.make_async_copy(extra[1].at[1], s2, sems.at[43]),
         ]
 
     for own in range(2):
@@ -270,7 +269,9 @@
             made[3][s] = (dka[HALF + s] * QK_SCALE).astype(BF)
             made[4][s] = (dva[HALF + s] * V_SCALE).astype(BF)
 
-    targets = outs if phase else (outs[0], outs[1], outs[2], outs[3].at[0], outs[3].at[1])
+    targets = outs
+    if phase == 0:
+        targets = (outs[0].at[0], outs[0].at[1], outs[1], outs[2].at[0], outs[2].at[1])
     going = []
     for part in range(4):
         lax.fori_loop(3 * part, 3 * part + 3, lambda s, _: (finish(s), 0)[1], 0)
@@ -284,16 +285,17 @@
         copy.wait()
 
 
-def piped(ins, shapes, in_sems, outs, staged, out_sems, compute):
+def sum_kernel(at, *refs):
+    (beside, back), ins, outs = refs[:2], refs[2:5], refs[5:9]
+    bufs, (staged, in_sems, out_sems) = refs[9:12], refs[12:]
+    dq, dk, dv = bufs
+    first = at[2] == 0
+
     def coming(d):
         rows = pl.ds(3 * d, 3)
         return [
-            pltpu.make_async_copy(
-                src.at[:, rows] if four else src.at[rows],
-                dst.at[:, rows] if four else dst.at[rows],
-                in_sems.at[d, n],
-            )
-            for n, (src, dst, four) in enumerate(zip(ins, shapes[0], shapes[1]))
+            pltpu.make_async_copy(src.at[rows], dst.at[rows], in_sems.at[d, n])
+            for n, (src, dst) in enumerate(zip(ins, bufs))
         ]
 
     def going(d):
@@ -305,38 +307,32 @@
     for d in range(4):
         for copy in coming(d):
             copy.wait()
-        compute(d)
-        going(d).start()
-    for d in range(4):
-        going(d).wait()
-
-
-def sum_kernel(at, *refs):
-    ins, outs = refs[:6], refs[6:10]
-    bufs, (staged, in_sems, out_sems) = refs[10:16], refs[16:]
-    dq, dk, dv, beside, a1, a2 = bufs
-    first = at[2] == 0
-
-    def compute(d):
         for m in range(3):
             s = 3 * d + m
-            far = a1[s].astype(F32)
-            last = jnp.where(first, 0.0, a2[s].astype(F32))
+            far = back[0, s].astype(F32)
+            last = jnp.where(first, 0.0, back[1, s].astype(F32))
             staged[d, 0, m] = (dq[s].astype(F32) + jnp.where(first, far, 0.0)).astype(BF)
             far = jnp.where(first, 0.0, far)
             staged[d, 1, m] = (dk[s].astype(F32) + beside[0, s].astype(F32) + far).astype(BF)
             staged[d, 2, m] = (dv[s].astype(F32) + beside[1, s].astype(F32) + last).astype(BF)
-
-    piped(ins, (bufs, (0, 0, 0, 1, 0, 0)), in_sems, outs, staged, out_sems, compute)
+        going(d).start()
+    for d in range(4):
+        going(d).wait()
 
 
 def join_kernel(arrays, at, *refs):
-    outs, (stage, sems) = refs[4 : 4 + arrays], refs[-2:]
-    moves = []
+    outs, sems = refs[4 : 4 + arrays], refs[-1]
+    copies = []
     for d in range(4):
         lanes = pl.ds(pl.multiple_of(lax.rem(at[0] + d, 4) * HEAD, HEAD), HEAD)
-        moves += [(refs[d].at[n], outs[n].at[:, lanes]) for n in range(arrays)]
-    relay(moves, stage, sems)
+        for n in range(arrays):
+            copies.append(
+                pltpu.make_async_copy(refs[d].at[n], outs[n].at[:, lanes], sems.at[arrays * d + n])
+            )
+    for copy in copies:
+        copy.start()
+    for copy in copies:
+        copy.wait()
 
 
 def call(kernel, outs, ins, scratch=(), limit=56, where=ANY, cost=None, **kw):
@@ -493,18 +489,16 @@
         ]
 
     parts = [pltpu.VMEM((HALF, BLK, HEAD), BF)] * 5
-    p1, p2, s1, beside = call(
+    far, s1, beside = call(
         functools.partial(pairs_kernel, 0),
-        [half, half, half, two],
+        [two, half, two],
         [SMEM] * 2 + [ANY] * 11,
         parts + scratch(PLANE) + [dma(44)],
         cost=pairs_cost(139),
         limit=56,
         name="far",
     )(at, tab, *r1, *r2, across, *near)
-    s2 = p2
-    p1 = lax.ppermute(p1, AXES, BACK_Z)
-    p2 = lax.ppermute(p2, AXES, BACK_Z_SECOND)
+    back = lax.ppermute(far, AXES, BACK_Z)
     beside = lax.ppermute(beside, AXES, OTHER_CORE)
     dq, dk, dv = call(
         functools.partial(pairs_kernel, 1),
@@ -514,24 +508,25 @@
         cost=pairs_cost(60),
         limit=56,
         name="own",
-    )(at, tab, *r1, *r2, s1, s2)
-    v3, v4 = pltpu.VMEM((HALF, BLK, HEAD), BF), pltpu.VMEM((2, HALF, BLK, HEAD), BF)
+    )(at, tab, *r1, *r2, s1, far)
+    v3 = pltpu.VMEM((HALF, BLK, HEAD), BF)
     sums = call(
         sum_kernel,
         [shape((3, 3, BLK, HEAD), BF)] * 4,
-        [SMEM] + [ANY] * 6,
-        [v3, v3, v3, v4, v3, v3, pltpu.VMEM((4, 3, 3, BLK, HEAD), BF), dma(4, 6), dma(4)],
+        [SMEM] + [VMEM] * 2 + [ANY] * 3,
+        [v3, v3, v3, pltpu.VMEM((4, 3, 3, BLK, HEAD), BF), dma(4, 3), dma(4)],
         limit=56,
         name="sums",
-    )(at, dq, dk, dv, beside, p1, p2)
+    )(at, beside, back, dq, dk, dv)
     back = send([p.reshape(3, rows, HEAD) for p in sums], from_heads)
     out = shape(queries.shape, BF)
     return tuple(
         call(
             functools.partial(join_kernel, 3),
             [out] * 3,
-            [SMEM] + [ANY] * 4,
-            [pltpu.VMEM((12, rows, HEAD), BF), dma(2, 12)],
+            [SMEM] + [VMEM] * 4,
+            [dma(12)],
+            limit=40,
             name="join",
         )(at, *back)
     )

time: 157 us -> 155 us (0.987)
    unnamed x38 -> x30, local copies, waits for them, and re-layouts: 5.39 us -> 4.62 us
    ppermute x2 -> x1, starting transfers between devices: 4.25 us -> 3.93 us  [body(): back = lax.ppermute(far, AXES, BACK_Z)]
  transfers between devices with their start and end apart: 18 -> 17, of which waited for: 7 -> 7; matrix products, arithmetic and copies ran while one was open for 1% -> 1% of each run, Pallas kernels for 19% -> 19%
where the time goes in v6:
time: 155 us; the launch traced here: 154 us
  Pallas kernels  70 us (45%)
  waiting for transfers between devices  48.6 us (31%)
  starting transfers between devices  28 us (18%)
  local copies, waits for them, and re-layouts  5.47 us (4%)
    ppermute x12, waiting for transfers between devices, send(): return [lax.ppermute(p, AXES, pairs(d)) for d, p in enumerate(pieces)]  42.2 us
    pallas_call x1, Pallas kernels, body(): call(functools.partial(pairs_kernel, 0), [two, half, two], [SMEM] * 2 + [...  30.2 us
    ppermute x12, starting transfers between devices, send(): return [lax.ppermute(p, AXES, pairs(d)) for d, p in enumerate(pieces)]  22.2 us
    pallas_call x1, Pallas kernels, body(): call(functools.partial(pairs_kernel, 1), [half, half, half], [SMEM] * 2 +...  19.7 us
    pallas_call x2, Pallas kernels, split(): call(functools.partial(split_kernel, first_round), [shape((2, rows, HEAD)...  6.18 us
    pallas_call x1, Pallas kernels, body(): call(sum_kernel, [shape((3, 3, BLK, HEAD), BF)] * 4, [SMEM] + [VMEM] * 2...  4.83 us
    unnamed x30, local copies, waits for them, and re-layouts  4.62 us
    ppermute x1, starting transfers between devices, body(): back = lax.ppermute(far, AXES, BACK_Z)  3.93 us
  transfers between devices with their start and end apart: 17, of which 7 were waited for; matrix products, arithmetic and copies ran while one was open for 1% of the time, Pallas kernels for 19%

profile of v6, /device:TPU:0, one launch (start us, length us, event | category | flops | bytes accessed | tf_op | source)
XLA Modules:
  0.0 153.8 jit_solution(14903334996310631832)
XLA Ops:
  1.3 3.1 %split.2 = (bf16[2,768,128]{2,1,0:T(8,128)(2,1)}, bf16[2,768,128]{2,1,0:T(8,128)(2,1)}, bf16[2,768,128]{2,1,0:T(8,128)(2,1)}, bf16[2,768,128]{2,1,0:T(8,128)(2,1)}) custom-call(s32[4]{0:T(128)} %pad_add_fusion.1.at, bf16[768,512]{1,0:T(8,128)(2,1)} %q.3, bf16[768,512]{1,0:T(8,128)(2,1)} %g.3, bf16[768,512]{1,0:T(8,128)(2,1)} %k.3, bf16[768,512]{1,0:T(8,128)(2,1)} %v.3), custom_call_target="tpu_custom_call" | custom-call | tf_op jit(solution)/shard_map/split/pallas_call | solution.py:441
  4.4 1.7 %collective-permute-start.1 = (bf16[2,768,128]{2,1,0:T(8,128)(2,1)}, bf16[2,768,128]{2,1,0:T(8,128)(2,1)S(1)}, u32[]{:S(2)}, u32[]{:S(2)}) collective-permute-start(bf16[2,768,128]{2,1,0:T(8,128)(2,1)} %get-tuple-element.24), channel_id=1, source_target_pairs={{0,4},{1,20},{2,6},{3,22},{4,8},{5,24},{6,10},{7,26},{8,12},{9,28}... | collective-permute-start | bytes 1179656 | tf_op jit(solution)/shard_map/ppermute | solution.py:451
  6.2 2.9 %collective-permute-start.2 = (bf16[2,768,128]{2,1,0:T(8,128)(2,1)}, bf16[2,768,128]{2,1,0:T(8,128)(2,1)S(1)}, u32[]{:S(2)}, u32[]{:S(2)}) collective-permute-start(bf16[2,768,128]{2,1,0:T(8,128)(2,1)} %get-tuple-element.25), channel_id=1, source_target_pairs={{0,8},{1,24},{2,10},{3,26},{4,12},{5,28},{6,14},{7,30},{8,0},{9,16... | collective-permute-start | bytes 1179656 | tf_op jit(solution)/shard_map/ppermute | solution.py:451
  12.9 1.9 %table.1.refs_1_.tab = s32[3,256]{1,0:T(4,128)} custom-call(s32[4]{0:T(128)} %pad_add_fusion.1.at, s32[96]{0:T(128)} %counts.1, s32[2,16,128]{2,1,0:T(8,128)} %pad.4.rows), custom_call_target="tpu_custom_call" | custom-call | tf_op jit(solution)/shard_map/table/pallas_call | solution.py:431
  14.8 3.0 %split.3 = (bf16[2,768,128]{2,1,0:T(8,128)(2,1)}, bf16[2,768,128]{2,1,0:T(8,128)(2,1)}, bf16[2,768,128]{2,1,0:T(8,128)(2,1)}, bf16[2,768,128]{2,1,0:T(8,128)(2,1)}) custom-call(s32[4]{0:T(128)} %pad_add_fusion.1.at, bf16[768,512]{1,0:T(8,128)(2,1)} %q.3, bf16[768,512]{1,0:T(8,128)(2,1)} %g.3, bf16[768,512]{1,0:T(8,128)(2,1)} %k.3, bf16[768,512]{1,0:T(8,128)(2,1)} %v.3, ...), custom_call_target="tpu_custom_call" | custom-call | tf_op jit(solution)/shard_map/split/pallas_call | solution.py:441
  18.6 3.5 %collective-permute-done.1 = bf16[2,768,128]{2,1,0:T(8,128)(2,1)S(1)} collective-permute-done((bf16[2,768,128]{2,1,0:T(8,128)(2,1)}, bf16[2,768,128]{2,1,0:T(8,128)(2,1)S(1)}, u32[]{:S(2)}, u32[]{:S(2)}) %collective-permute-start.1) | collective-permute-done | bytes 393248 | tf_op jit(solution)/shard_map/ppermute | solution.py:451
  22.1 6.3 %collective-permute-start.6 = (bf16[2,768,128]{2,1,0:T(8,128)(2,1)}, bf16[2,768,128]{2,1,0:T(8,128)(2,1)S(1)}, u32[]{:S(2)}, u32[]{:S(2)}) collective-permute-start(bf16[2,768,128]{2,1,0:T(8,128)(2,1)} %get-tuple-element.29), channel_id=1, source_target_pairs={{0,8},{1,24},{2,10},{3,26},{4,12},{5,28},{6,14},{7,30},{8,0},{9,16... | collective-permute-start | bytes 1179656 | tf_op jit(solution)/shard_map/ppermute | solution.py:451
  28.4 1.7 %collective-permute-start.4 = (bf16[2,768,128]{2,1,0:T(8,128)(2,1)}, bf16[2,768,128]{2,1,0:T(8,128)(2,1)S(1)}, u32[]{:S(2)}, u32[]{:S(2)}) collective-permute-start(bf16[2,768,128]{2,1,0:T(8,128)(2,1)} %get-tuple-element.27.refs_4_), channel_id=1, source_target_pairs={{0,0},{1,16},{2,2},{3,18},{4,4},{5,20},{6,6},{7,22},{8,8},{9,24},{... | collective-permute-start | bytes 1179656 | tf_op jit(solution)/shard_map/ppermute | solution.py:451
  30.8 2.2 %gather.1 = bf16[2,12,256,128]{3,2,1,0:T(8,128)(2,1)} custom-call(bf16[2,3,256,128]{3,2,1,0:T(8,128)(2,1)} %bitcast.30, bf16[2,3,256,128]{3,2,1,0:T(8,128)(2,1)} %bitcast.18, bf16[2,3,256,128]{3,2,1,0:T(8,128)(2,1)} %bitcast.22, bf16[2,3,256,128]{3,2,1,0:T(8,128)(2,1)} %bitcast.26, bf16[2,768,128]{2,1,0:T(8,128)(2,1)} %get-tuple-element.27.refs_4_), custom_call_target="tpu_custom_call" | custom-call | tf_op jit(solution)/shard_map/gather/pallas_call | solution.py:463
  34.4 5.4 %collective-permute-done.5 = bf16[2,768,128]{2,1,0:T(8,128)(2,1)S(1)} collective-permute-done((bf16[2,768,128]{2,1,0:T(8,128)(2,1)}, bf16[2,768,128]{2,1,0:T(8,128)(2,1)S(1)}, u32[]{:S(2)}, u32[]{:S(2)}) %collective-permute-start.5) | collective-permute-done | bytes 393248 | tf_op jit(solution)/shard_map/ppermute | solution.py:451
  39.8 4.8 %collective-permute-done.6 = bf16[2,768,128]{2,1,0:T(8,128)(2,1)S(1)} collective-permute-done((bf16[2,768,128]{2,1,0:T(8,128)(2,1)}, bf16[2,768,128]{2,1,0:T(8,128)(2,1)S(1)}, u32[]{:S(2)}, u32[]{:S(2)}) %collective-permute-start.6) | collective-permute-done | bytes 393248 | tf_op jit(solution)/shard_map/ppermute | solution.py:451
  45.7 3.0 %gather_keys.1 = (bf16[2,10,256,128]{3,2,1,0:T(8,128)(2,1)}, bf16[2,2,256,128]{3,2,1,0:T(8,128)(2,1)}) custom-call(s32[4]{0:T(128)} %pad_add_fusion.1.at, bf16[2,3,256,128]{3,2,1,0:T(8,128)(2,1)} %bitcast.31, bf16[2,3,256,128]{3,2,1,0:T(8,128)(2,1)} %bitcast.19, bf16[2,3,256,128]{3,2,1,0:T(8,128)(2,1)} %bitcast.23, bf16[2,3,256,128]{3,2,1,0:T(8,128)(2,1)} %bitcast.27, ...), custom_call_target="tpu_custom_call" | custom-call | tf_op jit(solution)/shard_map/gather_keys/pallas_call | solution.py:471
  49.3 3.1 %collective-permute-done.10.refs_10_ = bf16[2,2,256,128]{3,2,1,0:T(8,128)(2,1)S(1)} collective-permute-done((bf16[2,2,256,128]{3,2,1,0:T(8,128)(2,1)}, bf16[2,2,256,128]{3,2,1,0:T(8,128)(2,1)S(1)}, u32[]{:S(2)}, u32[]{:S(2)}) %collective-permute-start.10) | collective-permute-done | bytes 262176 | tf_op jit(solution)/shard_map/ppermute | solution.py:478
  52.4 3.2 %collective-permute-done.8.refs_8_ = bf16[2,12,256,128]{3,2,1,0:T(8,128)(2,1)S(1)} collective-permute-done((bf16[2,12,256,128]{3,2,1,0:T(8,128)(2,1)}, bf16[2,12,256,128]{3,2,1,0:T(8,128)(2,1)S(1)}, u32[]{:S(2)}, u32[]{:S(2)}) %collective-permute-start.8) | collective-permute-done | bytes 1572896 | tf_op jit(solution)/shard_map/ppermute | solution.py:470
  56.8 30.2 %far.1 = (bf16[2,12,256,128]{3,2,1,0:T(8,128)(2,1)}, bf16[12,256,128]{2,1,0:T(8,128)(2,1)}, bf16[2,12,256,128]{3,2,1,0:T(8,128)(2,1)}) custom-call(s32[4]{0:T(128)} %pad_add_fusion.1.at, s32[3,256]{1,0:T(4,128)} %table.1.refs_1_.tab, bf16[2,3,256,128]{3,2,1,0:T(8,128)(2,1)} %bitcast.32, bf16[2,3,256,128]{3,2,1,0:T(8,128)(2,1)} %bitcast.20, ...), custom_call_target="tpu_custom_call" | custom-call | flops 11660165120 | bytes 12582912 | tf_op jit(solution)/shard_map/far/pallas_call | solution.py:492
  87.0 3.9 %collective-permute-start.12 = (bf16[2,12,256,128]{3,2,1,0:T(8,128)(2,1)}, bf16[2,12,256,128]{3,2,1,0:T(8,128)(2,1)S(1)}, u32[]{:S(2)}, u32[]{:S(2)}) collective-permute-start(bf16[2,12,256,128]{3,2,1,0:T(8,128)(2,1)} %get-tuple-element.34.refs_9_), channel_id=1, source_target_pairs={{33,1},{35,3},{37,5},{39,7},{41,9},{43,11},{45,13},{47,15},{49,17}... | collective-permute-start | bytes 4718600 | tf_op jit(solution)/shard_map/ppermute | solution.py:501
  91.0 19.7 %own.1 = (bf16[12,256,128]{2,1,0:T(8,128)(2,1)}, bf16[12,256,128]{2,1,0:T(8,128)(2,1)}, bf16[12,256,128]{2,1,0:T(8,128)(2,1)}) custom-call(s32[4]{0:T(128)} %pad_add_fusion.1.at, s32[3,256]{1,0:T(4,128)} %table.1.refs_1_.tab, bf16[2,3,256,128]{3,2,1,0:T(8,128)(2,1)} %bitcast.33, bf16[2,3,256,128]{3,2,1,0:T(8,128)(2,1)} %bitcast.21, ...), custom_call_target="tpu_custom_call" | custom-call | flops 5033164800 | bytes 12582912 | tf_op jit(solution)/shard_map/own/pallas_call | solution.py:503
  112.4 4.8 %sums.1 = (bf16[3,3,256,128]{3,2,1,0:T(8,128)(2,1)}, bf16[3,3,256,128]{3,2,1,0:T(8,128)(2,1)}, bf16[3,3,256,128]{3,2,1,0:T(8,128)(2,1)}, bf16[3,3,256,128]{3,2,1,0:T(8,128)(2,1)}) custom-call(s32[4]{0:T(128)} %pad_add_fusion.1.at, bf16[2,12,256,128]{3,2,1,0:T(8,128)(2,1)} %copy-done.1, bf16[2,12,256,128]{3,2,1,0:T(8,128)(2,1)} %copy-done.2, ...), custom_call_target="tpu_custom_call" | custom-call | tf_op jit(solution)/shard_map/sums/pallas_call | solution.py:513
  117.2 2.1 %collective-permute-start.14 = (bf16[3,768,128]{2,1,0:T(8,128)(2,1)}, bf16[3,768,128]{2,1,0:T(8,128)(2,1)S(1)}, u32[]{:S(2)}, u32[]{:S(2)}) collective-permute-start(bf16[3,768,128]{2,1,0:T(8,128)(2,1)} %bitcast.51), channel_id=1, source_target_pairs={{4,0},{20,1},{6,2},{22,3},{8,4},{24,5},{10,6},{26,7},{12,8},{28,9}... | collective-permute-start | bytes 1769480 | tf_op jit(solution)/shard_map/ppermute | solution.py:451
  119.3 1.7 %collective-permute-start.13 = (bf16[3,768,128]{2,1,0:T(8,128)(2,1)}, bf16[3,768,128]{2,1,0:T(8,128)(2,1)S(1)}, u32[]{:S(2)}, u32[]{:S(2)}) collective-permute-start(bf16[3,768,128]{2,1,0:T(8,128)(2,1)} %bitcast.50), channel_id=1, source_target_pairs={{0,0},{16,1},{2,2},{18,3},{4,4},{20,5},{6,6},{22,7},{8,8},{24,9},{... | collective-permute-start | bytes 1769480 | tf_op jit(solution)/shard_map/ppermute | solution.py:451
  121.0 2.0 %collective-permute-start.15 = (bf16[3,768,128]{2,1,0:T(8,128)(2,1)}, bf16[3,768,128]{2,1,0:T(8,128)(2,1)S(1)}, u32[]{:S(2)}, u32[]{:S(2)}) collective-permute-start(bf16[3,768,128]{2,1,0:T(8,128)(2,1)} %bitcast.49), channel_id=1, source_target_pairs={{8,0},{24,1},{10,2},{26,3},{12,4},{28,5},{14,6},{30,7},{0,8},{16,9... | collective-permute-start | bytes 1769480 | tf_op jit(solution)/shard_map/ppermute | solution.py:451
  123.0 10.6 %collective-permute-done.14.refs_1_ = bf16[3,768,128]{2,1,0:T(8,128)(2,1)S(1)} collective-permute-done((bf16[3,768,128]{2,1,0:T(8,128)(2,1)}, bf16[3,768,128]{2,1,0:T(8,128)(2,1)S(1)}, u32[]{:S(2)}, u32[]{:S(2)}) %collective-permute-start.14) | collective-permute-done | bytes 589856 | tf_op jit(solution)/shard_map/ppermute | solution.py:451
  133.6 17.9 %collective-permute-done.16.refs_3_ = bf16[3,768,128]{2,1,0:T(8,128)(2,1)S(1)} collective-permute-done((bf16[3,768,128]{2,1,0:T(8,128)(2,1)}, bf16[3,768,128]{2,1,0:T(8,128)(2,1)S(1)}, u32[]{:S(2)}, u32[]{:S(2)}) %collective-permute-start.16) | collective-permute-done | bytes 589856 | tf_op jit(solution)/shard_map/ppermute | solution.py:451
  151.6 2.0 %join.1 = (bf16[768,512]{1,0:T(8,128)(2,1)}, bf16[768,512]{1,0:T(8,128)(2,1)}, bf16[768,512]{1,0:T(8,128)(2,1)}) custom-call(s32[4]{0:T(128)S(1)} %copy-done, bf16[3,768,128]{2,1,0:T(8,128)(2,1)S(1)} %collective-permute-done.13.refs_0_, bf16[3,768,128]{2,1,0:T(8,128)(2,1)S(1)} %collective-permute-done.14.refs_1_, ...), custom_call_target="tpu_custom_call" | custom-call | tf_op jit(solution)/shard_map/join/pallas_call | solution.py:524
  (55 shorter events, 11.8 us)
Async XLA Ops:
  1.3 10.8 %copy-start.11 = (s32[96,16]{0,1:T(8,128)S(1)}, s32[96,16]{0,1:T(8,128)}, u32[]{:S(2)}) copy-start(s32[96,16]{0,1:T(8,128)} %param.10) | copy-start | bytes 18436
  4.4 17.7 %collective-permute-start.1 = (bf16[2,768,128]{2,1,0:T(8,128)(2,1)}, bf16[2,768,128]{2,1,0:T(8,128)(2,1)S(1)}, u32[]{:S(2)}, u32[]{:S(2)}) collective-permute-start(bf16[2,768,128]{2,1,0:T(8,128)(2,1)} %get-tuple-element.24), channel_id=1, source_target_pairs={{0,4},{1,20},{2,6},{3,22},{4,8},{5,24},{6,10},{7,26},{8,12},{9,28}... | collective-permute-start | bytes 1179656 | tf_op jit(solution)/shard_map/ppermute | solution.py:451
  6.2 22.2 %collective-permute-start.2 = (bf16[2,768,128]{2,1,0:T(8,128)(2,1)}, bf16[2,768,128]{2,1,0:T(8,128)(2,1)S(1)}, u32[]{:S(2)}, u32[]{:S(2)}) collective-permute-start(bf16[2,768,128]{2,1,0:T(8,128)(2,1)} %get-tuple-element.25), channel_id=1, source_target_pairs={{0,8},{1,24},{2,10},{3,26},{4,12},{5,28},{6,14},{7,30},{8,0},{9,16... | collective-permute-start | bytes 1179656 | tf_op jit(solution)/shard_map/ppermute | solution.py:451
  9.1 19.4 %collective-permute-start.3 = (bf16[2,768,128]{2,1,0:T(8,128)(2,1)}, bf16[2,768,128]{2,1,0:T(8,128)(2,1)S(1)}, u32[]{:S(2)}, u32[]{:S(2)}) collective-permute-start(bf16[2,768,128]{2,1,0:T(8,128)(2,1)} %get-tuple-element.26), channel_id=1, source_target_pairs={{0,12},{1,28},{2,14},{3,30},{4,0},{5,16},{6,2},{7,18},{8,4},{9,20}... | collective-permute-start | bytes 1179656 | tf_op jit(solution)/shard_map/ppermute | solution.py:451
  10.4 19.7 %collective-permute-start = (bf16[2,768,128]{2,1,0:T(8,128)(2,1)}, bf16[2,768,128]{2,1,0:T(8,128)(2,1)S(1)}, u32[]{:S(2)}, u32[]{:S(2)}) collective-permute-start(bf16[2,768,128]{2,1,0:T(8,128)(2,1)} %get-tuple-element.23.refs_0_), channel_id=1, source_target_pairs={{0,0},{1,16},{2,2},{3,18},{4,4},{5,20},{6,6},{7,22},{8,8},{9,24},{... | collective-permute-start | bytes 1179656 | tf_op jit(solution)/shard_map/ppermute | solution.py:451
  17.9 21.9 %collective-permute-start.5 = (bf16[2,768,128]{2,1,0:T(8,128)(2,1)}, bf16[2,768,128]{2,1,0:T(8,128)(2,1)S(1)}, u32[]{:S(2)}, u32[]{:S(2)}) collective-permute-start(bf16[2,768,128]{2,1,0:T(8,128)(2,1)} %get-tuple-element.28), channel_id=1, source_target_pairs={{0,4},{1,20},{2,6},{3,22},{4,8},{5,24},{6,10},{7,26},{8,12},{9,28}... | collective-permute-start | bytes 1179656 | tf_op jit(solution)/shard_map/ppermute | solution.py:451
  22.1 8.0 %copy-start.3 = (bf16[2,768,128]{2,1,0:T(8,128)(2,1)}, bf16[2,768,128]{2,1,0:T(8,128)(2,1)S(1)}, u32[]{:S(2)}) copy-start(bf16[2,768,128]{2,1,0:T(8,128)(2,1)S(1)} %collective-permute-done.1) | copy-start | bytes 1179652
  22.1 22.4 %collective-permute-start.6 = (bf16[2,768,128]{2,1,0:T(8,128)(2,1)}, bf16[2,768,128]{2,1,0:T(8,128)(2,1)S(1)}, u32[]{:S(2)}, u32[]{:S(2)}) collective-permute-start(bf16[2,768,128]{2,1,0:T(8,128)(2,1)} %get-tuple-element.29), channel_id=1, source_target_pairs={{0,8},{1,24},{2,10},{3,26},{4,12},{5,28},{6,14},{7,30},{8,0},{9,16... | collective-permute-start | bytes 1179656 | tf_op jit(solution)/shard_map/ppermute | solution.py:451
  28.4 1.7 %copy-start.4 = (bf16[2,768,128]{2,1,0:T(8,128)(2,1)}, bf16[2,768,128]{2,1,0:T(8,128)(2,1)S(1)}, u32[]{:S(2)}) copy-start(bf16[2,768,128]{2,1,0:T(8,128)(2,1)S(1)} %collective-permute-done.2) | copy-start | bytes 1179652
  28.4 16.2 %collective-permute-start.7 = (bf16[2,768,128]{2,1,0:T(8,128)(2,1)}, bf16[2,768,128]{2,1,0:T(8,128)(2,1)S(1)}, u32[]{:S(2)}, u32[]{:S(2)}) collective-permute-start(bf16[2,768,128]{2,1,0:T(8,128)(2,1)} %get-tuple-element.30), channel_id=1, source_target_pairs={{0,12},{1,28},{2,14},{3,30},{4,0},{5,16},{6,2},{7,18},{8,4},{9,20}... | collective-permute-start | bytes 1179656 | tf_op jit(solution)/shard_map/ppermute | solution.py:451
  28.4 16.1 %collective-permute-start.4 = (bf16[2,768,128]{2,1,0:T(8,128)(2,1)}, bf16[2,768,128]{2,1,0:T(8,128)(2,1)S(1)}, u32[]{:S(2)}, u32[]{:S(2)}) collective-permute-start(bf16[2,768,128]{2,1,0:T(8,128)(2,1)} %get-tuple-element.27.refs_4_), channel_id=1, source_target_pairs={{0,0},{1,16},{2,2},{3,18},{4,4},{5,20},{6,6},{7,22},{8,8},{9,24},{... | collective-permute-start | bytes 1179656 | tf_op jit(solution)/shard_map/ppermute | solution.py:451
  33.1 22.5 %collective-permute-start.8 = (bf16[2,12,256,128]{3,2,1,0:T(8,128)(2,1)}, bf16[2,12,256,128]{3,2,1,0:T(8,128)(2,1)S(1)}, u32[]{:S(2)}, u32[]{:S(2)}) collective-permute-start(bf16[2,12,256,128]{3,2,1,0:T(8,128)(2,1)} %gather.1), channel_id=1, source_target_pairs={{1,33},{3,35},{5,37},{7,39},{9,41},{11,43},{13,45},{15,47},{17,49}... | collective-permute-start | bytes 4718600 | tf_op jit(solution)/shard_map/ppermute | solution.py:470
  39.8 4.8 %copy-start.7 = (bf16[2,768,128]{2,1,0:T(8,128)(2,1)}, bf16[2,768,128]{2,1,0:T(8,128)(2,1)S(1)}, u32[]{:S(2)}) copy-start(bf16[2,768,128]{2,1,0:T(8,128)(2,1)S(1)} %collective-permute-done.5) | copy-start | bytes 1179652
  48.7 3.7 %collective-permute-start.9 = (bf16[2,10,256,128]{3,2,1,0:T(8,128)(2,1)}, bf16[2,10,256,128]{3,2,1,0:T(8,128)(2,1)S(1)}, u32[]{:S(2)}, u32[]{:S(2)}) collective-permute-start(bf16[2,10,256,128]{3,2,1,0:T(8,128)(2,1)} %get-tuple-element.31), channel_id=1, source_target_pairs={{0,1},{1,0},{2,3},{3,2},{4,5},{5,4},{6,7},{7,6},{8,9},{9,8},{10,11... | collective-permute-start | bytes 3932168 | tf_op jit(solution)/shard_map/ppermute | solution.py:478
  48.8 3.6 %collective-permute-start.10 = (bf16[2,2,256,128]{3,2,1,0:T(8,128)(2,1)}, bf16[2,2,256,128]{3,2,1,0:T(8,128)(2,1)S(1)}, u32[]{:S(2)}, u32[]{:S(2)}) collective-permute-start(bf16[2,2,256,128]{3,2,1,0:T(8,128)(2,1)} %get-tuple-element.32), channel_id=1, source_target_pairs={{0,1},{1,0},{2,3},{3,2},{4,5},{5,4},{6,7},{7,6},{8,9},{9,8},{10,11... | collective-permute-start | bytes 786440 | tf_op jit(solution)/shard_map/ppermute | solution.py:478
  52.4 3.2 %copy-start.14 = (bf16[2,2,256,128]{3,2,1,0:T(8,128)(2,1)}, bf16[2,2,256,128]{3,2,1,0:T(8,128)(2,1)S(1)}, u32[]{:S(2)}) copy-start(bf16[2,2,256,128]{3,2,1,0:T(8,128)(2,1)S(1)} %collective-permute-done.10.refs_10_) | copy-start | bytes 786436
  52.4 3.2 %copy-start.13 = (bf16[2,10,256,128]{3,2,1,0:T(8,128)(2,1)}, bf16[2,10,256,128]{3,2,1,0:T(8,128)(2,1)S(1)}, u32[]{:S(2)}) copy-start(bf16[2,10,256,128]{3,2,1,0:T(8,128)(2,1)S(1)} %collective-permute-done.9.refs_9_) | copy-start | bytes 3932164
  86.9 23.7 %collective-permute-start.11 = (bf16[2,12,256,128]{3,2,1,0:T(8,128)(2,1)}, bf16[2,12,256,128]{3,2,1,0:T(8,128)(2,1)S(1)}, u32[]{:S(2)}, u32[]{:S(2)}) collective-permute-start(bf16[2,12,256,128]{3,2,1,0:T(8,128)(2,1)} %get-tuple-element.33), channel_id=1, source_target_pairs={{0,1},{1,0},{2,3},{3,2},{4,5},{5,4},{6,7},{7,6},{8,9},{9,8},{10,11... | collective-permute-start | bytes 4718600 | tf_op jit(solution)/shard_map/ppermute | solution.py:502
  87.0 23.7 %collective-permute-start.12 = (bf16[2,12,256,128]{3,2,1,0:T(8,128)(2,1)}, bf16[2,12,256,128]{3,2,1,0:T(8,128)(2,1)S(1)}, u32[]{:S(2)}, u32[]{:S(2)}) collective-permute-start(bf16[2,12,256,128]{3,2,1,0:T(8,128)(2,1)} %get-tuple-element.34.refs_9_), channel_id=1, source_target_pairs={{33,1},{35,3},{37,5},{39,7},{41,9},{43,11},{45,13},{47,15},{49,17}... | collective-permute-start | bytes 4718600 | tf_op jit(solution)/shard_map/ppermute | solution.py:501
  112.4 39.2 %copy-start = (s32[4]{0:T(128)S(1)}, s32[4]{0:T(128)}, u32[]{:S(2)}) copy-start(s32[4]{0:T(128)} %pad_add_fusion.1.at) | copy-start | bytes 52
  117.2 16.4 %collective-permute-start.14 = (bf16[3,768,128]{2,1,0:T(8,128)(2,1)}, bf16[3,768,128]{2,1,0:T(8,128)(2,1)S(1)}, u32[]{:S(2)}, u32[]{:S(2)}) collective-permute-start(bf16[3,768,128]{2,1,0:T(8,128)(2,1)} %bitcast.51), channel_id=1, source_target_pairs={{4,0},{20,1},{6,2},{22,3},{8,4},{24,5},{10,6},{26,7},{12,8},{28,9}... | collective-permute-start | bytes 1769480 | tf_op jit(solution)/shard_map/ppermute | solution.py:451
  119.3 14.3 %collective-permute-start.13 = (bf16[3,768,128]{2,1,0:T(8,128)(2,1)}, bf16[3,768,128]{2,1,0:T(8,128)(2,1)S(1)}, u32[]{:S(2)}, u32[]{:S(2)}) collective-permute-start(bf16[3,768,128]{2,1,0:T(8,128)(2,1)} %bitcast.50), channel_id=1, source_target_pairs={{0,0},{16,1},{2,2},{18,3},{4,4},{20,5},{6,6},{22,7},{8,8},{24,9},{... | collective-permute-start | bytes 1769480 | tf_op jit(solution)/shard_map/ppermute | solution.py:451
  121.0 12.6 %collective-permute-start.15 = (bf16[3,768,128]{2,1,0:T(8,128)(2,1)}, bf16[3,768,128]{2,1,0:T(8,128)(2,1)S(1)}, u32[]{:S(2)}, u32[]{:S(2)}) collective-permute-start(bf16[3,768,128]{2,1,0:T(8,128)(2,1)} %bitcast.49), channel_id=1, source_target_pairs={{8,0},{24,1},{10,2},{26,3},{12,4},{28,5},{14,6},{30,7},{0,8},{16,9... | collective-permute-start | bytes 1769480 | tf_op jit(solution)/shard_map/ppermute | solution.py:451
  123.0 28.5 %collective-permute-start.16 = (bf16[3,768,128]{2,1,0:T(8,128)(2,1)}, bf16[3,768,128]{2,1,0:T(8,128)(2,1)S(1)}, u32[]{:S(2)}, u32[]{:S(2)}) collective-permute-start(bf16[3,768,128]{2,1,0:T(8,128)(2,1)} %bitcast.48), channel_id=1, source_target_pairs={{12,0},{28,1},{14,2},{30,3},{0,4},{16,5},{2,6},{18,7},{4,8},{20,9}... | collective-permute-start | bytes 1769480 | tf_op jit(solution)/shard_map/ppermute | solution.py:451
  (8 other events, 9.2 us)

commit v7 on v6

--- a/solution.py
+++ b/solution.py
@@ -465,6 +465,7 @@
         [two],
         [ANY] * 5,
         [pltpu.VMEM((4, 2, 3, BLK, HEAD), BF), dma(2, 4)],
+        limit=40,
         name="gather",
     )(*r1, sent2[0])[0]
     across = lax.ppermute(first, AXES, ALONG_Z)
@@ -473,6 +474,7 @@
         [shape((2, n, BLK, HEAD), BF) for n in (MOST, HALF - MOST)],
         [SMEM] + [ANY] * 8,
         [pltpu.VMEM((HALF, 2, BLK, HEAD), BF), dma(2, HALF)],
+        limit=40,
         name="gather_keys",
     )(at, *r1, *r2)
     near = [lax.ppermute(n, AXES, OTHER_CORE) for n in near]

time: 155 us -> 153 us (0.987)
  Pallas kernels: 70 us -> 68.3 us
    unnamed x30 -> x34, local copies, waits for them, and re-layouts: 4.62 us -> 3.96 us
  transfers between devices with their start and end apart: 17 -> 17, of which waited for: 7 -> 8; matrix products, arithmetic and copies ran while one was open for 1% -> 1% of each run, Pallas kernels for 19% -> 19%
where the time goes in v7:
time: 153 us
  Pallas kernels  68.3 us (45%)
  waiting for transfers between devices  48.9 us (32%)
  starting transfers between devices  28.8 us (19%)
  local copies, waits for them, and re-layouts  4.8 us (3%)
    ppermute x12, waiting for transfers between devices, send(): return [lax.ppermute(p, AXES, pairs(d)) for d, p in enumerate(pieces)]  42.2 us
    pallas_call x1, Pallas kernels, body(): call(functools.partial(pairs_kernel, 0), [two, half, two], [SMEM] * 2 + [...  29.7 us
    ppermute x12, starting transfers between devices, send(): return [lax.ppermute(p, AXES, pairs(d)) for d, p in enumerate(pieces)]  22.2 us
    pallas_call x1, Pallas kernels, body(): call(functools.partial(pairs_kernel, 1), [half, half, half], [SMEM] * 2 +...  19.5 us
    pallas_call x2, Pallas kernels, split(): call(functools.partial(split_kernel, first_round), [shape((2, rows, HEAD)...  6.19 us
    pallas_call x1, Pallas kernels, body(): call(sum_kernel, [shape((3, 3, BLK, HEAD), BF)] * 4, [SMEM] + [VMEM] * 2...  4.84 us
    ppermute x1, starting transfers between devices, body(): back = lax.ppermute(far, AXES, BACK_Z)  4.7 us
    unnamed x34, local copies, waits for them, and re-layouts  3.96 us
  transfers between devices with their start and end apart: 17, of which 8 were waited for; matrix products, arithmetic and copies ran while one was open for 1% of the time, Pallas kernels for 19%

profile of v7, /device:TPU:0, one launch (start us, length us, event | category | flops | bytes accessed | tf_op | source)
XLA Modules:
  0.0 152.5 jit_solution(2848161801544600166)
XLA Ops:
  1.3 3.1 %split.2 = (bf16[2,768,128]{2,1,0:T(8,128)(2,1)}, bf16[2,768,128]{2,1,0:T(8,128)(2,1)}, bf16[2,768,128]{2,1,0:T(8,128)(2,1)}, bf16[2,768,128]{2,1,0:T(8,128)(2,1)}) custom-call(s32[4]{0:T(128)} %pad_add_fusion.1.at, bf16[768,512]{1,0:T(8,128)(2,1)} %q.3, bf16[768,512]{1,0:T(8,128)(2,1)} %g.3, bf16[768,512]{1,0:T(8,128)(2,1)} %k.3, bf16[768,512]{1,0:T(8,128)(2,1)} %v.3), custom_call_target="tpu_custom_call" | custom-call | tf_op jit(solution)/shard_map/split/pallas_call | solution.py:441
  4.4 1.7 %collective-permute-start.1 = (bf16[2,768,128]{2,1,0:T(8,128)(2,1)}, bf16[2,768,128]{2,1,0:T(8,128)(2,1)S(1)}, u32[]{:S(2)}, u32[]{:S(2)}) collective-permute-start(bf16[2,768,128]{2,1,0:T(8,128)(2,1)} %get-tuple-element.24), channel_id=1, source_target_pairs={{0,4},{1,20},{2,6},{3,22},{4,8},{5,24},{6,10},{7,26},{8,12},{9,28}... | collective-permute-start | bytes 1179656 | tf_op jit(solution)/shard_map/ppermute | solution.py:451
  6.2 2.9 %collective-permute-start.2 = (bf16[2,768,128]{2,1,0:T(8,128)(2,1)}, bf16[2,768,128]{2,1,0:T(8,128)(2,1)S(1)}, u32[]{:S(2)}, u32[]{:S(2)}) collective-permute-start(bf16[2,768,128]{2,1,0:T(8,128)(2,1)} %get-tuple-element.25), channel_id=1, source_target_pairs={{0,8},{1,24},{2,10},{3,26},{4,12},{5,28},{6,14},{7,30},{8,0},{9,16... | collective-permute-start | bytes 1179656 | tf_op jit(solution)/shard_map/ppermute | solution.py:451
  10.4 1.6 %collective-permute-start = (bf16[2,768,128]{2,1,0:T(8,128)(2,1)}, bf16[2,768,128]{2,1,0:T(8,128)(2,1)S(1)}, u32[]{:S(2)}, u32[]{:S(2)}) collective-permute-start(bf16[2,768,128]{2,1,0:T(8,128)(2,1)} %get-tuple-element.23.refs_0_), channel_id=1, source_target_pairs={{0,0},{1,16},{2,2},{3,18},{4,4},{5,20},{6,6},{7,22},{8,8},{9,24},{... | collective-permute-start | bytes 1179656 | tf_op jit(solution)/shard_map/ppermute | solution.py:451
  12.9 1.9 %table.1.refs_1_.tab = s32[3,256]{1,0:T(4,128)} custom-call(s32[4]{0:T(128)} %pad_add_fusion.1.at, s32[96]{0:T(128)} %counts.1, s32[2,16,128]{2,1,0:T(8,128)} %pad.4.rows), custom_call_target="tpu_custom_call" | custom-call | tf_op jit(solution)/shard_map/table/pallas_call | solution.py:431
  14.8 3.1 %split.3 = (bf16[2,768,128]{2,1,0:T(8,128)(2,1)}, bf16[2,768,128]{2,1,0:T(8,128)(2,1)}, bf16[2,768,128]{2,1,0:T(8,128)(2,1)}, bf16[2,768,128]{2,1,0:T(8,128)(2,1)}) custom-call(s32[4]{0:T(128)} %pad_add_fusion.1.at, bf16[768,512]{1,0:T(8,128)(2,1)} %q.3, bf16[768,512]{1,0:T(8,128)(2,1)} %g.3, bf16[768,512]{1,0:T(8,128)(2,1)} %k.3, bf16[768,512]{1,0:T(8,128)(2,1)} %v.3, ...), custom_call_target="tpu_custom_call" | custom-call | tf_op jit(solution)/shard_map/split/pallas_call | solution.py:441
  18.6 3.5 %collective-permute-done.1 = bf16[2,768,128]{2,1,0:T(8,128)(2,1)S(1)} collective-permute-done((bf16[2,768,128]{2,1,0:T(8,128)(2,1)}, bf16[2,768,128]{2,1,0:T(8,128)(2,1)S(1)}, u32[]{:S(2)}, u32[]{:S(2)}) %collective-permute-start.1) | collective-permute-done | bytes 393248 | tf_op jit(solution)/shard_map/ppermute | solution.py:451
  22.1 6.3 %collective-permute-start.6 = (bf16[2,768,128]{2,1,0:T(8,128)(2,1)}, bf16[2,768,128]{2,1,0:T(8,128)(2,1)S(1)}, u32[]{:S(2)}, u32[]{:S(2)}) collective-permute-start(bf16[2,768,128]{2,1,0:T(8,128)(2,1)} %get-tuple-element.29), channel_id=1, source_target_pairs={{0,8},{1,24},{2,10},{3,26},{4,12},{5,28},{6,14},{7,30},{8,0},{9,16... | collective-permute-start | bytes 1179656 | tf_op jit(solution)/shard_map/ppermute | solution.py:451
  28.4 1.7 %collective-permute-start.4 = (bf16[2,768,128]{2,1,0:T(8,128)(2,1)}, bf16[2,768,128]{2,1,0:T(8,128)(2,1)S(1)}, u32[]{:S(2)}, u32[]{:S(2)}) collective-permute-start(bf16[2,768,128]{2,1,0:T(8,128)(2,1)} %get-tuple-element.27.refs_4_), channel_id=1, source_target_pairs={{0,0},{1,16},{2,2},{3,18},{4,4},{5,20},{6,6},{7,22},{8,8},{9,24},{... | collective-permute-start | bytes 1179656 | tf_op jit(solution)/shard_map/ppermute | solution.py:451
  33.8 6.0 %collective-permute-done.5 = bf16[2,768,128]{2,1,0:T(8,128)(2,1)S(1)} collective-permute-done((bf16[2,768,128]{2,1,0:T(8,128)(2,1)}, bf16[2,768,128]{2,1,0:T(8,128)(2,1)S(1)}, u32[]{:S(2)}, u32[]{:S(2)}) %collective-permute-start.5) | collective-permute-done | bytes 393248 | tf_op jit(solution)/shard_map/ppermute | solution.py:451
  39.8 4.8 %collective-permute-done.6 = bf16[2,768,128]{2,1,0:T(8,128)(2,1)S(1)} collective-permute-done((bf16[2,768,128]{2,1,0:T(8,128)(2,1)}, bf16[2,768,128]{2,1,0:T(8,128)(2,1)S(1)}, u32[]{:S(2)}, u32[]{:S(2)}) %collective-permute-start.6) | collective-permute-done | bytes 393248 | tf_op jit(solution)/shard_map/ppermute | solution.py:451
  44.6 2.8 %gather_keys.1 = (bf16[2,10,256,128]{3,2,1,0:T(8,128)(2,1)S(1)}, bf16[2,2,256,128]{3,2,1,0:T(8,128)(2,1)S(1)}) custom-call(s32[4]{0:T(128)S(1)} %copy-done.9, bf16[2,3,256,128]{3,2,1,0:T(8,128)(2,1)S(1)} %bitcast.31, bf16[2,3,256,128]{3,2,1,0:T(8,128)(2,1)S(1)} %bitcast.19, bf16[2,3,256,128]{3,2,1,0:T(8,128)(2,1)S(1)} %bitcast.23, ...), custom_call_target="tpu_custom_call" | custom-call | tf_op jit(solution)/shard_map/gather_keys/pallas_call | solution.py:472
  48.1 2.9 %collective-permute-done.10.refs_10_ = bf16[2,2,256,128]{3,2,1,0:T(8,128)(2,1)S(1)} collective-permute-done((bf16[2,2,256,128]{3,2,1,0:T(8,128)(2,1)S(1)}, bf16[2,2,256,128]{3,2,1,0:T(8,128)(2,1)S(1)}, u32[]{:S(2)}, u32[]{:S(2)}) %collective-permute-start.10) | collective-permute-done | bytes 262176 | tf_op jit(solution)/shard_map/ppermute | solution.py:480
  51.0 3.8 %collective-permute-done.8.refs_8_ = bf16[2,12,256,128]{3,2,1,0:T(8,128)(2,1)S(1)} collective-permute-done((bf16[2,12,256,128]{3,2,1,0:T(8,128)(2,1)S(1)}, bf16[2,12,256,128]{3,2,1,0:T(8,128)(2,1)S(1)}, u32[]{:S(2)}, u32[]{:S(2)}) %collective-permute-start.8) | collective-permute-done | bytes 1572896 | tf_op jit(solution)/shard_map/ppermute | solution.py:471
  55.9 29.7 %far.1 = (bf16[2,12,256,128]{3,2,1,0:T(8,128)(2,1)}, bf16[12,256,128]{2,1,0:T(8,128)(2,1)}, bf16[2,12,256,128]{3,2,1,0:T(8,128)(2,1)}) custom-call(s32[4]{0:T(128)} %pad_add_fusion.1.at, s32[3,256]{1,0:T(4,128)} %table.1.refs_1_.tab, bf16[2,3,256,128]{3,2,1,0:T(8,128)(2,1)} %bitcast.32, bf16[2,3,256,128]{3,2,1,0:T(8,128)(2,1)} %bitcast.20, ...), custom_call_target="tpu_custom_call" | custom-call | flops 11660165120 | bytes 12582912 | tf_op jit(solution)/shard_map/far/pallas_call | solution.py:494
  85.7 4.7 %collective-permute-start.12 = (bf16[2,12,256,128]{3,2,1,0:T(8,128)(2,1)}, bf16[2,12,256,128]{3,2,1,0:T(8,128)(2,1)S(1)}, u32[]{:S(2)}, u32[]{:S(2)}) collective-permute-start(bf16[2,12,256,128]{3,2,1,0:T(8,128)(2,1)} %get-tuple-element.34.refs_9_), channel_id=1, source_target_pairs={{33,1},{35,3},{37,5},{39,7},{41,9},{43,11},{45,13},{47,15},{49,17}... | collective-permute-start | bytes 4718600 | tf_op jit(solution)/shard_map/ppermute | solution.py:503
  90.4 19.5 %own.1 = (bf16[12,256,128]{2,1,0:T(8,128)(2,1)}, bf16[12,256,128]{2,1,0:T(8,128)(2,1)}, bf16[12,256,128]{2,1,0:T(8,128)(2,1)}) custom-call(s32[4]{0:T(128)} %pad_add_fusion.1.at, s32[3,256]{1,0:T(4,128)} %table.1.refs_1_.tab, bf16[2,3,256,128]{3,2,1,0:T(8,128)(2,1)} %bitcast.33, bf16[2,3,256,128]{3,2,1,0:T(8,128)(2,1)} %bitcast.21, ...), custom_call_target="tpu_custom_call" | custom-call | flops 5033164800 | bytes 12582912 | tf_op jit(solution)/shard_map/own/pallas_call | solution.py:505
  111.7 4.8 %sums.1 = (bf16[3,3,256,128]{3,2,1,0:T(8,128)(2,1)}, bf16[3,3,256,128]{3,2,1,0:T(8,128)(2,1)}, bf16[3,3,256,128]{3,2,1,0:T(8,128)(2,1)}, bf16[3,3,256,128]{3,2,1,0:T(8,128)(2,1)}) custom-call(s32[4]{0:T(128)} %pad_add_fusion.1.at, bf16[2,12,256,128]{3,2,1,0:T(8,128)(2,1)} %copy-done.11, bf16[2,12,256,128]{3,2,1,0:T(8,128)(2,1)} %copy-done.12, ...), custom_call_target="tpu_custom_call" | custom-call | tf_op jit(solution)/shard_map/sums/pallas_call | solution.py:515
  116.5 1.6 %collective-permute-start.14 = (bf16[3,768,128]{2,1,0:T(8,128)(2,1)}, bf16[3,768,128]{2,1,0:T(8,128)(2,1)S(1)}, u32[]{:S(2)}, u32[]{:S(2)}) collective-permute-start(bf16[3,768,128]{2,1,0:T(8,128)(2,1)} %bitcast.51), channel_id=1, source_target_pairs={{4,0},{20,1},{6,2},{22,3},{8,4},{24,5},{10,6},{26,7},{12,8},{28,9}... | collective-permute-start | bytes 1769480 | tf_op jit(solution)/shard_map/ppermute | solution.py:451
  118.1 1.7 %collective-permute-start.13 = (bf16[3,768,128]{2,1,0:T(8,128)(2,1)}, bf16[3,768,128]{2,1,0:T(8,128)(2,1)S(1)}, u32[]{:S(2)}, u32[]{:S(2)}) collective-permute-start(bf16[3,768,128]{2,1,0:T(8,128)(2,1)} %bitcast.50), channel_id=1, source_target_pairs={{0,0},{16,1},{2,2},{18,3},{4,4},{20,5},{6,6},{22,7},{8,8},{24,9},{... | collective-permute-start | bytes 1769480 | tf_op jit(solution)/shard_map/ppermute | solution.py:451
  119.8 2.6 %collective-permute-start.15 = (bf16[3,768,128]{2,1,0:T(8,128)(2,1)}, bf16[3,768,128]{2,1,0:T(8,128)(2,1)S(1)}, u32[]{:S(2)}, u32[]{:S(2)}) collective-permute-start(bf16[3,768,128]{2,1,0:T(8,128)(2,1)} %bitcast.49), channel_id=1, source_target_pairs={{8,0},{24,1},{10,2},{26,3},{12,4},{28,5},{14,6},{30,7},{0,8},{16,9... | collective-permute-start | bytes 1769480 | tf_op jit(solution)/shard_map/ppermute | solution.py:451
  122.4 9.0 %collective-permute-done.14.refs_1_ = bf16[3,768,128]{2,1,0:T(8,128)(2,1)S(1)} collective-permute-done((bf16[3,768,128]{2,1,0:T(8,128)(2,1)}, bf16[3,768,128]{2,1,0:T(8,128)(2,1)S(1)}, u32[]{:S(2)}, u32[]{:S(2)}) %collective-permute-start.14) | collective-permute-done | bytes 589856 | tf_op jit(solution)/shard_map/ppermute | solution.py:451
  131.5 18.9 %collective-permute-done.16.refs_3_ = bf16[3,768,128]{2,1,0:T(8,128)(2,1)S(1)} collective-permute-done((bf16[3,768,128]{2,1,0:T(8,128)(2,1)}, bf16[3,768,128]{2,1,0:T(8,128)(2,1)S(1)}, u32[]{:S(2)}, u32[]{:S(2)}) %collective-permute-start.16) | collective-permute-done | bytes 589856 | tf_op jit(solution)/shard_map/ppermute | solution.py:451
  150.3 2.0 %join.1 = (bf16[768,512]{1,0:T(8,128)(2,1)}, bf16[768,512]{1,0:T(8,128)(2,1)}, bf16[768,512]{1,0:T(8,128)(2,1)}) custom-call(s32[4]{0:T(128)S(1)} %copy-done.10, bf16[3,768,128]{2,1,0:T(8,128)(2,1)S(1)} %collective-permute-done.13.refs_0_, bf16[3,768,128]{2,1,0:T(8,128)(2,1)S(1)} %collective-permute-done.14.refs_1_, ...), custom_call_target="tpu_custom_call" | custom-call | tf_op jit(solution)/shard_map/join/pallas_call | solution.py:526
  (59 shorter events, 10.8 us)
Async XLA Ops:
  1.3 10.8 %copy-start.13 = (s32[96,16]{0,1:T(8,128)S(1)}, s32[96,16]{0,1:T(8,128)}, u32[]{:S(2)}) copy-start(s32[96,16]{0,1:T(8,128)} %param.10) | copy-start | bytes 18436
  4.4 17.7 %collective-permute-start.1 = (bf16[2,768,128]{2,1,0:T(8,128)(2,1)}, bf16[2,768,128]{2,1,0:T(8,128)(2,1)S(1)}, u32[]{:S(2)}, u32[]{:S(2)}) collective-permute-start(bf16[2,768,128]{2,1,0:T(8,128)(2,1)} %get-tuple-element.24), channel_id=1, source_target_pairs={{0,4},{1,20},{2,6},{3,22},{4,8},{5,24},{6,10},{7,26},{8,12},{9,28}... | collective-permute-start | bytes 1179656 | tf_op jit(solution)/shard_map/ppermute | solution.py:451
  6.2 22.2 %collective-permute-start.2 = (bf16[2,768,128]{2,1,0:T(8,128)(2,1)}, bf16[2,768,128]{2,1,0:T(8,128)(2,1)S(1)}, u32[]{:S(2)}, u32[]{:S(2)}) collective-permute-start(bf16[2,768,128]{2,1,0:T(8,128)(2,1)} %get-tuple-element.25), channel_id=1, source_target_pairs={{0,8},{1,24},{2,10},{3,26},{4,12},{5,28},{6,14},{7,30},{8,0},{9,16... | collective-permute-start | bytes 1179656 | tf_op jit(solution)/shard_map/ppermute | solution.py:451
  9.1 19.4 %collective-permute-start.3 = (bf16[2,768,128]{2,1,0:T(8,128)(2,1)}, bf16[2,768,128]{2,1,0:T(8,128)(2,1)S(1)}, u32[]{:S(2)}, u32[]{:S(2)}) collective-permute-start(bf16[2,768,128]{2,1,0:T(8,128)(2,1)} %get-tuple-element.26), channel_id=1, source_target_pairs={{0,12},{1,28},{2,14},{3,30},{4,0},{5,16},{6,2},{7,18},{8,4},{9,20}... | collective-permute-start | bytes 1179656 | tf_op jit(solution)/shard_map/ppermute | solution.py:451
  10.4 19.7 %collective-permute-start = (bf16[2,768,128]{2,1,0:T(8,128)(2,1)}, bf16[2,768,128]{2,1,0:T(8,128)(2,1)S(1)}, u32[]{:S(2)}, u32[]{:S(2)}) collective-permute-start(bf16[2,768,128]{2,1,0:T(8,128)(2,1)} %get-tuple-element.23.refs_0_), channel_id=1, source_target_pairs={{0,0},{1,16},{2,2},{3,18},{4,4},{5,20},{6,6},{7,22},{8,8},{9,24},{... | collective-permute-start | bytes 1179656 | tf_op jit(solution)/shard_map/ppermute | solution.py:451
  17.9 21.9 %collective-permute-start.5 = (bf16[2,768,128]{2,1,0:T(8,128)(2,1)}, bf16[2,768,128]{2,1,0:T(8,128)(2,1)S(1)}, u32[]{:S(2)}, u32[]{:S(2)}) collective-permute-start(bf16[2,768,128]{2,1,0:T(8,128)(2,1)} %get-tuple-element.28), channel_id=1, source_target_pairs={{0,4},{1,20},{2,6},{3,22},{4,8},{5,24},{6,10},{7,26},{8,12},{9,28}... | collective-permute-start | bytes 1179656 | tf_op jit(solution)/shard_map/ppermute | solution.py:451
  22.1 22.5 %copy-start = (bf16[2,768,128]{2,1,0:T(8,128)(2,1)}, bf16[2,768,128]{2,1,0:T(8,128)(2,1)S(1)}, u32[]{:S(2)}) copy-start(bf16[2,768,128]{2,1,0:T(8,128)(2,1)S(1)} %collective-permute-done.1) | copy-start | bytes 1179652
  22.1 22.4 %collective-permute-start.6 = (bf16[2,768,128]{2,1,0:T(8,128)(2,1)}, bf16[2,768,128]{2,1,0:T(8,128)(2,1)S(1)}, u32[]{:S(2)}, u32[]{:S(2)}) collective-permute-start(bf16[2,768,128]{2,1,0:T(8,128)(2,1)} %get-tuple-element.29), channel_id=1, source_target_pairs={{0,8},{1,24},{2,10},{3,26},{4,12},{5,28},{6,14},{7,30},{8,0},{9,16... | collective-permute-start | bytes 1179656 | tf_op jit(solution)/shard_map/ppermute | solution.py:451
  28.4 16.2 %copy-start.1 = (bf16[2,768,128]{2,1,0:T(8,128)(2,1)}, bf16[2,768,128]{2,1,0:T(8,128)(2,1)S(1)}, u32[]{:S(2)}) copy-start(bf16[2,768,128]{2,1,0:T(8,128)(2,1)S(1)} %collective-permute-done.2) | copy-start | bytes 1179652
  28.4 16.2 %collective-permute-start.7 = (bf16[2,768,128]{2,1,0:T(8,128)(2,1)}, bf16[2,768,128]{2,1,0:T(8,128)(2,1)S(1)}, u32[]{:S(2)}, u32[]{:S(2)}) collective-permute-start(bf16[2,768,128]{2,1,0:T(8,128)(2,1)} %get-tuple-element.30), channel_id=1, source_target_pairs={{0,12},{1,28},{2,14},{3,30},{4,0},{5,16},{6,2},{7,18},{8,4},{9,20}... | collective-permute-start | bytes 1179656 | tf_op jit(solution)/shard_map/ppermute | solution.py:451
  28.4 16.2 %copy-start.2 = (bf16[2,768,128]{2,1,0:T(8,128)(2,1)}, bf16[2,768,128]{2,1,0:T(8,128)(2,1)S(1)}, u32[]{:S(2)}) copy-start(bf16[2,768,128]{2,1,0:T(8,128)(2,1)S(1)} %collective-permute-done.3) | copy-start | bytes 1179652
  28.4 16.1 %collective-permute-start.4 = (bf16[2,768,128]{2,1,0:T(8,128)(2,1)}, bf16[2,768,128]{2,1,0:T(8,128)(2,1)S(1)}, u32[]{:S(2)}, u32[]{:S(2)}) collective-permute-start(bf16[2,768,128]{2,1,0:T(8,128)(2,1)} %get-tuple-element.27.refs_4_), channel_id=1, source_target_pairs={{0,0},{1,16},{2,2},{3,18},{4,4},{5,20},{6,6},{7,22},{8,8},{9,24},{... | collective-permute-start | bytes 1179656 | tf_op jit(solution)/shard_map/ppermute | solution.py:451
  30.1 14.5 %copy-start.3 = (bf16[2,768,128]{2,1,0:T(8,128)(2,1)}, bf16[2,768,128]{2,1,0:T(8,128)(2,1)S(1)}, u32[]{:S(2)}) copy-start(bf16[2,768,128]{2,1,0:T(8,128)(2,1)S(1)} %collective-permute-done) | copy-start | bytes 1179652
  31.2 13.4 %copy-start.9 = (s32[4]{0:T(128)S(1)}, s32[4]{0:T(128)}, u32[]{:S(2)}) copy-start(s32[4]{0:T(128)} %pad_add_fusion.1.at) | copy-start | bytes 52
  32.5 22.3 %collective-permute-start.8 = (bf16[2,12,256,128]{3,2,1,0:T(8,128)(2,1)S(1)}, bf16[2,12,256,128]{3,2,1,0:T(8,128)(2,1)S(1)}, u32[]{:S(2)}, u32[]{:S(2)}) collective-permute-start(bf16[2,12,256,128]{3,2,1,0:T(8,128)(2,1)S(1)} %gather.1), channel_id=1, source_target_pairs={{1,33},{3,35},{5,37},{7,39},{9,41},{11,43},{13,45},{15,47},{17,49}... | collective-permute-start | bytes 4718600 | tf_op jit(solution)/shard_map/ppermute | solution.py:471
  47.5 3.5 %collective-permute-start.9 = (bf16[2,10,256,128]{3,2,1,0:T(8,128)(2,1)S(1)}, bf16[2,10,256,128]{3,2,1,0:T(8,128)(2,1)S(1)}, u32[]{:S(2)}, u32[]{:S(2)}) collective-permute-start(bf16[2,10,256,128]{3,2,1,0:T(8,128)(2,1)S(1)} %get-tuple-element.31), channel_id=1, source_target_pairs={{0,1},{1,0},{2,3},{3,2},{4,5},{5,4},{6,7},{7,6},{8,9},{9,8},{10,11... | collective-permute-start | bytes 3932168 | tf_op jit(solution)/shard_map/ppermute | solution.py:480
  47.6 3.4 %collective-permute-start.10 = (bf16[2,2,256,128]{3,2,1,0:T(8,128)(2,1)S(1)}, bf16[2,2,256,128]{3,2,1,0:T(8,128)(2,1)S(1)}, u32[]{:S(2)}, u32[]{:S(2)}) collective-permute-start(bf16[2,2,256,128]{3,2,1,0:T(8,128)(2,1)S(1)} %get-tuple-element.32), channel_id=1, source_target_pairs={{0,1},{1,0},{2,3},{3,2},{4,5},{5,4},{6,7},{7,6},{8,9},{9,8},{10,11... | collective-permute-start | bytes 786440 | tf_op jit(solution)/shard_map/ppermute | solution.py:480
  85.6 24.4 %collective-permute-start.11 = (bf16[2,12,256,128]{3,2,1,0:T(8,128)(2,1)}, bf16[2,12,256,128]{3,2,1,0:T(8,128)(2,1)S(1)}, u32[]{:S(2)}, u32[]{:S(2)}) collective-permute-start(bf16[2,12,256,128]{3,2,1,0:T(8,128)(2,1)} %get-tuple-element.33), channel_id=1, source_target_pairs={{0,1},{1,0},{2,3},{3,2},{4,5},{5,4},{6,7},{7,6},{8,9},{9,8},{10,11... | collective-permute-start | bytes 4718600 | tf_op jit(solution)/shard_map/ppermute | solution.py:504
  85.7 24.3 %collective-permute-start.12 = (bf16[2,12,256,128]{3,2,1,0:T(8,128)(2,1)}, bf16[2,12,256,128]{3,2,1,0:T(8,128)(2,1)S(1)}, u32[]{:S(2)}, u32[]{:S(2)}) collective-permute-start(bf16[2,12,256,128]{3,2,1,0:T(8,128)(2,1)} %get-tuple-element.34.refs_9_), channel_id=1, source_target_pairs={{33,1},{35,3},{37,5},{39,7},{41,9},{43,11},{45,13},{47,15},{49,17}... | collective-permute-start | bytes 4718600 | tf_op jit(solution)/shard_map/ppermute | solution.py:503
  111.7 38.7 %copy-start.10 = (s32[4]{0:T(128)S(1)}, s32[4]{0:T(128)}, u32[]{:S(2)}) copy-start(s32[4]{0:T(128)} %pad_add_fusion.1.at) | copy-start | bytes 52
  116.5 14.9 %collective-permute-start.14 = (bf16[3,768,128]{2,1,0:T(8,128)(2,1)}, bf16[3,768,128]{2,1,0:T(8,128)(2,1)S(1)}, u32[]{:S(2)}, u32[]{:S(2)}) collective-permute-start(bf16[3,768,128]{2,1,0:T(8,128)(2,1)} %bitcast.51), channel_id=1, source_target_pairs={{4,0},{20,1},{6,2},{22,3},{8,4},{24,5},{10,6},{26,7},{12,8},{28,9}... | collective-permute-start | bytes 1769480 | tf_op jit(solution)/shard_map/ppermute | solution.py:451
  118.1 13.3 %collective-permute-start.13 = (bf16[3,768,128]{2,1,0:T(8,128)(2,1)}, bf16[3,768,128]{2,1,0:T(8,128)(2,1)S(1)}, u32[]{:S(2)}, u32[]{:S(2)}) collective-permute-start(bf16[3,768,128]{2,1,0:T(8,128)(2,1)} %bitcast.50), channel_id=1, source_target_pairs={{0,0},{16,1},{2,2},{18,3},{4,4},{20,5},{6,6},{22,7},{8,8},{24,9},{... | collective-permute-start | bytes 1769480 | tf_op jit(solution)/shard_map/ppermute | solution.py:451
  119.8 11.7 %collective-permute-start.15 = (bf16[3,768,128]{2,1,0:T(8,128)(2,1)}, bf16[3,768,128]{2,1,0:T(8,128)(2,1)S(1)}, u32[]{:S(2)}, u32[]{:S(2)}) collective-permute-start(bf16[3,768,128]{2,1,0:T(8,128)(2,1)} %bitcast.49), channel_id=1, source_target_pairs={{8,0},{24,1},{10,2},{26,3},{12,4},{28,5},{14,6},{30,7},{0,8},{16,9... | collective-permute-start | bytes 1769480 | tf_op jit(solution)/shard_map/ppermute | solution.py:451
  122.4 28.0 %collective-permute-start.16 = (bf16[3,768,128]{2,1,0:T(8,128)(2,1)}, bf16[3,768,128]{2,1,0:T(8,128)(2,1)S(1)}, u32[]{:S(2)}, u32[]{:S(2)}) collective-permute-start(bf16[3,768,128]{2,1,0:T(8,128)(2,1)} %bitcast.48), channel_id=1, source_target_pairs={{12,0},{28,1},{14,2},{30,3},{0,4},{16,5},{2,6},{18,7},{4,8},{20,9}... | collective-permute-start | bytes 1769480 | tf_op jit(solution)/shard_map/ppermute | solution.py:451
  (10 other events, 29.1 us)
